TPU v7x, 256 devices: a whole 4x4x8 slice. The times are simulated.
256 devices in a mesh: rows: 32 (over y, x, core), cols: 8 (over z).
Axes of the slice: x: 4, y: 4, z: 8, core: 2. Of those that a mesh axis runs over, the one named last changes fastest.
Arguments:
- latent: float32 [2048, 16384], P('rows', 'cols'), may hold values from -3 to 3
- counts: int32 [2048, 16384], P('rows', 'cols'), may hold values from 0 to 39
- exposure: int32 [2048, 16384], P('rows', 'cols'), may hold values from 1 to 32
Outputs:
- newton_step: float32 [2048, 16384], P('rows', 'cols')
- residual: float32 [2048, 16384], P('rows', 'cols')
- direction: float32 [2048, 16384], P('rows', 'cols')
All inputs are finite; a program needn't handle non-finite values.
Results may differ from a plain program's by a relative error of at most 0.0003.
Values sent between devices are 32-bit elements; how exact they have to be, the bound alone decides.
No kernel may reach another device: no remote copies, remote signals or barrier semaphores. Data moves between devices by JAX's collectives and lax.ppermute only.
A program may use at most 128 MiB of HBM per device.

v0:
```python
import math

import jax
import jax.numpy as jnp
from jax import lax
from jax.sharding import PartitionSpec as P

dispersion = 4.0
prior_scale = 0.25
kappa_sq = 0.05
weight_shift = 1.0
highest = lax.Precision.HIGHEST


def extended(cells, sides, width):
    for axis, dim in sides:
        count = lax.axis_size(axis)
        ends = count - 1
        head = lax.slice_in_dim(cells, 0, width, axis=dim)
        tail = lax.slice_in_dim(cells, cells.shape[dim] - width, cells.shape[dim], axis=dim)
        cells = jnp.concatenate(
            [
                lax.ppermute(tail, axis, [(i, (i + 1) % count) for i in range(ends)]),
                cells,
                lax.ppermute(head, axis, [((i + 1) % count, i) for i in range(ends)]),
            ],
            axis=dim,
        )
    return cells


def dft_table(length):
    index_line = lax.iota(jnp.int32, length)
    product = index_line[:, None] * index_line[None, :] % length
    angle = 2.0 * math.pi / length * product.astype(jnp.float32)
    return (jnp.cos(angle), jnp.sin(angle))


def twiddle_table(outer_len, inner_len):
    product = lax.iota(jnp.int32, outer_len)[:, None] * lax.iota(jnp.int32, inner_len)[None, :]
    angle = 2.0 * math.pi / (outer_len * inner_len) * product.astype(jnp.float32)
    return (jnp.cos(angle), jnp.sin(angle))


def left_apply(table, data):
    return jnp.dot(table, data, precision=highest)


def middle_apply(table, data):
    return jnp.einsum("ka,lab->lkb", table, data, precision=highest)


def last_apply(data, table):
    line_rows, outer_len, inner_len = data.shape
    flat = jnp.dot(data.reshape(line_rows * outer_len, inner_len), table, precision=highest)
    return flat.reshape(line_rows, outer_len, inner_len)


def split_lengths(total_cols):
    inner_len = math.gcd(total_cols, 128)
    return (total_cols // inner_len, inner_len)


def columns_forward(real_part, imag_part):
    line_rows, total_cols = real_part.shape
    outer_len, inner_len = split_lengths(total_cols)
    outer_cos, outer_sin = dft_table(outer_len)
    inner_cos, inner_sin = dft_table(inner_len)
    twist_cos, twist_sin = twiddle_table(outer_len, inner_len)
    real_cube = real_part.reshape(line_rows, outer_len, inner_len)
    imag_cube = imag_part.reshape(line_rows, outer_len, inner_len)
    section_real = middle_apply(outer_cos, real_cube) + middle_apply(outer_sin, imag_cube)
    section_imag = middle_apply(outer_cos, imag_cube) - middle_apply(outer_sin, real_cube)
    turned_real = section_real * twist_cos + section_imag * twist_sin
    turned_imag = section_imag * twist_cos - section_real * twist_sin
    final_real = last_apply(turned_real, inner_cos) + last_apply(turned_imag, inner_sin)
    final_imag = last_apply(turned_imag, inner_cos) - last_apply(turned_real, inner_sin)
    return (final_real.reshape(line_rows, total_cols), final_imag.reshape(line_rows, total_cols))


def columns_inverse(real_part, imag_part):
    line_rows, total_cols = real_part.shape
    outer_len, inner_len = split_lengths(total_cols)
    outer_cos, outer_sin = dft_table(outer_len)
    inner_cos, inner_sin = dft_table(inner_len)
    twist_cos, twist_sin = twiddle_table(outer_len, inner_len)
    real_cube = real_part.reshape(line_rows, outer_len, inner_len)
    imag_cube = imag_part.reshape(line_rows, outer_len, inner_len)
    section_real = last_apply(real_cube, inner_cos) - last_apply(imag_cube, inner_sin)
    section_imag = last_apply(imag_cube, inner_cos) + last_apply(real_cube, inner_sin)
    turned_real = section_real * twist_cos - section_imag * twist_sin
    turned_imag = section_imag * twist_cos + section_real * twist_sin
    final_real = middle_apply(outer_cos, turned_real) - middle_apply(outer_sin, turned_imag)
    final_imag = middle_apply(outer_cos, turned_imag) + middle_apply(outer_sin, turned_real)
    return (final_real.reshape(line_rows, total_cols), final_imag.reshape(line_rows, total_cols))


def inverse_symbol(row_freq, col_freq, band_rows, total_cols):
    row_sine = jnp.sin(math.pi * row_freq.astype(jnp.float32) / band_rows)
    col_sine = jnp.sin(math.pi * col_freq.astype(jnp.float32) / total_cols)
    inner_term = kappa_sq + 4.0 * row_sine * row_sine + 4.0 * col_sine * col_sine
    symbol = prior_scale * inner_term * inner_term + weight_shift
    quarter = total_cols // 4
    retained = (col_freq < quarter) | (col_freq > total_cols - quarter)
    weight = jnp.where(retained, 1.0 / symbol, 1.0)
    return weight / float(band_rows * total_cols)


def frequency_of(position, outer_len, inner_len):
    return position // inner_len + outer_len * (position % inner_len)


def precondition(grid_field):
    band_rows, block_cols = grid_field.shape
    col_parts = lax.axis_size("cols")
    col_index = lax.axis_index("cols")
    total_cols = block_cols * col_parts
    outer_len, inner_len = split_lengths(total_cols)
    row_cos, row_sin = dft_table(band_rows)
    spectrum = jnp.stack([left_apply(row_cos, grid_field), -left_apply(row_sin, grid_field)])
    whole_lines = lax.all_to_all(spectrum, "cols", split_axis=1, concat_axis=2, tiled=True)
    line_rows = band_rows // col_parts
    spec_real, spec_imag = columns_forward(whole_lines[0], whole_lines[1])
    row_freq = col_index * line_rows + lax.iota(jnp.int32, line_rows)
    col_freq = frequency_of(lax.iota(jnp.int32, total_cols), outer_len, inner_len)
    spectral_scale = inverse_symbol(row_freq[:, None], col_freq[None, :], band_rows, total_cols)
    back_real, back_imag = columns_inverse(spec_real * spectral_scale, spec_imag * spectral_scale)
    blocks = lax.all_to_all(
        jnp.stack([back_real, back_imag]), "cols", split_axis=2, concat_axis=1, tiled=True
    )
    return left_apply(row_cos, blocks[0]) - left_apply(row_sin, blocks[1])


def prior_apply(grid_field):
    padded = extended(grid_field, (("rows", 0), ("cols", 1)), 2)
    row_count, col_count = grid_field.shape

    def offset_view(shift_row, shift_col):
        return padded[
            2 + shift_row : 2 + shift_row + row_count, 2 + shift_col : 2 + shift_col + col_count
        ]

    centre = kappa_sq + 4.0
    nearest = offset_view(1, 0) + offset_view(-1, 0) + offset_view(0, 1) + offset_view(0, -1)
    diagonal = offset_view(1, 1) + offset_view(1, -1) + offset_view(-1, 1) + offset_view(-1, -1)
    distant = offset_view(2, 0) + offset_view(-2, 0) + offset_view(0, 2) + offset_view(0, -2)
    return prior_scale * (
        (centre * centre + 4.0) * grid_field - 2.0 * centre * nearest + 2.0 * diagonal + distant
    )


def on_device(latent, counts, exposure):
    mean_rate = exposure.astype(jnp.float32) * jnp.exp(latent)
    fisher = dispersion * mean_rate / (dispersion + mean_rate)
    score = (counts.astype(jnp.float32) - mean_rate) * dispersion / (dispersion + mean_rate)
    gradient = score - prior_apply(latent)
    first_search = precondition(gradient)
    first_product = lax.psum(jnp.sum(gradient * first_search), ("rows", "cols"))
    image = prior_apply(first_search) + fisher * first_search
    curvature = lax.psum(jnp.sum(first_search * image), ("rows", "cols"))
    step_size = first_product / curvature
    residual = gradient - step_size * image
    next_search = precondition(residual)
    next_product = lax.psum(jnp.sum(residual * next_search), ("rows", "cols"))
    newton_step = step_size * first_search
    direction = next_search + next_product / first_product * first_search
    return (newton_step, residual, direction)


def solution(mesh):
    placed = (P("rows", "cols"), P("rows", "cols"), P("rows", "cols"))
    return jax.shard_map(
        on_device,
        mesh=mesh,
        in_specs=placed,
        out_specs=(P("rows", "cols"), P("rows", "cols"), P("rows", "cols")),
        check_vma=False,
    )
```

profile of v0, /device:TPU:8, one launch (start us, length us, event | category | flops | bytes accessed | tf_op | source)
XLA Modules:
  0.0 561.3 jit_solution(15677637600210697787)
XLA Ops:
  0.6 0.9 fusion.333
  1.5 4.0 collective-permute-start
  5.5 1.9 collective-permute-start.1
  7.4 1.1 constant_dynamic-update-slice_fusion.1
  8.5 4.1 collective-permute-done.1
  13.5 1.3 collective-permute-start.2
  14.8 4.5 collective-permute-start.3
  19.4 1.6 collective-permute-done.3
  21.0 1.5 pad_maximum_fusion.4
  22.5 2.9 fusion.34
  26.9 1.8 copy.128
  28.7 10.4 %all-to-all-start = ((f32[2,64,2048]{2,0,1:T(2,128)}), f32[2,64,2048]{2,0,1:T(2,128)S(1)}, u32[]{:S(2)}, u32[]{:S(2)}) async-start(f32[2,64,2048]{2,0,1:T(2,128)} %copy.128), calls=%async_computation | async-start | bytes 2097152 | tf_op jit(solution)/shard_map/all_to_all | solution.py:121
  40.1 22.2 %all-to-all-done = f32[2,64,2048]{2,0,1:T(2,128)S(1)} async-done(((f32[2,64,2048]{2,0,1:T(2,128)}), f32[2,64,2048]{2,0,1:T(2,128)S(1)}, u32[]{:S(2)}, u32[]{:S(2)}) %all-to-all-start) | async-done | bytes 1048608 | tf_op jit(solution)/shard_map/all_to_all | solution.py:121
  63.2 1.1 fusion.102
  64.4 1.1 fusion.104
  65.5 1.1 fusion.12
  66.6 1.1 fusion.13
  67.7 1.2 fusion.54
  68.9 1.2 fusion.53
  70.1 1.3 fusion.10
  72.3 1.8 fusion.11
  75.9 0.9 convolution_subtract_fusion.7
  79.5 0.9 stack_reshape.13
  81.5 1.1 pad_maximum_fusion.1
  82.6 14.7 %copy.146 = f32[2,8,16384]{1,0,2:T(2,128)} copy(f32[2,8,16384]{2,1,0:T(8,128)S(1)} %pad_maximum_fusion.1) | data formatting | bytes 2097152 | tf_op jit(solution)/shard_map/stack | solution.py:129
  97.3 28.3 %reshape.237 = f32[8,1,32768]{2,1,0:T(1,128)S(1)} reshape(f32[16384,2,8]{2,1,0:T(2,128)} %bitcast.148) | data formatting | bytes 2097152
  125.6 27.5 %all_to_all.60 = f32[8,1,32768]{2,1,0:T(1,128)S(1)} all-to-all(f32[8,1,32768]{2,1,0:T(1,128)S(1)} %reshape.237), channel_id=1, replica_groups=mesh['rows'=32,'cols'=8] {'cols'}, dimensions={0} | all-to-all | bytes 2097152 | tf_op jit(solution)/shard_map/all_to_all | solution.py:128
  153.7 3.2 reduce
  156.9 32.3 %reshape.238 = f32[16384,2,8]{2,1,0:T(2,128)} reshape(f32[8,32768]{1,0:T(8,128)S(1)} %reduce) | data formatting | bytes 2097152
  189.2 13.2 %copy.194 = f32[2,8,8,2048]{3,2,1,0:T(8,128)S(1)} copy(f32[2,8,8,2048]{1,0,3,2:T(2,128)} %bitcast.149) | data formatting | bytes 2097152 | tf_op jit(solution)/shard_map/all_to_all | solution.py:128
  202.5 0.9 fusion.47
  203.4 0.9 convolution_subtract_fusion.1
  204.4 1.9 collective-permute-start.5
  206.3 9.7 %collective-permute-start.4 = (f32[2,2048]{1,0:T(2,128)S(1)}, f32[2,2048]{1,0:T(2,128)S(1)}, u32[]{:S(2)}, u32[]{:S(2)}) collective-permute-start(f32[2,2048]{1,0:T(2,128)S(1)} %get-tuple-element.27), channel_id=1, source_target_pairs={{8,0},{16,8},{24,16},{32,24},{40,32},{48,40},{56,48},{64,56},{72,6... | collective-permute-start | bytes 49160 | tf_op jit(solution)/shard_map/ppermute | solution.py:25
  216.1 1.4 collective-permute-done.4
  217.6 1.3 collective-permute-start.6
  218.9 4.5 collective-permute-start.7
  223.4 1.6 collective-permute-done.7
  225.3 1.8 multiply_reduce_fusion.1
  227.2 75.3 %all-reduce = (f32[]{:T(128)}, f32[]{:T(128)}) all-reduce(f32[]{:T(128)} %get-tuple-element.4, f32[]{:T(128)} %get-tuple-element.3), channel_id=1, replica_groups=mesh['rows'=32,'cols'=8] {'rows','cols'}, use_global_device_ids=true, to_apply=%region_1.2 | all-reduce | flops 2 | bytes 16 | tf_op jit(solution)/shard_map/psum | solution.py:158
  306.2 33.5 %all_to_all.61 = f32[2,64,2048]{2,0,1:T(2,128)S(1)} all-to-all(f32[2,64,2048]{2,0,1:T(2,128)S(1)} %copy.150), channel_id=1, replica_groups=mesh['rows'=32,'cols'=8] {'cols'}, dimensions={1} | all-to-all | bytes 2097152 | tf_op jit(solution)/shard_map/all_to_all | solution.py:121
  340.6 1.1 fusion.90
  341.7 1.1 fusion.92
  342.8 1.1 fusion.6
  343.9 1.1 fusion.7
  345.1 1.2 fusion.58
  346.3 1.2 fusion.57
  347.5 1.3 fusion.4
  349.6 1.3 fusion.5
  350.9 1.1 fusion.87
  352.9 0.9 convolution_subtract_fusion.3
  356.3 1.0 copy.165
  357.3 1.9 stack_reshape.15
  360.4 1.1 pad_maximum_fusion.3
  361.5 14.7 %copy.166 = f32[2,8,16384]{1,0,2:T(2,128)} copy(f32[2,8,16384]{2,1,0:T(8,128)S(1)} %pad_maximum_fusion.3) | data formatting | bytes 2097152 | tf_op jit(solution)/shard_map/stack | solution.py:129
  376.2 28.3 %reshape.239 = f32[8,1,32768]{2,1,0:T(1,128)S(1)} reshape(f32[16384,2,8]{2,1,0:T(2,128)} %bitcast.150) | data formatting | bytes 2097152
  404.5 30.4 %all_to_all.62 = f32[8,1,32768]{2,1,0:T(1,128)} all-to-all(f32[8,1,32768]{2,1,0:T(1,128)S(1)} %reshape.239), channel_id=1, replica_groups=mesh['rows'=32,'cols'=8] {'cols'}, dimensions={0} | all-to-all | bytes 2097152 | tf_op jit(solution)/shard_map/all_to_all | solution.py:128
  434.9 4.4 reduce.1
  439.3 32.1 %reshape.240 = f32[16384,2,8]{2,1,0:T(2,128)} reshape(f32[8,32768]{1,0:T(8,128)S(1)} %reduce.1) | data formatting | bytes 2097152
  471.4 13.2 %copy.195 = f32[2,8,8,2048]{3,2,1,0:T(8,128)S(1)} copy(f32[2,8,8,2048]{1,0,3,2:T(2,128)} %bitcast.151) | data formatting | bytes 2097152 | tf_op jit(solution)/shard_map/all_to_all | solution.py:128
  484.6 0.9 fusion.44
  485.6 1.6 multiply_reduce_fusion
  487.1 71.6 %psum.23 = f32[]{:T(128)} all-reduce(f32[]{:T(128)} %get-tuple-element.30), channel_id=1, replica_groups=mesh['rows'=32,'cols'=8] {'rows','cols'}, use_global_device_ids=true, to_apply=%region_5.6 | all-reduce | flops 1 | bytes 8 | tf_op jit(solution)/shard_map/psum | solution.py:164
  560.0 1.1 multiply_add_fusion
  (59 shorter events, 20.3 us)
Async XLA Ops:
  1.5 7.0 %collective-permute-start = (f32[2,2048]{1,0:T(2,128)S(1)}, f32[2,2048]{1,0:T(2,128)S(1)}, u32[]{:S(2)}, u32[]{:S(2)}) collective-permute-start(f32[2,2048]{1,0:T(2,128)S(1)} %get-tuple-element.28), channel_id=1, source_target_pairs={{8,0},{16,8},{24,16},{32,24},{40,32},{48,40},{56,48},{64,56},{72,6... | collective-permute-start | bytes 49160 | tf_op jit(solution)/shard_map/ppermute | solution.py:25
  5.5 7.2 %collective-permute-start.1 = (f32[2,2048]{1,0:T(2,128)S(1)}, f32[2,2048]{1,0:T(2,128)S(1)}, u32[]{:S(2)}, u32[]{:S(2)}) collective-permute-start(f32[2,2048]{1,0:T(2,128)S(1)} %get-tuple-element.29), channel_id=1, source_target_pairs={{0,8},{8,16},{16,24},{24,32},{32,40},{40,48},{48,56},{56,64},{64,7... | collective-permute-start | bytes 49160 | tf_op jit(solution)/shard_map/ppermute | solution.py:23
  13.5 5.9 %collective-permute-start.2 = (f32[68,2]{1,0:T(8,128)S(1)}, f32[68,2]{1,0:T(8,128)S(1)}, u32[]{:S(2)}, u32[]{:S(2)}) collective-permute-start(f32[68,2]{1,0:T(8,128)S(1)} %get-tuple-element.22), channel_id=1, source_target_pairs={{1,0},{2,1},{3,2},{4,3},{5,4},{6,5},{7,6},{9,8},{10,9},{11,10},{12... | collective-permute-start | bytes 1640 | tf_op jit(solution)/shard_map/ppermute | solution.py:25
  14.8 6.2 %collective-permute-start.3 = (f32[68,2]{1,0:T(8,128)S(1)}, f32[68,2]{1,0:T(8,128)S(1)}, u32[]{:S(2)}, u32[]{:S(2)}) collective-permute-start(f32[68,2]{1,0:T(8,128)S(1)} %get-tuple-element.23), channel_id=1, source_target_pairs={{0,1},{1,2},{2,3},{3,4},{4,5},{5,6},{6,7},{8,9},{9,10},{10,11},{11... | collective-permute-start | bytes 1640 | tf_op jit(solution)/shard_map/ppermute | solution.py:23
  28.7 33.7 %all-to-all-start = ((f32[2,64,2048]{2,0,1:T(2,128)}), f32[2,64,2048]{2,0,1:T(2,128)S(1)}, u32[]{:S(2)}, u32[]{:S(2)}) async-start(f32[2,64,2048]{2,0,1:T(2,128)} %copy.128), calls=%async_computation | async-start | bytes 2097152 | tf_op jit(solution)/shard_map/all_to_all | solution.py:121
  189.2 36.2 %copy-start = (f32[64,2048]{1,0:T(8,128)S(1)}, f32[64,2048]{1,0:T(8,128)}, u32[]{:S(2)}) copy-start(f32[64,2048]{1,0:T(8,128)} %param.3) | copy-start | bytes 1572868
  189.2 36.2 %copy-start.2 = (s32[64,2048]{1,0:T(8,128)S(1)}, s32[64,2048]{1,0:T(8,128)}, u32[]{:S(2)}) copy-start(s32[64,2048]{1,0:T(8,128)} %param.5) | copy-start | bytes 1572868
  204.4 11.7 %collective-permute-start.5 = (f32[2,2048]{1,0:T(2,128)S(1)}, f32[2,2048]{1,0:T(2,128)S(1)}, u32[]{:S(2)}, u32[]{:S(2)}) collective-permute-start(f32[2,2048]{1,0:T(2,128)S(1)} %get-tuple-element.26), channel_id=1, source_target_pairs={{0,8},{8,16},{16,24},{24,32},{32,40},{40,48},{48,56},{56,64},{64,7... | collective-permute-start | bytes 49160 | tf_op jit(solution)/shard_map/ppermute | solution.py:23
  206.3 11.2 %collective-permute-start.4 = (f32[2,2048]{1,0:T(2,128)S(1)}, f32[2,2048]{1,0:T(2,128)S(1)}, u32[]{:S(2)}, u32[]{:S(2)}) collective-permute-start(f32[2,2048]{1,0:T(2,128)S(1)} %get-tuple-element.27), channel_id=1, source_target_pairs={{8,0},{16,8},{24,16},{32,24},{40,32},{48,40},{56,48},{64,56},{72,6... | collective-permute-start | bytes 49160 | tf_op jit(solution)/shard_map/ppermute | solution.py:25
  217.6 5.9 %collective-permute-start.6 = (f32[68,2]{1,0:T(8,128)S(1)}, f32[68,2]{1,0:T(8,128)S(1)}, u32[]{:S(2)}, u32[]{:S(2)}) collective-permute-start(f32[68,2]{1,0:T(8,128)S(1)} %get-tuple-element.18), channel_id=1, source_target_pairs={{1,0},{2,1},{3,2},{4,3},{5,4},{6,5},{7,6},{9,8},{10,9},{11,10},{12... | collective-permute-start | bytes 1640 | tf_op jit(solution)/shard_map/ppermute | solution.py:25
  218.9 6.2 %collective-permute-start.7 = (f32[68,2]{1,0:T(8,128)S(1)}, f32[68,2]{1,0:T(8,128)S(1)}, u32[]{:S(2)}, u32[]{:S(2)}) collective-permute-start(f32[68,2]{1,0:T(8,128)S(1)} %get-tuple-element.19), channel_id=1, source_target_pairs={{0,1},{1,2},{2,3},{3,4},{4,5},{5,6},{6,7},{8,9},{9,10},{10,11},{11... | collective-permute-start | bytes 1640 | tf_op jit(solution)/shard_map/ppermute | solution.py:23
  303.8 181.8 %copy-start.1 = (f32[64,2048]{1,0:T(8,128)}, f32[64,2048]{1,0:T(8,128)S(1)}, u32[]{:S(2)}) copy-start(f32[64,2048]{1,0:T(8,128)S(1)} %multiply_subtract_fusion.2) | copy-start | bytes 1572868
where the time goes:
time: 569 us; the launch traced here: 561 us
  blocking collectives  238 us (42%)
  local copies, waits for them, and re-layouts  189 us (33%)
  matrix products  40.4 us (7%)
  starting transfers between devices  39.6 us (7%)
  waiting for transfers between devices  31 us (5%)
  other arithmetic  19.3 us (3%)
    unnamed x11, local copies, waits for them, and re-layouts  122 us
    psum x1, blocking collectives, on_device(): first_product = lax.psum(jnp.sum(gradient * first_search), ('rows', 'cols'))  75.3 us
    psum x1, blocking collectives, on_device(): next_product = lax.psum(jnp.sum(residual * next_search), ('rows', 'cols'))  71.6 us
    all_to_all x2, blocking collectives, precondition(): lax.all_to_all(jnp.stack([back_real, back_imag]), 'cols', split_axis=2, c...  57.9 us
    all_to_all x1, blocking collectives, precondition(): lax.all_to_all(spectrum, 'cols', split_axis=1, concat_axis=2, tiled=True)  33.5 us
    another operation x6, local copies, waits for them, and re-layouts, precondition(): jnp.stack([back_real, back_imag])  32.4 us
    all_to_all x3, local copies, waits for them, and re-layouts, precondition(): lax.all_to_all(jnp.stack([back_real, back_imag]), 'cols', split_axis=2, c...  27 us
    all_to_all x1, waiting for transfers between devices, precondition(): lax.all_to_all(spectrum, 'cols', split_axis=1, concat_axis=2, tiled=True)  22.2 us
  transfers between devices with their start and end apart: 9, of which 5 were waited for; matrix products, arithmetic and copies ran while one was open for 0% of the time, Pallas kernels for 0%

commit v1 on v0

v1 whole, which is shorter than its diff:
```python
import functools
import math

import jax
import jax.numpy as jnp
import ml_dtypes
import numpy as np
from jax import lax
from jax.experimental import pallas as pl
from jax.experimental.pallas import tpu as pltpu
from jax.sharding import PartitionSpec as P

dispersion = 4.0
prior_scale = 0.25
kappa_sq = 0.05
weight_shift = 1.0
centre = kappa_sq + 4.0

band = 64
width = 2048
lanes = 128
tiles = width // lanes
parts = 8
total_cols = width * parts
lines = band // parts
half = 72
kept = 64
vmem_bytes = 48 * 1024 * 1024


def high_low(table):
    high = table.astype(ml_dtypes.bfloat16)
    low = (table - high.astype(np.float64)).astype(ml_dtypes.bfloat16)
    return high, low


@functools.cache
def tables():
    rows = np.arange(band)
    freq = np.zeros(band)
    basis = np.zeros((band, band))
    basis[0] = 1.0 / math.sqrt(band)
    for k in range(1, band // 2):
        angle = 2.0 * np.pi * ((k * rows) % band) / band
        basis[2 * k - 1] = np.cos(angle) * math.sqrt(2.0 / band)
        basis[2 * k] = np.sin(angle) * math.sqrt(2.0 / band)
        freq[2 * k - 1] = freq[2 * k] = k
    basis[band - 1] = (1.0 - 2.0 * (rows % 2)) / math.sqrt(band)
    freq[band - 1] = band // 2
    row_term = kappa_sq + 4.0 * np.sin(np.pi * freq / band) ** 2
    out = {}
    high, low = high_low(basis)
    out["row_forward"] = np.concatenate([high, high, low], 1)
    high, low = high_low(basis.T)
    out["row_inverse"] = np.concatenate([high, high, low], 1)
    out["row_term"] = np.tile(row_term[:, None], (1, lanes)).astype(np.float32)

    count = lanes // 2 + 1
    outer = np.arange(count)
    inner = np.arange(lanes)
    angle = 2.0 * np.pi * ((outer[:, None] * inner[None, :]) % lanes) / lanes
    section = np.zeros((2 * half, lanes))
    section[:count] = np.cos(angle)
    section[half : half + count] = np.sin(angle)
    high, low = high_low(section)
    out["outer_forward"] = np.concatenate([high, high, low], 1)
    section = section.T.copy()
    section[:, half:] *= -1.0
    high, low = high_low(section)
    out["outer_inverse"] = np.concatenate([high, high, low], 1)

    angle = 2.0 * np.pi * outer[:, None] * inner[None, :] / total_cols
    twist = np.zeros((2, half, lanes), np.float32)
    twist[0, :count] = np.cos(angle)
    twist[1, :count] = np.sin(angle)
    out["twist"] = twist

    kept_inner = np.concatenate([np.arange(kept // 2), np.arange(lanes - kept // 2, lanes)])
    angle = 2.0 * np.pi * ((inner[:, None] * kept_inner[None, :]) % lanes) / lanes
    cosine, sine = np.cos(angle), np.sin(angle)
    high, low = high_low(np.block([[cosine, -sine], [sine, cosine]]))
    out["inner_forward"] = np.concatenate([high, low], 1)
    high, low = high_low(np.block([[cosine.T, sine.T], [-sine.T, cosine.T]]))
    out["inner_inverse"] = np.concatenate([high, high, low], 0)

    col_freq = outer[:, None] + lanes * kept_inner[None, :]
    quarter = total_cols // 4
    retained = (col_freq < quarter) | (col_freq > total_cols - quarter)
    twice = np.where((outer == 0) | (outer == lanes // 2), 1.0, 2.0)[:, None]
    weight = np.zeros((half, 2 * kept))
    weight[:count] = np.tile(np.where(retained, twice / total_cols, 0.0), (1, 2))
    term = np.zeros((half, 2 * kept))
    term[:count] = np.tile(4.0 * np.sin(np.pi * col_freq / total_cols) ** 2, (1, 2))
    out["weight"] = weight.astype(np.float32)
    out["col_term"] = term.astype(np.float32)
    return out


def split(value):
    high = value.astype(jnp.bfloat16)
    low = (value - high.astype(jnp.float32)).astype(jnp.bfloat16)
    return high, low


def dot(left, right):
    return jnp.dot(left, right, preferred_element_type=jnp.float32)


def left_product(table, value):
    high, low = split(value)
    return dot(table, jnp.concatenate([high, low, high], 0))


def lane_index(shape):
    return lax.broadcasted_iota(jnp.int32, shape, 1)


def stencil(pad):
    full = width + lanes
    field = pad[8:72, :]
    near = pad[7:71, :] + pad[9:73, :]
    far = pad[6:70, :] + pad[10:74, :]
    beside = 2.0 * near - (2.0 * centre) * field
    across = pltpu.roll(beside, 1, 1) + pltpu.roll(beside, full - 1, 1)
    distant = far + pltpu.roll(field, 2, 1) + pltpu.roll(field, full - 2, 1)
    return prior_scale * ((centre * centre + 4.0) * field - 2.0 * centre * near + across + distant)


def store_coefs(coefs, out, count):
    for part in range(parts):
        for tile in range(count):
            out[part, tile * lines : (tile + 1) * lines, :] = coefs[
                part * lines : (part + 1) * lines, tile * lanes : (tile + 1) * lanes
            ]


def load_coefs(ref, count):
    return jnp.concatenate(
        [
            jnp.concatenate(
                [ref[part, tile * lines : (tile + 1) * lines, :] for part in range(parts)], 0
            )
            for tile in range(count)
        ],
        1,
    )


def gradient_kernel(
    place, latent, counts, exposure, swap_a, swap_b, basis, payload, grad, beyond, fisher, pad
):
    even = place[0] % 2 == 0
    pad[8:72, :width] = latent[...]
    pad[6:8, :width] = jnp.where(even, swap_b[...], swap_a[...])
    pad[72:74, :width] = jnp.where(even, swap_a[...], swap_b[...])
    pad[0:80, width:] = jnp.zeros((80, lanes), jnp.float32)
    prior = stencil(pad)
    mean_rate = exposure[...].astype(jnp.float32) * jnp.exp(latent[...])
    ratio = dispersion / (dispersion + mean_rate)
    fisher[...] = mean_rate * ratio
    score = (counts[...].astype(jnp.float32) - mean_rate) * ratio
    inside = score - prior[:, :width]
    outside = -prior[:, width:]
    grad[...] = inside
    beyond[...] = outside
    coefs = left_product(basis[...], jnp.concatenate([inside, outside], 1))
    store_coefs(coefs, payload, tiles + 1)


def filter_kernel(
    place,
    incoming,
    row_term,
    col_term,
    weight,
    outer_forward,
    outer_inverse,
    inner_forward,
    inner_inverse,
    twist,
    out,
    energy,
    *,
    edges,
):
    lane = lane_index((tiles, lanes))
    sub = lax.broadcasted_iota(jnp.int32, (tiles, lanes), 0)
    first = (sub == 0) & (lane < lanes // 2)
    last = (sub == tiles - 1) & (lane >= lanes // 2)
    line_fields = []
    for line in range(lines):
        blocks = [
            incoming[part, pl.ds(line, tiles, stride=lines), :] for part in range(parts)
        ]
        if edges:
            spill = [
                incoming[part, tiles * lines + line : tiles * lines + line + 1, :]
                for part in range(parts)
            ]
            for part in range(parts):
                if part > 0:
                    blocks[part] = blocks[part] + jnp.where(first, spill[part - 1], 0.0)
                if part < parts - 1:
                    blocks[part] = blocks[part] + jnp.where(last, spill[part + 1], 0.0)
        line_fields.append(jnp.concatenate(blocks, 0))
    field = jnp.concatenate(line_fields, 1)
    section = left_product(outer_forward[...], field)
    cosine, sine = twist[0], twist[1]
    turned = []
    for line in range(lines):
        cols = slice(line * lanes, (line + 1) * lanes)
        even_part, odd_part = section[:half, cols], section[half:, cols]
        real = even_part * cosine - odd_part * sine
        imag = -(odd_part * cosine + even_part * sine)
        turned.append(jnp.concatenate([real, imag], 1))
    high, low = split(jnp.concatenate(turned, 0))
    both = dot(high, inner_forward[...])
    spectrum = both[:, : 2 * kept] + both[:, 2 * kept :] + dot(low, inner_forward[:, : 2 * kept])
    row_line = row_term[pl.ds(pl.multiple_of(place[1] * lines, lines), lines), :]
    scaled = []
    total = jnp.zeros((half, 2 * kept), jnp.float32)
    for line in range(lines):
        inner_term = row_line[line : line + 1, :] + col_term[...]
        quad = prior_scale * inner_term * inner_term
        gain = -quad / (quad + weight_shift) * weight[...]
        piece = spectrum[line * half : (line + 1) * half, :]
        scaled.append(piece * gain)
        if not edges:
            total = total + piece * scaled[-1]
    if not edges:
        energy[...] = jnp.broadcast_to(jnp.sum(total, axis=(0, 1), keepdims=True), (8, lanes))
    high, low = split(jnp.concatenate(scaled, 0))
    back = dot(jnp.concatenate([high, low], 1), inner_inverse[: 4 * kept, :]) + dot(
        high, inner_inverse[4 * kept :, :]
    )
    reals, imags = [], []
    for line in range(lines):
        rows = slice(line * half, (line + 1) * half)
        real, imag = back[rows, :lanes], back[rows, lanes:]
        reals.append(real * cosine - imag * sine)
        imags.append(imag * cosine + real * sine)
    folded = jnp.concatenate([jnp.concatenate(reals, 1), jnp.concatenate(imags, 1)], 0)
    result = left_product(outer_inverse[...], folded)
    edge_lane = lane_index((1, lanes)) < lanes // 2
    for line in range(lines):
        cols = slice(line * lanes, (line + 1) * lanes)
        for part in range(parts):
            out[part, pl.ds(line, tiles, stride=lines), :] = result[
                part * tiles : (part + 1) * tiles, cols
            ]
        if edges:
            for part in range(parts):
                nothing = jnp.zeros((1, lanes), jnp.float32)
                after, before = nothing, nothing
                if part < parts - 1:
                    row = slice((part + 1) * tiles, (part + 1) * tiles + 1)
                    after = result[row, cols] + field[row, cols]
                if part > 0:
                    row = slice(part * tiles - 1, part * tiles)
                    before = result[row, cols] + field[row, cols]
                out[part, tiles * lines + line : tiles * lines + line + 1, :] = jnp.where(
                    edge_lane, after, before
                )


def search_kernel(place, incoming, grad, left, right, basis, full_grad, search, send_a, send_b):
    even = place[0] % 2 == 0
    coefs = load_coefs(incoming, tiles + 1)
    update = left_product(basis[...], coefs)
    lane = lane_index((band, lanes))
    head = grad[:, :lanes] + jnp.where(lane < lanes // 2, left[...], 0.0)
    tail = grad[:, width - lanes :] + jnp.where(lane >= lanes // 2, right[...], 0.0)
    whole = jnp.concatenate([head, grad[:, lanes : width - lanes], tail], 1)
    full_grad[...] = whole
    found = jnp.concatenate([whole + update[:, :width], update[:, width:]], 1)
    search[...] = found
    top, bottom = found[:2, :], found[band - 2 :, :]
    send_a[...] = jnp.where(even, bottom, top)
    send_b[...] = jnp.where(even, top, bottom)


def image_kernel(
    place, search, swap_a, swap_b, fisher, grad, basis, payload, image, sums, pad
):
    even = place[0] % 2 == 0
    pad[8:72, :] = search[...]
    pad[6:8, :] = jnp.where(even, swap_b[...], swap_a[...])
    pad[72:74, :] = jnp.where(even, swap_a[...], swap_b[...])
    prior = stencil(pad)
    field = search[:, :width]
    result = prior[:, :width] + fisher[...] * field
    image[...] = result
    products = (grad[...] * field, field * result, result * result)
    for row, product in enumerate(products):
        total = jnp.sum(product, axis=(0, 1), keepdims=True)
        sums[row : row + 1, :] = jnp.broadcast_to(total, (1, lanes))
    sums[3:8, :] = jnp.zeros((5, lanes), jnp.float32)
    store_coefs(left_product(basis[...], result), payload, tiles)


def second_kernel(incoming, image, basis, second):
    second[...] = image[...] + left_product(basis[...], load_coefs(incoming, tiles))


def final_kernel(sums, search, grad, image, second, step, residual, direction):
    total = jnp.sum(sums[...], axis=0)
    first_product = total[0:1, 0:1]
    curvature = total[1:2, 0:1]
    image_product = total[2:3, 0:1]
    step_size = first_product / curvature
    ratio = step_size * (image_product / curvature) - 1.0
    field = search[:, :width]
    step[...] = step_size * field
    residual[...] = grad[...] - step_size * image[...]
    direction[...] = (field - step_size * second[...]) + ratio * field


def call(kernel, shapes, args, scratch=(), flops=0):
    in_specs = [pl.BlockSpec(memory_space=pltpu.SMEM if a.dtype == jnp.int32 and a.ndim == 1 else pltpu.VMEM) for a in args]
    outs = tuple(jax.ShapeDtypeStruct(s, jnp.float32) for s in shapes)
    moved = 4 * (sum(a.size for a in args) + sum(o.size for o in outs))
    return pl.pallas_call(
        kernel,
        out_shape=outs,
        in_specs=in_specs,
        out_specs=tuple(pl.BlockSpec(memory_space=pltpu.VMEM) for _ in outs),
        scratch_shapes=list(scratch),
        compiler_params=pltpu.CompilerParams(vmem_limit_bytes=vmem_bytes),
        cost_estimate=pl.CostEstimate(flops=flops, bytes_accessed=moved, transcendentals=0),
    )(*args)


def row_swaps():
    count = lax.axis_size("rows")
    inner = [(i, i ^ 1) for i in range(count)]
    outer = [(i, i + 1) for i in range(1, count - 1, 2)] + [(i + 1, i) for i in range(1, count - 1, 2)]
    return inner, outer


def swap_rows(send_a, send_b):
    inner, outer = row_swaps()
    return lax.ppermute(send_a, "rows", inner), lax.ppermute(send_b, "rows", outer)


def exchange(payload):
    return lax.all_to_all(payload, "cols", split_axis=0, concat_axis=0, tiled=True)


def sum_over_rows(value):
    count = lax.axis_size("rows")

    def swap(mask):
        return lax.ppermute(value, "rows", [(i, i ^ mask) for i in range(count)])

    value = value + swap(1)
    value = value + swap(2) + swap(4) + swap(6)
    return value + swap(8) + swap(16) + swap(24)


def on_device(latent, counts, exposure):
    consts = tables()
    tab = {name: jnp.asarray(value) for name, value in consts.items()}
    row_index = lax.axis_index("rows")
    place = jnp.stack([row_index, lax.axis_index("cols")]).astype(jnp.int32)
    pad = pltpu.VMEM((80, width + lanes), jnp.float32)
    wide = (parts, (tiles + 1) * lines, lanes)
    slim = (parts, tiles * lines, lanes)
    block = (band, width)
    filters = [
        tab[name]
        for name in (
            "row_term",
            "col_term",
            "weight",
            "outer_forward",
            "outer_inverse",
            "inner_forward",
            "inner_inverse",
            "twist",
        )
    ]

    even = row_index % 2 == 0
    top, bottom = latent[:2], latent[band - 2 :]
    swap_a, swap_b = swap_rows(jnp.where(even, bottom, top), jnp.where(even, top, bottom))
    payload, grad_part, beyond, fisher = call(
        gradient_kernel,
        (wide, block, (band, lanes), block),
        (place, latent, counts, exposure, swap_a, swap_b, tab["row_forward"]),
        (pad,),
        flops=10**8,
    )
    incoming = exchange(payload)
    ends = parts - 1
    from_left = lax.ppermute(beyond, "cols", [(i, i + 1) for i in range(ends)])
    from_right = lax.ppermute(beyond, "cols", [(i + 1, i) for i in range(ends)])
    back, _ = call(
        functools.partial(filter_kernel, edges=True),
        (wide, (8, lanes)),
        (place, incoming, *filters),
        flops=10**9,
    )
    incoming = exchange(back)
    grad, search, send_a, send_b = call(
        search_kernel,
        (block, (band, width + lanes), (2, width + lanes), (2, width + lanes)),
        (place, incoming, grad_part, from_left, from_right, tab["row_inverse"]),
        flops=10**8,
    )
    swap_a, swap_b = swap_rows(send_a, send_b)
    payload, image, sums = call(
        image_kernel,
        (slim, block, (8, lanes)),
        (place, search, swap_a, swap_b, fisher, grad, tab["row_forward"]),
        (pad,),
        flops=10**8,
    )
    incoming = exchange(payload)
    back, energy = call(
        functools.partial(filter_kernel, edges=False),
        (slim, (8, lanes)),
        (place, incoming, *filters),
        flops=10**9,
    )
    incoming = exchange(back)
    image_row = lax.broadcasted_iota(jnp.int32, (8, lanes), 0) == 2
    sums = sum_over_rows(sums + jnp.where(image_row, energy, 0.0))
    sums = exchange(jnp.broadcast_to(sums[None], (parts, 8, lanes)))
    (second,) = call(second_kernel, (block,), (incoming, image, tab["row_inverse"]), flops=10**8)
    return call(
        final_kernel, (block, block, block), (sums, search, grad, image, second), flops=10**6
    )


def solution(mesh):
    placed = (P("rows", "cols"), P("rows", "cols"), P("rows", "cols"))
    return jax.shard_map(
        on_device,
        mesh=mesh,
        in_specs=placed,
        out_specs=placed,
        check_vma=False,
    )
```

time: 569 us -> 132 us (0.23); the launches traced: 561 us -> 132 us
  blocking collectives: 238 us -> 42.6 us
  local copies, waits for them, and re-layouts: 189 us -> 3.81 us
  matrix products: 40.4 us -> 0 us
  other arithmetic: 19.3 us -> 1.06 us
  Pallas kernels: 0 us -> 10.9 us
    psum x2 -> x0, blocking collectives: 147 us -> none  [the longest x1 75.3 us: on_device(): first_product = lax.psum(jnp.sum(gradient * first_search), ('rows', 'cols'))]
    unnamed x11 -> x28, local copies, waits for them, and re-layouts: 122 us -> 3.19 us
    all_to_all x3 -> x2, blocking collectives: 91.4 us -> 42.6 us  [exchange(): lax.all_to_all(payload, 'cols', split_axis=0, concat_axis=0, tiled=True)]
    dot_general x40 -> x0, matrix products: 40.4 us -> none  [the longest x16 17.6 us: last_apply(): jnp.dot(data.reshape(line_rows * outer_len, inner_len), table, precision=...]
    another operation x12 -> x0, local copies, waits for them, and re-layouts: 35.3 us -> none  [the longest x6 32.4 us: precondition(): jnp.stack([back_real, back_imag])]
    all_to_all x5 -> x0, local copies, waits for them, and re-layouts: 28.2 us -> none  [the longest x3 27 us: precondition(): lax.all_to_all(jnp.stack([back_real, back_imag]), 'cols', split_axis=2, c...]
    pallas_call x0 -> x7, Pallas kernels: none -> 10.9 us  [call(): pl.pallas_call(kernel, out_shape=outs, in_specs=in_specs, out_specs=tuple...]
    all_to_all x1 -> x3, waiting for transfers between devices: 22.2 us -> 11.3 us  [exchange(): lax.all_to_all(payload, 'cols', split_axis=0, concat_axis=0, tiled=True)]
  transfers between devices with their start and end apart: 9 -> 16, of which waited for: 5 -> 9; matrix products, arithmetic and copies ran while one was open for 0% -> 0% of each run, Pallas kernels for 0% -> 0%
where the time goes in v1:
time: 132 us
  starting transfers between devices  42.6 us (32%)
  blocking collectives  42.6 us (32%)
  waiting for transfers between devices  29.7 us (22%)
  Pallas kernels  10.9 us (8%)
  local copies, waits for them, and re-layouts  3.81 us (3%)
    all_to_all x2, blocking collectives, exchange(): lax.all_to_all(payload, 'cols', split_axis=0, concat_axis=0, tiled=True)  42.6 us
    all_to_all x3, starting transfers between devices, exchange(): lax.all_to_all(payload, 'cols', split_axis=0, concat_axis=0, tiled=True)  14 us
    ppermute x2, starting transfers between devices, swap_rows(): lax.ppermute(send_b, 'rows', outer)  12.5 us
    all_to_all x3, waiting for transfers between devices, exchange(): lax.all_to_all(payload, 'cols', split_axis=0, concat_axis=0, tiled=True)  11.3 us
    pallas_call x7, Pallas kernels, call(): pl.pallas_call(kernel, out_shape=outs, in_specs=in_specs, out_specs=tuple...  10.9 us
    ppermute x7, starting transfers between devices, swap(): return lax.ppermute(value, 'rows', [(i, i ^ mask) for i in range(count)])  10.1 us
    ppermute x7, waiting for transfers between devices, swap(): return lax.ppermute(value, 'rows', [(i, i ^ mask) for i in range(count)])  8 us
    ppermute x1, waiting for transfers between devices, on_device(): from_right = lax.ppermute(beyond, 'cols', [(i + 1, i) for i in range(ends)])  5.99 us
  transfers between devices with their start and end apart: 16, of which 9 were waited for; matrix products, arithmetic and copies ran while one was open for 0% of the time, Pallas kernels for 0%

profile of v1, /device:TPU:8, one launch (start us, length us, event | category | flops | bytes accessed | tf_op | source)
XLA Modules:
  0.0 131.7 jit_solution(14322692724633651716)
XLA Ops:
  0.6 0.0 copy-start.4
  0.7 0.9 broadcast_select_fusion
  1.5 4.0 %collective-permute-start.1 = (f32[2,2048]{1,0:T(2,128)S(1)}, f32[2,2048]{1,0:T(2,128)S(1)}, u32[]{:S(2)}, u32[]{:S(2)}) collective-permute-start(f32[2,2048]{1,0:T(2,128)S(1)} %get-tuple-element.31), channel_id=1, source_target_pairs={{8,16},{24,32},{40,48},{56,64},{72,80},{88,96},{104,112},{120,128}... | collective-permute-start | bytes 49160 | tf_op jit(solution)/shard_map/ppermute | solution.py:342
  5.5 0.1 collective-permute-start
  5.7 0.1 pad_add_fusion.place
  5.7 3.0 %collective-permute-done.1.swap_b = f32[2,2048]{1,0:T(2,128)S(1)} collective-permute-done((f32[2,2048]{1,0:T(2,128)S(1)}, f32[2,2048]{1,0:T(2,128)S(1)}, u32[]{:S(2)}, u32[]{:S(2)}) %collective-permute-start.1) | collective-permute-done | bytes 16416 | tf_op jit(solution)/shard_map/ppermute | solution.py:342
  8.7 0.0 collective-permute-done.swap_a
  8.7 0.0 copy-done.4
  8.7 1.0 copy-done
  9.8 1.0 copy-done.1
  10.8 1.0 copy-done.2
  11.9 1.9 %shard_map.148 = (f32[8,136,128]{2,1,0:T(8,128)S(1)}, f32[64,2048]{1,0:T(8,128)S(1)}, f32[64,128]{1,0:T(8,128)S(1)}, f32[64,2048]{1,0:T(8,128)S(1)}) custom-call(s32[2]{0:T(128)S(1)} %pad_add_fusion.place, f32[64,2048]{1,0:T(8,128)S(1)} %copy-done, s32[64,2048]{1,0:T(8,128)S(1)} %copy-done.1, s32[64,2048]{1,0:T(8,128)S(1)} %copy-done.2, ...), custom_call_target="tpu_custom_call" | custom-call | flops 100000000 | bytes 3293192 | tf_op jit(solution)/shard_map/pallas_call | solution.py:322
  13.7 0.0 copy-start.5
  13.8 0.0 copy-start.6
  13.8 0.0 copy-start.7
  13.8 0.0 copy-start.8
  13.8 0.0 copy-start.9
  13.8 0.0 copy-start.10
  13.8 0.0 copy-start.11
  13.8 0.0 copy-start.12
  13.8 25.0 %all_to_all.25.incoming = f32[8,136,128]{2,1,0:T(8,128)S(1)} all-to-all(f32[8,136,128]{2,1,0:T(8,128)S(1)} %get-tuple-element.17), channel_id=1, replica_groups=mesh['rows'=32,'cols'=8] {'cols'}, dimensions={0} | all-to-all | bytes 1114112 | tf_op jit(solution)/shard_map/all_to_all | solution.py:346
  38.9 0.0 copy-done.5
  38.9 0.0 copy-done.6
  38.9 0.0 copy-done.7
  38.9 0.0 copy-done.8
  38.9 2.5 %shard_map.149 = (f32[8,136,128]{2,1,0:T(8,128)}, f32[8,128]{1,0:T(8,128)}) custom-call(s32[2]{0:T(128)S(1)} %pad_add_fusion.place, f32[8,136,128]{2,1,0:T(8,128)S(1)} %all_to_all.25.incoming, f32[64,128]{1,0:T(8,128)S(1)} %copy-done.12, f32[72,128]{1,0:T(8,128)S(1)} %copy-done.10, f32[72,128]{1,0:T(8,128)S(1)} %copy-done.11, ...), custom_call_target="tpu_custom_call" | custom-call | flops 1000000000 | bytes 2396168 | tf_op jit(solution)/shard_map/pallas_call | solution.py:322
  41.4 3.7 %all-to-all-start.1 = ((f32[8,136,128]{2,1,0:T(8,128)}), f32[8,136,128]{2,1,0:T(8,128)S(1)}, u32[]{:S(2)}, u32[]{:S(2)}) async-start(f32[8,136,128]{2,1,0:T(8,128)} %get-tuple-element.18), calls=%async_computation.1 | async-start | bytes 1114112 | tf_op jit(solution)/shard_map/all_to_all | solution.py:346
  45.1 1.3 collective-permute-start.3
  46.4 4.5 %collective-permute-start.2 = (f32[64,128]{1,0:T(8,128)S(1)}, f32[64,128]{1,0:T(8,128)S(1)}, u32[]{:S(2)}, u32[]{:S(2)}) collective-permute-start(f32[64,128]{1,0:T(8,128)S(1)} %get-tuple-element.20), channel_id=1, source_target_pairs={{0,1},{1,2},{2,3},{3,4},{4,5},{5,6},{6,7},{8,9},{9,10},{10,11},{11... | collective-permute-start | bytes 98312 | tf_op jit(solution)/shard_map/ppermute | solution.py:395
  50.9 6.0 %collective-permute-done.3.right = f32[64,128]{1,0:T(8,128)S(1)} collective-permute-done((f32[64,128]{1,0:T(8,128)S(1)}, f32[64,128]{1,0:T(8,128)S(1)}, u32[]{:S(2)}, u32[]{:S(2)}) %collective-permute-start.3) | collective-permute-done | bytes 32800 | tf_op jit(solution)/shard_map/ppermute | solution.py:396
  56.9 0.0 collective-permute-done.2.left
  56.9 3.6 %all-to-all-done.1.incoming = f32[8,136,128]{2,1,0:T(8,128)S(1)} async-done(((f32[8,136,128]{2,1,0:T(8,128)}), f32[8,136,128]{2,1,0:T(8,128)S(1)}, u32[]{:S(2)}, u32[]{:S(2)}) %all-to-all-start.1) | async-done | bytes 557088 | tf_op jit(solution)/shard_map/all_to_all | solution.py:346
  60.5 0.8 shard_map.150
  61.3 0.1 collective-permute-start.4
  61.4 8.5 %collective-permute-start.5 = (f32[2,2176]{1,0:T(2,128)S(1)}, f32[2,2176]{1,0:T(2,128)S(1)}, u32[]{:S(2)}, u32[]{:S(2)}) collective-permute-start(f32[2,2176]{1,0:T(2,128)S(1)} %get-tuple-element.23), channel_id=1, source_target_pairs={{8,16},{24,32},{40,48},{56,64},{72,80},{88,96},{104,112},{120,128}... | collective-permute-start | bytes 52232 | tf_op jit(solution)/shard_map/ppermute | solution.py:342
  70.0 0.0 collective-permute-done.4.swap_a
  70.0 1.4 %collective-permute-done.5.swap_b = f32[2,2176]{1,0:T(2,128)S(1)} collective-permute-done((f32[2,2176]{1,0:T(2,128)S(1)}, f32[2,2176]{1,0:T(2,128)S(1)}, u32[]{:S(2)}, u32[]{:S(2)}) %collective-permute-start.5) | collective-permute-done | bytes 17440 | tf_op jit(solution)/shard_map/ppermute | solution.py:342
  71.4 1.8 %shard_map.151 = (f32[8,128,128]{2,1,0:T(8,128)S(1)}, f32[64,2048]{1,0:T(8,128)S(1)}, f32[8,128]{1,0:T(8,128)S(1)}) custom-call(s32[2]{0:T(128)S(1)} %pad_add_fusion.place, f32[64,2176]{1,0:T(8,128)S(1)} %get-tuple-element.21.search, f32[2,2176]{1,0:T(2,128)S(1)} %collective-permute-done.4.swap_a, f32[2,2176]{1,0:T(2,128)S(1)} %collective-permute-done.5.swap_b, ...), custom_call_target="tpu_custom_call" | custom-call | flops 100000000 | bytes 2742280 | tf_op jit(solution)/shard_map/pallas_call | solution.py:322
  73.2 0.0 copy-start.13
  73.2 17.6 %all_to_all.26.incoming = f32[8,128,128]{2,1,0:T(8,128)S(1)} all-to-all(f32[8,128,128]{2,1,0:T(8,128)S(1)} %get-tuple-element.27), channel_id=1, replica_groups=mesh['rows'=32,'cols'=8] {'cols'}, dimensions={0} | all-to-all | bytes 1048576 | tf_op jit(solution)/shard_map/all_to_all | solution.py:346
  90.8 0.0 copy-done.13
  90.8 2.4 %shard_map.152 = (f32[8,128,128]{2,1,0:T(8,128)}, f32[8,128]{1,0:T(8,128)S(1)}) custom-call(s32[2]{0:T(128)S(1)} %pad_add_fusion.place, f32[8,128,128]{2,1,0:T(8,128)S(1)} %all_to_all.26.incoming, f32[64,128]{1,0:T(8,128)S(1)} %copy-done.13, f32[72,128]{1,0:T(8,128)S(1)} %copy-done.10, f32[72,128]{1,0:T(8,128)S(1)} %copy-done.11, ...), custom_call_target="tpu_custom_call" | custom-call | flops 1000000000 | bytes 2330632 | tf_op jit(solution)/shard_map/pallas_call | solution.py:322
  93.2 3.5 %all-to-all-start.4 = ((f32[8,128,128]{2,1,0:T(8,128)}), f32[8,128,128]{2,1,0:T(8,128)S(1)}, u32[]{:S(2)}, u32[]{:S(2)}) async-start(f32[8,128,128]{2,1,0:T(8,128)} %get-tuple-element.30), calls=%async_computation.4 | async-start | bytes 1048576 | tf_op jit(solution)/shard_map/all_to_all | solution.py:346
  96.7 0.1 select_add_fusion
  96.8 0.0 collective-permute-start.6
  96.8 1.2 collective-permute-done.6
  98.0 5.0 %collective-permute-start.9 = (f32[8,128]{1,0:T(8,128)S(1)}, f32[8,128]{1,0:T(8,128)S(1)}, u32[]{:S(2)}, u32[]{:S(2)}) collective-permute-start(f32[8,128]{1,0:T(8,128)S(1)} %add.30), channel_id=1, source_target_pairs={{0,48},{8,56},{16,32},{24,40},{32,16},{40,24},{48,0},{56,8},{64,11... | collective-permute-start | bytes 12296 | tf_op jit(solution)/shard_map/ppermute | solution.py:353
  103.0 0.0 collective-permute-start.8
  103.0 0.9 collective-permute-start.7
  103.8 0.7 collective-permute-done.9
  104.6 3.5 %collective-permute-done.8 = f32[8,128]{1,0:T(8,128)S(1)} collective-permute-done((f32[8,128]{1,0:T(8,128)S(1)}, f32[8,128]{1,0:T(8,128)S(1)}, u32[]{:S(2)}, u32[]{:S(2)}) %collective-permute-start.8) | collective-permute-done | bytes 4128 | tf_op jit(solution)/shard_map/ppermute | solution.py:353
  108.1 0.0 collective-permute-done.7
  108.1 1.7 %collective-permute-start.12 = (f32[8,128]{1,0:T(8,128)S(1)}, f32[8,128]{1,0:T(8,128)S(1)}, u32[]{:S(2)}, u32[]{:S(2)}) collective-permute-start(f32[8,128]{1,0:T(8,128)S(1)} %add_add_fusion.1), channel_id=1, source_target_pairs={{0,192},{8,200},{16,208},{24,216},{32,224},{40,232},{48,240},{56,2... | collective-permute-start | bytes 12296 | tf_op jit(solution)/shard_map/ppermute | solution.py:353
  109.8 0.9 collective-permute-start.11
  110.7 1.6 %collective-permute-start.10 = (f32[8,128]{1,0:T(8,128)S(1)}, f32[8,128]{1,0:T(8,128)S(1)}, u32[]{:S(2)}, u32[]{:S(2)}) collective-permute-start(f32[8,128]{1,0:T(8,128)S(1)} %add_add_fusion.1), channel_id=1, source_target_pairs={{0,64},{8,72},{16,80},{24,88},{32,96},{40,104},{48,112},{56,120},{... | collective-permute-start | bytes 12296 | tf_op jit(solution)/shard_map/ppermute | solution.py:353
  112.3 0.0 collective-permute-done.12
  112.3 2.6 %collective-permute-done.11 = f32[8,128]{1,0:T(8,128)S(1)} collective-permute-done((f32[8,128]{1,0:T(8,128)S(1)}, f32[8,128]{1,0:T(8,128)S(1)}, u32[]{:S(2)}, u32[]{:S(2)}) %collective-permute-start.11) | collective-permute-done | bytes 4128 | tf_op jit(solution)/shard_map/ppermute | solution.py:353
  114.9 0.0 collective-permute-done.10
  114.9 0.0 all-to-all-done.4.incoming
  114.9 0.6 broadcast_in_dim.11
  115.5 6.8 %all-to-all-start.3 = ((f32[8,8,128]{2,1,0:T(8,128)}), f32[8,8,128]{2,1,0:T(8,128)S(1)}, u32[]{:S(2)}, u32[]{:S(2)}) async-start(f32[8,8,128]{2,1,0:T(8,128)} %broadcast_in_dim.11), calls=%async_computation.3 | async-start | bytes 65536 | tf_op jit(solution)/shard_map/all_to_all | solution.py:346
  122.4 0.3 shard_map.153.second
  122.6 7.8 %all-to-all-done.3.sums = f32[8,8,128]{2,1,0:T(8,128)S(1)} async-done(((f32[8,8,128]{2,1,0:T(8,128)}), f32[8,8,128]{2,1,0:T(8,128)S(1)}, u32[]{:S(2)}, u32[]{:S(2)}) %all-to-all-start.3) | async-done | bytes 32800 | tf_op jit(solution)/shard_map/all_to_all | solution.py:346
  130.4 1.3 shard_map.154
  (13 shorter events, 0.0 us)
Async XLA Ops:
  0.6 8.1 %copy-start.4 = (bf16[64,192]{1,0:T(8,128)(2,1)S(1)}, bf16[64,192]{1,0:T(8,128)(2,1)}, u32[]{:S(2)}) copy-start(bf16[64,192]{1,0:T(8,128)(2,1)} %constant.46.clone.basis) | copy-start | bytes 73732
  1.5 7.2 %collective-permute-start.1 = (f32[2,2048]{1,0:T(2,128)S(1)}, f32[2,2048]{1,0:T(2,128)S(1)}, u32[]{:S(2)}, u32[]{:S(2)}) collective-permute-start(f32[2,2048]{1,0:T(2,128)S(1)} %get-tuple-element.31), channel_id=1, source_target_pairs={{8,16},{24,32},{40,48},{56,64},{72,80},{88,96},{104,112},{120,128}... | collective-permute-start | bytes 49160 | tf_op jit(solution)/shard_map/ppermute | solution.py:342
  5.5 3.2 %collective-permute-start = (f32[2,2048]{1,0:T(2,128)S(1)}, f32[2,2048]{1,0:T(2,128)S(1)}, u32[]{:S(2)}, u32[]{:S(2)}) collective-permute-start(f32[2,2048]{1,0:T(2,128)S(1)} %get-tuple-element.32), channel_id=1, source_target_pairs={{0,8},{8,0},{16,24},{24,16},{32,40},{40,32},{48,56},{56,48},{64,72... | collective-permute-start | bytes 49160 | tf_op jit(solution)/shard_map/ppermute | solution.py:342
  8.7 1.0 copy-start
  9.8 1.0 copy-start.1
  10.8 1.0 copy-start.2
  13.7 25.1 %copy-start.5 = (bf16[384,256]{1,0:T(8,128)(2,1)S(1)}, bf16[384,256]{1,0:T(8,128)(2,1)}, u32[]{:S(2)}) copy-start(bf16[384,256]{1,0:T(8,128)(2,1)} %constant.53.clone.inner_inverse) | copy-start | bytes 589828
  13.8 25.1 %copy-start.6 = (bf16[256,256]{1,0:T(8,128)(2,1)S(1)}, bf16[256,256]{1,0:T(8,128)(2,1)}, u32[]{:S(2)}) copy-start(bf16[256,256]{1,0:T(8,128)(2,1)} %constant.52.clone.inner_forward) | copy-start | bytes 393220
  13.8 25.1 %copy-start.7 = (bf16[128,432]{1,0:T(8,128)(2,1)S(1)}, bf16[128,432]{1,0:T(8,128)(2,1)}, u32[]{:S(2)}) copy-start(bf16[128,432]{1,0:T(8,128)(2,1)} %constant.50.clone.outer_inverse) | copy-start | bytes 331780
  13.8 25.1 %copy-start.8 = (bf16[144,384]{1,0:T(8,128)(2,1)S(1)}, bf16[144,384]{1,0:T(8,128)(2,1)}, u32[]{:S(2)}) copy-start(bf16[144,384]{1,0:T(8,128)(2,1)} %constant.49.clone.outer_forward) | copy-start | bytes 331780
  13.8 25.1 %copy-start.9 = (f32[2,72,128]{2,1,0:T(8,128)S(1)}, f32[2,72,128]{2,1,0:T(8,128)}, u32[]{:S(2)}) copy-start(f32[2,72,128]{2,1,0:T(8,128)} %constant.51.clone.twist) | copy-start | bytes 221188
  13.8 25.1 %copy-start.10 = (f32[72,128]{1,0:T(8,128)S(1)}, f32[72,128]{1,0:T(8,128)}, u32[]{:S(2)}) copy-start(f32[72,128]{1,0:T(8,128)} %constant.55.clone.col_term) | copy-start | bytes 110596
  13.8 25.1 %copy-start.11 = (f32[72,128]{1,0:T(8,128)S(1)}, f32[72,128]{1,0:T(8,128)}, u32[]{:S(2)}) copy-start(f32[72,128]{1,0:T(8,128)} %constant.54.clone.weight) | copy-start | bytes 110596
  13.8 25.1 %copy-start.12 = (f32[64,128]{1,0:T(8,128)S(1)}, f32[64,128]{1,0:T(8,128)}, u32[]{:S(2)}) copy-start(f32[64,128]{1,0:T(8,128)} %constant.48.clone.row_term) | copy-start | bytes 98308
  41.4 19.1 %copy-start.3 = (bf16[64,192]{1,0:T(8,128)(2,1)S(1)}, bf16[64,192]{1,0:T(8,128)(2,1)}, u32[]{:S(2)}) copy-start(bf16[64,192]{1,0:T(8,128)(2,1)} %constant.47.clone.basis) | copy-start | bytes 73732
  41.4 19.1 %all-to-all-start.1 = ((f32[8,136,128]{2,1,0:T(8,128)}), f32[8,136,128]{2,1,0:T(8,128)S(1)}, u32[]{:S(2)}, u32[]{:S(2)}) async-start(f32[8,136,128]{2,1,0:T(8,128)} %get-tuple-element.18), calls=%async_computation.1 | async-start | bytes 1114112 | tf_op jit(solution)/shard_map/all_to_all | solution.py:346
  45.1 11.8 %collective-permute-start.3 = (f32[64,128]{1,0:T(8,128)S(1)}, f32[64,128]{1,0:T(8,128)S(1)}, u32[]{:S(2)}, u32[]{:S(2)}) collective-permute-start(f32[64,128]{1,0:T(8,128)S(1)} %get-tuple-element.20), channel_id=1, source_target_pairs={{1,0},{2,1},{3,2},{4,3},{5,4},{6,5},{7,6},{9,8},{10,9},{11,10},{12... | collective-permute-start | bytes 98312 | tf_op jit(solution)/shard_map/ppermute | solution.py:396
  46.4 10.6 %collective-permute-start.2 = (f32[64,128]{1,0:T(8,128)S(1)}, f32[64,128]{1,0:T(8,128)S(1)}, u32[]{:S(2)}, u32[]{:S(2)}) collective-permute-start(f32[64,128]{1,0:T(8,128)S(1)} %get-tuple-element.20), channel_id=1, source_target_pairs={{0,1},{1,2},{2,3},{3,4},{4,5},{5,6},{6,7},{8,9},{9,10},{10,11},{11... | collective-permute-start | bytes 98312 | tf_op jit(solution)/shard_map/ppermute | solution.py:395
  61.3 8.6 %collective-permute-start.4 = (f32[2,2176]{1,0:T(2,128)S(1)}, f32[2,2176]{1,0:T(2,128)S(1)}, u32[]{:S(2)}, u32[]{:S(2)}) collective-permute-start(f32[2,2176]{1,0:T(2,128)S(1)} %get-tuple-element.22), channel_id=1, source_target_pairs={{0,8},{8,0},{16,24},{24,16},{32,40},{40,32},{48,56},{56,48},{64,72... | collective-permute-start | bytes 52232 | tf_op jit(solution)/shard_map/ppermute | solution.py:342
  61.4 10.0 %collective-permute-start.5 = (f32[2,2176]{1,0:T(2,128)S(1)}, f32[2,2176]{1,0:T(2,128)S(1)}, u32[]{:S(2)}, u32[]{:S(2)}) collective-permute-start(f32[2,2176]{1,0:T(2,128)S(1)} %get-tuple-element.23), channel_id=1, source_target_pairs={{8,16},{24,32},{40,48},{56,64},{72,80},{88,96},{104,112},{120,128}... | collective-permute-start | bytes 52232 | tf_op jit(solution)/shard_map/ppermute | solution.py:342
  73.2 17.6 %copy-start.13 = (f32[64,128]{1,0:T(8,128)S(1)}, f32[64,128]{1,0:T(8,128)}, u32[]{:S(2)}) copy-start(f32[64,128]{1,0:T(8,128)} %constant.48.clone.row_term) | copy-start | bytes 98308
  93.2 21.7 %all-to-all-start.4 = ((f32[8,128,128]{2,1,0:T(8,128)}), f32[8,128,128]{2,1,0:T(8,128)S(1)}, u32[]{:S(2)}, u32[]{:S(2)}) async-start(f32[8,128,128]{2,1,0:T(8,128)} %get-tuple-element.30), calls=%async_computation.4 | async-start | bytes 1048576 | tf_op jit(solution)/shard_map/all_to_all | solution.py:346
  96.8 1.2 collective-permute-start.6
  98.0 6.6 %collective-permute-start.9 = (f32[8,128]{1,0:T(8,128)S(1)}, f32[8,128]{1,0:T(8,128)S(1)}, u32[]{:S(2)}, u32[]{:S(2)}) collective-permute-start(f32[8,128]{1,0:T(8,128)S(1)} %add.30), channel_id=1, source_target_pairs={{0,48},{8,56},{16,32},{24,40},{32,16},{40,24},{48,0},{56,8},{64,11... | collective-permute-start | bytes 12296 | tf_op jit(solution)/shard_map/ppermute | solution.py:353
  103.0 5.1 %collective-permute-start.8 = (f32[8,128]{1,0:T(8,128)S(1)}, f32[8,128]{1,0:T(8,128)S(1)}, u32[]{:S(2)}, u32[]{:S(2)}) collective-permute-start(f32[8,128]{1,0:T(8,128)S(1)} %add.30), channel_id=1, source_target_pairs={{0,32},{8,40},{16,48},{24,56},{32,0},{40,8},{48,16},{56,24},{64,96... | collective-permute-start | bytes 12296 | tf_op jit(solution)/shard_map/ppermute | solution.py:353
  103.0 5.1 %collective-permute-start.7 = (f32[8,128]{1,0:T(8,128)S(1)}, f32[8,128]{1,0:T(8,128)S(1)}, u32[]{:S(2)}, u32[]{:S(2)}) collective-permute-start(f32[8,128]{1,0:T(8,128)S(1)} %add.30), channel_id=1, source_target_pairs={{0,16},{8,24},{16,0},{24,8},{32,48},{40,56},{48,32},{56,40},{64,80... | collective-permute-start | bytes 12296 | tf_op jit(solution)/shard_map/ppermute | solution.py:353
  108.1 4.2 %collective-permute-start.12 = (f32[8,128]{1,0:T(8,128)S(1)}, f32[8,128]{1,0:T(8,128)S(1)}, u32[]{:S(2)}, u32[]{:S(2)}) collective-permute-start(f32[8,128]{1,0:T(8,128)S(1)} %add_add_fusion.1), channel_id=1, source_target_pairs={{0,192},{8,200},{16,208},{24,216},{32,224},{40,232},{48,240},{56,2... | collective-permute-start | bytes 12296 | tf_op jit(solution)/shard_map/ppermute | solution.py:353
  109.8 5.1 %collective-permute-start.11 = (f32[8,128]{1,0:T(8,128)S(1)}, f32[8,128]{1,0:T(8,128)S(1)}, u32[]{:S(2)}, u32[]{:S(2)}) collective-permute-start(f32[8,128]{1,0:T(8,128)S(1)} %add_add_fusion.1), channel_id=1, source_target_pairs={{0,128},{8,136},{16,144},{24,152},{32,160},{40,168},{48,176},{56,1... | collective-permute-start | bytes 12296 | tf_op jit(solution)/shard_map/ppermute | solution.py:353
  110.7 4.2 %collective-permute-start.10 = (f32[8,128]{1,0:T(8,128)S(1)}, f32[8,128]{1,0:T(8,128)S(1)}, u32[]{:S(2)}, u32[]{:S(2)}) collective-permute-start(f32[8,128]{1,0:T(8,128)S(1)} %add_add_fusion.1), channel_id=1, source_target_pairs={{0,64},{8,72},{16,80},{24,88},{32,96},{40,104},{48,112},{56,120},{... | collective-permute-start | bytes 12296 | tf_op jit(solution)/shard_map/ppermute | solution.py:353
  115.5 14.9 %all-to-all-start.3 = ((f32[8,8,128]{2,1,0:T(8,128)}), f32[8,8,128]{2,1,0:T(8,128)S(1)}, u32[]{:S(2)}, u32[]{:S(2)}) async-start(f32[8,8,128]{2,1,0:T(8,128)} %broadcast_in_dim.11), calls=%async_computation.3 | async-start | bytes 65536 | tf_op jit(solution)/shard_map/all_to_all | solution.py:346

commit v2 on v1

--- a/solution.py
+++ b/solution.py
@@ -51,6 +51,13 @@
     out = {}
     high, low = high_low(basis)
     out["row_forward"] = np.concatenate([high, high, low], 1)
+    share = np.zeros((band, 16))
+    for row, at in ((0, 0), (1, 1), (2, band - 2), (3, band - 1)):
+        share[:, row] = prior_scale * basis[:, at]
+    share[:, 8 + 1] = prior_scale * basis[:, 0]
+    share[:, 8 + 2] = prior_scale * basis[:, band - 1]
+    high, low = high_low(share)
+    out["halo_forward"] = np.concatenate([high, high, low], 1)
     high, low = high_low(basis.T)
     out["row_inverse"] = np.concatenate([high, high, low], 1)
     out["row_term"] = np.tile(row_term[:, None], (1, lanes)).astype(np.float32)
@@ -115,30 +122,81 @@
     return lax.broadcasted_iota(jnp.int32, shape, 1)
 
 
+def neighbours(field):
+    full = field.shape[1]
+    return pltpu.roll(field, 1, 1) + pltpu.roll(field, full - 1, 1)
+
+
 def stencil(pad):
     full = width + lanes
     field = pad[8:72, :]
     near = pad[7:71, :] + pad[9:73, :]
     far = pad[6:70, :] + pad[10:74, :]
-    beside = 2.0 * near - (2.0 * centre) * field
-    across = pltpu.roll(beside, 1, 1) + pltpu.roll(beside, full - 1, 1)
+    across = neighbours(2.0 * near - (2.0 * centre) * field)
     distant = far + pltpu.roll(field, 2, 1) + pltpu.roll(field, full - 2, 1)
     return prior_scale * ((centre * centre + 4.0) * field - 2.0 * centre * near + across + distant)
 
 
-def store_coefs(coefs, out, count):
+def halo_terms(place, swap_a, swap_b, halo):
+    even = place[0] % 2 == 0
+    span = swap_a.shape[1]
+    halo[...] = jnp.zeros((8, width + lanes), jnp.float32)
+    halo[0:2, :span] = jnp.where(even, swap_b[...], swap_a[...])
+    halo[2:4, :span] = jnp.where(even, swap_a[...], swap_b[...])
+    rows = halo[...]
+    beside = 2.0 * neighbours(rows) - (2.0 * centre) * rows
+    return rows, beside
+
+
+def halo_rows(rows, beside):
+    return prior_scale * jnp.concatenate(
+        [
+            beside[1:2] + rows[0:1],
+            rows[1:2],
+            jnp.zeros((4, width + lanes), jnp.float32),
+            rows[2:3],
+            beside[2:3] + rows[3:4],
+        ],
+        0,
+    )
+
+
+def add_halo_rows(field, added):
+    index = lax.broadcasted_iota(jnp.int32, added.shape, 0)
+    return jnp.concatenate(
+        [
+            field[:8] + jnp.where(index < 4, added, 0.0),
+            field[8 : band - 8],
+            field[band - 8 :] + jnp.where(index >= 4, added, 0.0),
+        ],
+        0,
+    )
+
+
+def store_coefs(place, coefs, buffer, outs, count):
     for part in range(parts):
         for tile in range(count):
-            out[part, tile * lines : (tile + 1) * lines, :] = coefs[
+            buffer[part, tile * lines : (tile + 1) * lines, :] = coefs[
                 part * lines : (part + 1) * lines, tile * lanes : (tile + 1) * lanes
             ]
-
-
-def load_coefs(ref, count):
+    store_blocks(place, buffer, outs)
+
+
+def store_blocks(place, buffer, outs):
+    for mask, out in enumerate(outs):
+        out[...] = buffer[place[1] ^ mask]
+
+
+def load_blocks(place, refs, buffer):
+    for mask, ref in enumerate(refs):
+        buffer[place[1] ^ mask] = ref[...]
+
+
+def load_coefs(buffer, count):
     return jnp.concatenate(
         [
             jnp.concatenate(
-                [ref[part, tile * lines : (tile + 1) * lines, :] for part in range(parts)], 0
+                [buffer[part, tile * lines : (tile + 1) * lines, :] for part in range(parts)], 0
             )
             for tile in range(count)
         ],
@@ -146,47 +204,50 @@
     )
 
 
-def gradient_kernel(
-    place, latent, counts, exposure, swap_a, swap_b, basis, payload, grad, beyond, fisher, pad
-):
-    even = place[0] % 2 == 0
+def gradient_kernel(latent, counts, exposure, basis, coefs, grad, fisher, pad):
+    pad[0:8, :] = jnp.zeros((8, width + lanes), jnp.float32)
+    pad[72:80, :] = jnp.zeros((8, width + lanes), jnp.float32)
     pad[8:72, :width] = latent[...]
-    pad[6:8, :width] = jnp.where(even, swap_b[...], swap_a[...])
-    pad[72:74, :width] = jnp.where(even, swap_a[...], swap_b[...])
-    pad[0:80, width:] = jnp.zeros((80, lanes), jnp.float32)
+    pad[8:72, width:] = jnp.zeros((band, lanes), jnp.float32)
     prior = stencil(pad)
     mean_rate = exposure[...].astype(jnp.float32) * jnp.exp(latent[...])
     ratio = dispersion / (dispersion + mean_rate)
     fisher[...] = mean_rate * ratio
     score = (counts[...].astype(jnp.float32) - mean_rate) * ratio
     inside = score - prior[:, :width]
-    outside = -prior[:, width:]
     grad[...] = inside
-    beyond[...] = outside
-    coefs = left_product(basis[...], jnp.concatenate([inside, outside], 1))
-    store_coefs(coefs, payload, tiles + 1)
-
-
-def filter_kernel(
-    place,
-    incoming,
-    row_term,
-    col_term,
-    weight,
-    outer_forward,
-    outer_inverse,
-    inner_forward,
-    inner_inverse,
-    twist,
-    out,
-    energy,
-    *,
-    edges,
-):
+    coefs[...] = left_product(basis[...], jnp.concatenate([inside, -prior[:, width:]], 1))
+
+
+def gradient_halo_kernel(place, coefs, swap_a, swap_b, basis, *rest):
+    outs, (added, halo, buffer) = rest[:parts], rest[parts:]
+    rows, beside = halo_terms(place, swap_a, swap_b, halo)
+    added[...] = -halo_rows(rows, beside)
+    whole = coefs[...] - left_product(basis[...], jnp.concatenate([rows, beside], 0))
+    spill = whole[:, width:]
+    spill = spill + pltpu.roll(spill, lanes // 2, 1)
+    store_coefs(place, jnp.concatenate([whole[:, :width], spill], 1), buffer, outs, tiles + 1)
+
+
+def filter_kernel(place, *rest, edges):
+    blocks_in, rest = rest[:parts], rest[parts:]
+    (
+        sums,
+        row_term,
+        col_term,
+        weight,
+        outer_forward,
+        outer_inverse,
+        inner_forward,
+        inner_inverse,
+        twist,
+    ) = rest[:9]
+    blocks_out, (incoming, out) = rest[9 : 9 + parts], rest[9 + parts :]
+    load_blocks(place, blocks_in, incoming)
     lane = lane_index((tiles, lanes))
     sub = lax.broadcasted_iota(jnp.int32, (tiles, lanes), 0)
-    first = (sub == 0) & (lane < lanes // 2)
-    last = (sub == tiles - 1) & (lane >= lanes // 2)
+    first = (sub == 0) & (lane < 2)
+    last = (sub == tiles - 1) & (lane >= lanes - 2)
     line_fields = []
     for line in range(lines):
         blocks = [
@@ -228,7 +289,11 @@
         if not edges:
             total = total + piece * scaled[-1]
     if not edges:
-        energy[...] = jnp.broadcast_to(jnp.sum(total, axis=(0, 1), keepdims=True), (8, lanes))
+        energy = jnp.sum(total, axis=(0, 1), keepdims=True)
+        third = lax.broadcasted_iota(jnp.int32, (8, lanes), 0) == 2
+        known = sums[...] + jnp.where(third, energy, 0.0)
+        for part in range(parts):
+            out[part, tiles * lines :, :] = known
     high, low = split(jnp.concatenate(scaled, 0))
     back = dot(jnp.concatenate([high, low], 1), inner_inverse[: 4 * kept, :]) + dot(
         high, inner_inverse[4 * kept :, :]
@@ -241,7 +306,8 @@
         imags.append(imag * cosine + real * sine)
     folded = jnp.concatenate([jnp.concatenate(reals, 1), jnp.concatenate(imags, 1)], 0)
     result = left_product(outer_inverse[...], folded)
-    edge_lane = lane_index((1, lanes)) < lanes // 2
+    edge_lane = lane_index((1, lanes))
+    nothing = jnp.zeros((1, lanes), jnp.float32)
     for line in range(lines):
         cols = slice(line * lanes, (line + 1) * lanes)
         for part in range(parts):
@@ -249,57 +315,84 @@
                 part * tiles : (part + 1) * tiles, cols
             ]
         if edges:
+            spot = tiles * lines + line
             for part in range(parts):
-                nothing = jnp.zeros((1, lanes), jnp.float32)
-                after, before = nothing, nothing
+                after, before, from_left, from_right = nothing, nothing, nothing, nothing
                 if part < parts - 1:
                     row = slice((part + 1) * tiles, (part + 1) * tiles + 1)
                     after = result[row, cols] + field[row, cols]
+                    from_right = incoming[part + 1, spot : spot + 1, :]
                 if part > 0:
                     row = slice(part * tiles - 1, part * tiles)
                     before = result[row, cols] + field[row, cols]
-                out[part, tiles * lines + line : tiles * lines + line + 1, :] = jnp.where(
-                    edge_lane, after, before
+                    from_left = incoming[part - 1, spot : spot + 1, :]
+                middle = jnp.where(edge_lane >= lanes // 2, from_left, from_right)
+                out[part, spot : spot + 1, :] = jnp.where(
+                    edge_lane < 2, after, jnp.where(edge_lane >= lanes - 2, before, middle)
                 )
-
-
-def search_kernel(place, incoming, grad, left, right, basis, full_grad, search, send_a, send_b):
+    store_blocks(place, out, blocks_out)
+
+
+def search_kernel(place, *rest):
+    blocks, (grad, added, basis, full_grad, search, send_a, send_b, buffer) = (
+        rest[:parts],
+        rest[parts:],
+    )
     even = place[0] % 2 == 0
-    coefs = load_coefs(incoming, tiles + 1)
-    update = left_product(basis[...], coefs)
+    load_blocks(place, blocks, buffer)
+    update = left_product(basis[...], load_coefs(buffer, tiles + 1))
+    beyond = update[:, width:]
+    spill = pltpu.roll(beyond, lanes // 2, 1)
     lane = lane_index((band, lanes))
-    head = grad[:, :lanes] + jnp.where(lane < lanes // 2, left[...], 0.0)
-    tail = grad[:, width - lanes :] + jnp.where(lane >= lanes // 2, right[...], 0.0)
-    whole = jnp.concatenate([head, grad[:, lanes : width - lanes], tail], 1)
+    base = add_halo_rows(grad[...], added[:, :width])
+    head = base[:, :lanes] + jnp.where(lane < 2, spill, 0.0)
+    tail = base[:, width - lanes :] + jnp.where(lane >= lanes - 2, spill, 0.0)
+    whole = jnp.concatenate([head, base[:, lanes : width - lanes], tail], 1)
     full_grad[...] = whole
-    found = jnp.concatenate([whole + update[:, :width], update[:, width:]], 1)
+    found = jnp.concatenate([whole + update[:, :width], beyond], 1)
     search[...] = found
     top, bottom = found[:2, :], found[band - 2 :, :]
     send_a[...] = jnp.where(even, bottom, top)
     send_b[...] = jnp.where(even, top, bottom)
 
 
-def image_kernel(
-    place, search, swap_a, swap_b, fisher, grad, basis, payload, image, sums, pad
-):
-    even = place[0] % 2 == 0
+def image_kernel(search, fisher, basis, coefs, image, pad):
+    pad[0:8, :] = jnp.zeros((8, width + lanes), jnp.float32)
+    pad[72:80, :] = jnp.zeros((8, width + lanes), jnp.float32)
     pad[8:72, :] = search[...]
-    pad[6:8, :] = jnp.where(even, swap_b[...], swap_a[...])
-    pad[72:74, :] = jnp.where(even, swap_a[...], swap_b[...])
-    prior = stencil(pad)
+    result = stencil(pad)[:, :width] + fisher[...] * search[:, :width]
+    image[...] = result
+    coefs[...] = left_product(basis[...], result)
+
+
+def image_halo_kernel(place, coefs, swap_a, swap_b, basis, *rest):
+    outs, (added, halo, buffer) = rest[:parts], rest[parts:]
+    rows, beside = halo_terms(place, swap_a, swap_b, halo)
+    added[...] = halo_rows(rows, beside)
+    both = jnp.concatenate([rows, beside], 0)[:, :width]
+    store_coefs(place, coefs[...] + left_product(basis[...], both), buffer, outs, tiles)
+
+
+def sums_kernel(search, grad, partial, added, image, sums):
     field = search[:, :width]
-    result = prior[:, :width] + fisher[...] * field
+    result = add_halo_rows(partial[...], added[:, :width])
     image[...] = result
     products = (grad[...] * field, field * result, result * result)
     for row, product in enumerate(products):
         total = jnp.sum(product, axis=(0, 1), keepdims=True)
         sums[row : row + 1, :] = jnp.broadcast_to(total, (1, lanes))
     sums[3:8, :] = jnp.zeros((5, lanes), jnp.float32)
-    store_coefs(left_product(basis[...], result), payload, tiles)
-
-
-def second_kernel(incoming, image, basis, second):
-    second[...] = image[...] + left_product(basis[...], load_coefs(incoming, tiles))
+
+
+def second_kernel(place, *rest):
+    blocks, (image, basis, second, spread, buffer) = rest[:parts], rest[parts:]
+    load_blocks(place, blocks, buffer)
+    total = buffer[0, tiles * lines :, :]
+    for part in range(1, parts):
+        total = total + buffer[part, tiles * lines :, :]
+    for row in range(spread.shape[0]):
+        spread[row] = total
+    second[...] = image[...] + left_product(basis[...], load_coefs(buffer, tiles))
 
 
 def final_kernel(sums, search, grad, image, second, step, residual, direction):
@@ -337,24 +430,17 @@
     return inner, outer
 
 
+def exchange(blocks):
+    count = lax.axis_size("cols")
+    got = {}
+    for mask in (4, 3, 5, 2, 6, 1, 7):
+        got[mask] = lax.ppermute(blocks[mask], "cols", [(i, i ^ mask) for i in range(count)])
+    return [blocks[0]] + [got[mask] for mask in range(1, parts)]
+
+
 def swap_rows(send_a, send_b):
     inner, outer = row_swaps()
     return lax.ppermute(send_a, "rows", inner), lax.ppermute(send_b, "rows", outer)
-
-
-def exchange(payload):
-    return lax.all_to_all(payload, "cols", split_axis=0, concat_axis=0, tiled=True)
-
-
-def sum_over_rows(value):
-    count = lax.axis_size("rows")
-
-    def swap(mask):
-        return lax.ppermute(value, "rows", [(i, i ^ mask) for i in range(count)])
-
-    value = value + swap(1)
-    value = value + swap(2) + swap(4) + swap(6)
-    return value + swap(8) + swap(16) + swap(24)
 
 
 def on_device(latent, counts, exposure):
@@ -362,10 +448,15 @@
     tab = {name: jnp.asarray(value) for name, value in consts.items()}
     row_index = lax.axis_index("rows")
     place = jnp.stack([row_index, lax.axis_index("cols")]).astype(jnp.int32)
-    pad = pltpu.VMEM((80, width + lanes), jnp.float32)
-    wide = (parts, (tiles + 1) * lines, lanes)
-    slim = (parts, tiles * lines, lanes)
+    full = width + lanes
+    pad = pltpu.VMEM((80, full), jnp.float32)
+    halo = pltpu.VMEM((8, full), jnp.float32)
+    wide = ((tiles + 1) * lines, lanes)
+    slim = (tiles * lines, lanes)
+    wide_buffer = pltpu.VMEM((parts, *wide), jnp.float32)
+    slim_buffer = pltpu.VMEM((parts, *slim), jnp.float32)
     block = (band, width)
+    extended = (band, full)
     filters = [
         tab[name]
         for name in (
@@ -383,50 +474,71 @@
     even = row_index % 2 == 0
     top, bottom = latent[:2], latent[band - 2 :]
     swap_a, swap_b = swap_rows(jnp.where(even, bottom, top), jnp.where(even, top, bottom))
-    payload, grad_part, beyond, fisher = call(
+    coefs, grad_part, fisher = call(
         gradient_kernel,
-        (wide, block, (band, lanes), block),
-        (place, latent, counts, exposure, swap_a, swap_b, tab["row_forward"]),
+        (extended, block, block),
+        (latent, counts, exposure, tab["row_forward"]),
         (pad,),
-        flops=10**8,
-    )
-    incoming = exchange(payload)
-    ends = parts - 1
-    from_left = lax.ppermute(beyond, "cols", [(i, i + 1) for i in range(ends)])
-    from_right = lax.ppermute(beyond, "cols", [(i + 1, i) for i in range(ends)])
-    back, _ = call(
+        flops=10**9,
+    )
+    *blocks, added = call(
+        gradient_halo_kernel,
+        (wide,) * parts + ((8, full),),
+        (place, coefs, swap_a, swap_b, tab["halo_forward"]),
+        (halo, wide_buffer),
+        flops=10**7,
+    )
+    blocks = exchange(blocks)
+    blocks = call(
         functools.partial(filter_kernel, edges=True),
-        (wide, (8, lanes)),
-        (place, incoming, *filters),
+        (wide,) * parts,
+        (place, *blocks, jnp.zeros((8, lanes), jnp.float32), *filters),
+        (wide_buffer, wide_buffer),
         flops=10**9,
     )
-    incoming = exchange(back)
+    blocks = exchange(blocks)
     grad, search, send_a, send_b = call(
         search_kernel,
-        (block, (band, width + lanes), (2, width + lanes), (2, width + lanes)),
-        (place, incoming, grad_part, from_left, from_right, tab["row_inverse"]),
+        (block, extended, (2, full), (2, full)),
+        (place, *blocks, grad_part, added, tab["row_inverse"]),
+        (wide_buffer,),
         flops=10**8,
     )
     swap_a, swap_b = swap_rows(send_a, send_b)
-    payload, image, sums = call(
+    coefs, partial = call(
         image_kernel,
-        (slim, block, (8, lanes)),
-        (place, search, swap_a, swap_b, fisher, grad, tab["row_forward"]),
+        (block, block),
+        (search, fisher, tab["row_forward"]),
         (pad,),
+        flops=10**9,
+    )
+    *blocks, added = call(
+        image_halo_kernel,
+        (slim,) * parts + ((8, full),),
+        (place, coefs, swap_a, swap_b, tab["halo_forward"]),
+        (halo, slim_buffer),
+        flops=10**7,
+    )
+    blocks = exchange(blocks)
+    image, sums = call(
+        sums_kernel, (block, (8, lanes)), (search, grad, partial, added), flops=10**8
+    )
+    blocks = call(
+        functools.partial(filter_kernel, edges=False),
+        (wide,) * parts,
+        (place, *blocks, sums, *filters),
+        (slim_buffer, wide_buffer),
+        flops=10**9,
+    )
+    blocks = exchange(blocks)
+    second, spread = call(
+        second_kernel,
+        (block, (lax.axis_size("rows"), 8, lanes)),
+        (place, *blocks, image, tab["row_inverse"]),
+        (wide_buffer,),
         flops=10**8,
     )
-    incoming = exchange(payload)
-    back, energy = call(
-        functools.partial(filter_kernel, edges=False),
-        (slim, (8, lanes)),
-        (place, incoming, *filters),
-        flops=10**9,
-    )
-    incoming = exchange(back)
-    image_row = lax.broadcasted_iota(jnp.int32, (8, lanes), 0) == 2
-    sums = sum_over_rows(sums + jnp.where(image_row, energy, 0.0))
-    sums = exchange(jnp.broadcast_to(sums[None], (parts, 8, lanes)))
-    (second,) = call(second_kernel, (block,), (incoming, image, tab["row_inverse"]), flops=10**8)
+    sums = lax.all_to_all(spread, "rows", split_axis=0, concat_axis=0, tiled=True)
     return call(
         final_kernel, (block, block, block), (sums, search, grad, image, second), flops=10**6
     )

time: 132 us -> 128 us (0.970); the launches traced: 132 us -> 125 us
  blocking collectives: 42.6 us -> 14.4 us
  starting transfers between devices: 42.6 us -> 68.3 us
  waiting for transfers between devices: 29.7 us -> 26.2 us
    ppermute x9 -> x28, starting transfers between devices: 15.9 us -> 60.1 us  [exchange(): lax.ppermute(blocks[mask], 'cols', [(i, i ^ mask) for i in range(count)])]
    all_to_all x2 -> x1, blocking collectives: 42.6 us -> 14.4 us  [on_device(): lax.all_to_all(spread, 'rows', split_axis=0, concat_axis=0, tiled=True)]
    all_to_all x3 -> x0, starting transfers between devices: 14 us -> none  [exchange(): lax.all_to_all(payload, 'cols', split_axis=0, concat_axis=0, tiled=True)]
    all_to_all x3 -> x0, waiting for transfers between devices: 11.3 us -> none  [exchange(): lax.all_to_all(payload, 'cols', split_axis=0, concat_axis=0, tiled=True)]
    ppermute x9 -> x28, waiting for transfers between devices: 14 us -> 24.1 us  [exchange(): lax.ppermute(blocks[mask], 'cols', [(i, i ^ mask) for i in range(count)])]
    ppermute x2, starting transfers between devices: 12.5 us -> 7.98 us  [swap_rows(): lax.ppermute(send_b, 'rows', outer)]
    ppermute x2, waiting for transfers between devices: 4.41 us -> 2.08 us  [swap_rows(): lax.ppermute(send_b, 'rows', outer)]
    pallas_call x7 -> x10, Pallas kernels: 10.9 us -> 11.1 us  [call(): pl.pallas_call(kernel, out_shape=outs, in_specs=in_specs, out_specs=tuple...]
  transfers between devices with their start and end apart: 16 -> 32, of which waited for: 9 -> 13; matrix products, arithmetic and copies ran while one was open for 0% -> 0% of each run, Pallas kernels for 0% -> 2%
where the time goes in v2:
time: 128 us; the launch traced here: 125 us
  starting transfers between devices  68.3 us (53%)
  waiting for transfers between devices  26.2 us (20%)
  blocking collectives  14.4 us (11%)
  Pallas kernels  11.1 us (9%)
  local copies, waits for them, and re-layouts  3.19 us (2%)
    ppermute x28, starting transfers between devices, exchange(): lax.ppermute(blocks[mask], 'cols', [(i, i ^ mask) for i in range(count)])  60.1 us
    ppermute x28, waiting for transfers between devices, exchange(): lax.ppermute(blocks[mask], 'cols', [(i, i ^ mask) for i in range(count)])  24.1 us
    all_to_all x1, blocking collectives, on_device(): lax.all_to_all(spread, 'rows', split_axis=0, concat_axis=0, tiled=True)  14.4 us
    pallas_call x10, Pallas kernels, call(): pl.pallas_call(kernel, out_shape=outs, in_specs=in_specs, out_specs=tuple...  11.1 us
    ppermute x2, starting transfers between devices, swap_rows(): lax.ppermute(send_b, 'rows', outer)  7.98 us
    unnamed x28, local copies, waits for them, and re-layouts  3.19 us
  transfers between devices with their start and end apart: 32, of which 13 were waited for; matrix products, arithmetic and copies ran while one was open for 0% of the time, Pallas kernels for 2%

profile of v2, /device:TPU:8, one launch (start us, length us, event | category | flops | bytes accessed | tf_op | source)
XLA Modules:
  0.0 125.1 jit_solution(17835312786901384436)
XLA Ops:
  0.6 0.0 copy-start.13
  0.7 0.9 broadcast_select_fusion
  1.5 4.0 %collective-permute-start.1 = (f32[2,2048]{1,0:T(2,128)S(1)}, f32[2,2048]{1,0:T(2,128)S(1)}, u32[]{:S(2)}, u32[]{:S(2)}) collective-permute-start(f32[2,2048]{1,0:T(2,128)S(1)} %get-tuple-element.97), channel_id=1, source_target_pairs={{8,16},{24,32},{40,48},{56,64},{72,80},{88,96},{104,112},{120,128}... | collective-permute-start | bytes 49160 | tf_op jit(solution)/shard_map/ppermute | solution.py:443
  5.5 0.1 collective-permute-start
  5.7 0.1 pad_add_fusion.place
  5.7 1.0 copy-done.2
  6.8 1.0 copy-done.3
  7.8 1.0 copy-done.4
  8.9 1.3 %shard_map.157 = (f32[64,2176]{1,0:T(8,128)S(1)}, f32[64,2048]{1,0:T(8,128)S(1)}, f32[64,2048]{1,0:T(8,128)S(1)}) custom-call(f32[64,2048]{1,0:T(8,128)S(1)} %copy-done.2, s32[64,2048]{1,0:T(8,128)S(1)} %copy-done.3, s32[64,2048]{1,0:T(8,128)S(1)} %copy-done.4, bf16[64,192]{1,0:T(8,128)(2,1)S(1)} %copy-done.13), custom_call_target="tpu_custom_call" | custom-call | flops 1000000000 | bytes 3227648 | tf_op jit(solution)/shard_map/pallas_call | solution.py:415
  10.2 0.0 copy-start.6
  10.2 0.0 copy-start.7
  10.2 0.0 copy-start.8
  10.2 0.0 copy-start.10
  10.2 1.0 shard_map.158
  11.2 2.0 %collective-permute-start.2 = (f32[136,128]{1,0:T(8,128)S(1)}, f32[136,128]{1,0:T(8,128)S(1)}, u32[]{:S(2)}, u32[]{:S(2)}) collective-permute-start(f32[136,128]{1,0:T(8,128)S(1)} %get-tuple-element.52), channel_id=1, source_target_pairs={{0,1},{1,0},{2,3},{3,2},{4,5},{5,4},{6,7},{7,6},{8,9},{9,8},{10,11... | collective-permute-start | bytes 208904 | tf_op jit(solution)/shard_map/ppermute | solution.py:437
  13.2 3.3 %collective-permute-start.3 = (f32[136,128]{1,0:T(8,128)S(1)}, f32[136,128]{1,0:T(8,128)S(1)}, u32[]{:S(2)}, u32[]{:S(2)}) collective-permute-start(f32[136,128]{1,0:T(8,128)S(1)} %get-tuple-element.53), channel_id=1, source_target_pairs={{0,2},{1,3},{2,0},{3,1},{4,6},{5,7},{6,4},{7,5},{8,10},{9,11},{10,... | collective-permute-start | bytes 208904 | tf_op jit(solution)/shard_map/ppermute | solution.py:437
  16.5 6.4 %collective-permute-start.5 = (f32[136,128]{1,0:T(8,128)S(1)}, f32[136,128]{1,0:T(8,128)S(1)}, u32[]{:S(2)}, u32[]{:S(2)}) collective-permute-start(f32[136,128]{1,0:T(8,128)S(1)} %get-tuple-element.55), channel_id=1, source_target_pairs={{0,4},{1,5},{2,6},{3,7},{4,0},{5,1},{6,2},{7,3},{8,12},{9,13},{10,... | collective-permute-start | bytes 208904 | tf_op jit(solution)/shard_map/ppermute | solution.py:437
  22.9 4.6 %collective-permute-start.7 = (f32[136,128]{1,0:T(8,128)S(1)}, f32[136,128]{1,0:T(8,128)S(1)}, u32[]{:S(2)}, u32[]{:S(2)}) collective-permute-start(f32[136,128]{1,0:T(8,128)S(1)} %get-tuple-element.57), channel_id=1, source_target_pairs={{0,6},{1,7},{2,4},{3,5},{4,2},{5,3},{6,0},{7,1},{8,14},{9,15},{10,... | collective-permute-start | bytes 208904 | tf_op jit(solution)/shard_map/ppermute | solution.py:437
  27.5 2.9 %collective-permute-start.8 = (f32[136,128]{1,0:T(8,128)S(1)}, f32[136,128]{1,0:T(8,128)S(1)}, u32[]{:S(2)}, u32[]{:S(2)}) collective-permute-start(f32[136,128]{1,0:T(8,128)S(1)} %get-tuple-element.58), channel_id=1, source_target_pairs={{0,7},{1,6},{2,5},{3,4},{4,3},{5,2},{6,1},{7,0},{8,15},{9,14},{10,... | collective-permute-start | bytes 208904 | tf_op jit(solution)/shard_map/ppermute | solution.py:437
  30.4 2.0 %collective-permute-done.6.rest_5_ = f32[136,128]{1,0:T(8,128)S(1)} collective-permute-done((f32[136,128]{1,0:T(8,128)S(1)}, f32[136,128]{1,0:T(8,128)S(1)}, u32[]{:S(2)}, u32[]{:S(2)}) %collective-permute-start.6) | collective-permute-done | bytes 69664 | tf_op jit(solution)/shard_map/ppermute | solution.py:437
  32.4 0.8 collective-permute-done.7.rest_6_
  33.3 2.6 %collective-permute-done.8.rest_7_ = f32[136,128]{1,0:T(8,128)S(1)} collective-permute-done((f32[136,128]{1,0:T(8,128)S(1)}, f32[136,128]{1,0:T(8,128)S(1)}, u32[]{:S(2)}, u32[]{:S(2)}) %collective-permute-start.8) | collective-permute-done | bytes 69664 | tf_op jit(solution)/shard_map/ppermute | solution.py:437
  35.9 1.8 %shard_map.159 = (f32[136,128]{1,0:T(8,128)S(1)}, f32[136,128]{1,0:T(8,128)S(1)}, f32[136,128]{1,0:T(8,128)S(1)}, f32[136,128]{1,0:T(8,128)S(1)}, f32[136,128]{1...) custom-call(s32[2]{0:T(128)S(1)} %pad_add_fusion.place, ...), custom_call_target="tpu_custom_call" | custom-call | flops 1000000000 | bytes 2396168 | tf_op jit(solution)/shard_map/pallas_call | solution.py:415
  37.7 0.7 collective-permute-start.9
  38.3 1.7 %collective-permute-start.10 = (f32[136,128]{1,0:T(8,128)S(1)}, f32[136,128]{1,0:T(8,128)S(1)}, u32[]{:S(2)}, u32[]{:S(2)}) collective-permute-start(f32[136,128]{1,0:T(8,128)S(1)} %get-tuple-element.61), channel_id=1, source_target_pairs={{0,2},{1,3},{2,0},{3,1},{4,6},{5,7},{6,4},{7,5},{8,10},{9,11},{10,... | collective-permute-start | bytes 208904 | tf_op jit(solution)/shard_map/ppermute | solution.py:437
  40.0 2.1 %collective-permute-start.11 = (f32[136,128]{1,0:T(8,128)S(1)}, f32[136,128]{1,0:T(8,128)S(1)}, u32[]{:S(2)}, u32[]{:S(2)}) collective-permute-start(f32[136,128]{1,0:T(8,128)S(1)} %get-tuple-element.62), channel_id=1, source_target_pairs={{0,3},{1,2},{2,1},{3,0},{4,7},{5,6},{6,5},{7,4},{8,11},{9,10},{10,... | collective-permute-start | bytes 208904 | tf_op jit(solution)/shard_map/ppermute | solution.py:437
  42.2 3.3 %collective-permute-start.12 = (f32[136,128]{1,0:T(8,128)S(1)}, f32[136,128]{1,0:T(8,128)S(1)}, u32[]{:S(2)}, u32[]{:S(2)}) collective-permute-start(f32[136,128]{1,0:T(8,128)S(1)} %get-tuple-element.63), channel_id=1, source_target_pairs={{0,4},{1,5},{2,6},{3,7},{4,0},{5,1},{6,2},{7,3},{8,12},{9,13},{10,... | collective-permute-start | bytes 208904 | tf_op jit(solution)/shard_map/ppermute | solution.py:437
  45.5 0.8 collective-permute-start.13
  46.3 3.8 %collective-permute-start.14 = (f32[136,128]{1,0:T(8,128)S(1)}, f32[136,128]{1,0:T(8,128)S(1)}, u32[]{:S(2)}, u32[]{:S(2)}) collective-permute-start(f32[136,128]{1,0:T(8,128)S(1)} %get-tuple-element.65), channel_id=1, source_target_pairs={{0,6},{1,7},{2,4},{3,5},{4,2},{5,3},{6,0},{7,1},{8,14},{9,15},{10,... | collective-permute-start | bytes 208904 | tf_op jit(solution)/shard_map/ppermute | solution.py:437
  50.1 1.3 %collective-permute-start.15 = (f32[136,128]{1,0:T(8,128)S(1)}, f32[136,128]{1,0:T(8,128)S(1)}, u32[]{:S(2)}, u32[]{:S(2)}) collective-permute-start(f32[136,128]{1,0:T(8,128)S(1)} %get-tuple-element.66), channel_id=1, source_target_pairs={{0,7},{1,6},{2,5},{3,4},{4,3},{5,2},{6,1},{7,0},{8,15},{9,14},{10,... | collective-permute-start | bytes 208904 | tf_op jit(solution)/shard_map/ppermute | solution.py:437
  51.3 2.5 %collective-permute-done.13.rest_5_ = f32[136,128]{1,0:T(8,128)S(1)} collective-permute-done((f32[136,128]{1,0:T(8,128)S(1)}, f32[136,128]{1,0:T(8,128)S(1)}, u32[]{:S(2)}, u32[]{:S(2)}) %collective-permute-start.13) | collective-permute-done | bytes 69664 | tf_op jit(solution)/shard_map/ppermute | solution.py:437
  53.8 1.6 %collective-permute-done.14.rest_6_ = f32[136,128]{1,0:T(8,128)S(1)} collective-permute-done((f32[136,128]{1,0:T(8,128)S(1)}, f32[136,128]{1,0:T(8,128)S(1)}, u32[]{:S(2)}, u32[]{:S(2)}) %collective-permute-start.14) | collective-permute-done | bytes 69664 | tf_op jit(solution)/shard_map/ppermute | solution.py:437
  55.4 3.0 %collective-permute-done.15.rest_7_ = f32[136,128]{1,0:T(8,128)S(1)} collective-permute-done((f32[136,128]{1,0:T(8,128)S(1)}, f32[136,128]{1,0:T(8,128)S(1)}, u32[]{:S(2)}, u32[]{:S(2)}) %collective-permute-start.15) | collective-permute-done | bytes 69664 | tf_op jit(solution)/shard_map/ppermute | solution.py:437
  58.4 0.9 shard_map.160
  59.3 0.1 collective-permute-start.16
  59.4 4.0 %collective-permute-start.17 = (f32[2,2176]{1,0:T(2,128)S(1)}, f32[2,2176]{1,0:T(2,128)S(1)}, u32[]{:S(2)}, u32[]{:S(2)}) collective-permute-start(f32[2,2176]{1,0:T(2,128)S(1)} %get-tuple-element.73), channel_id=1, source_target_pairs={{8,16},{24,32},{40,48},{56,64},{72,80},{88,96},{104,112},{120,128}... | collective-permute-start | bytes 52232 | tf_op jit(solution)/shard_map/ppermute | solution.py:443
  63.4 1.1 shard_map.161
  64.5 2.1 %collective-permute-done.17.swap_b = f32[2,2176]{1,0:T(2,128)S(1)} collective-permute-done((f32[2,2176]{1,0:T(2,128)S(1)}, f32[2,2176]{1,0:T(2,128)S(1)}, u32[]{:S(2)}, u32[]{:S(2)}) %collective-permute-start.17) | collective-permute-done | bytes 17440 | tf_op jit(solution)/shard_map/ppermute | solution.py:443
  66.6 0.9 shard_map.162
  67.5 0.8 collective-permute-start.18
  68.3 1.4 %collective-permute-start.19 = (f32[128,128]{1,0:T(8,128)S(1)}, f32[128,128]{1,0:T(8,128)S(1)}, u32[]{:S(2)}, u32[]{:S(2)}) collective-permute-start(f32[128,128]{1,0:T(8,128)S(1)} %get-tuple-element.76), channel_id=1, source_target_pairs={{0,2},{1,3},{2,0},{3,1},{4,6},{5,7},{6,4},{7,5},{8,10},{9,11},{10,... | collective-permute-start | bytes 196616 | tf_op jit(solution)/shard_map/ppermute | solution.py:437
  69.7 2.3 %collective-permute-start.20 = (f32[128,128]{1,0:T(8,128)S(1)}, f32[128,128]{1,0:T(8,128)S(1)}, u32[]{:S(2)}, u32[]{:S(2)}) collective-permute-start(f32[128,128]{1,0:T(8,128)S(1)} %get-tuple-element.77), channel_id=1, source_target_pairs={{0,3},{1,2},{2,1},{3,0},{4,7},{5,6},{6,5},{7,4},{8,11},{9,10},{10,... | collective-permute-start | bytes 196616 | tf_op jit(solution)/shard_map/ppermute | solution.py:437
  72.0 2.9 %collective-permute-start.21 = (f32[128,128]{1,0:T(8,128)S(1)}, f32[128,128]{1,0:T(8,128)S(1)}, u32[]{:S(2)}, u32[]{:S(2)}) collective-permute-start(f32[128,128]{1,0:T(8,128)S(1)} %get-tuple-element.78), channel_id=1, source_target_pairs={{0,4},{1,5},{2,6},{3,7},{4,0},{5,1},{6,2},{7,3},{8,12},{9,13},{10,... | collective-permute-start | bytes 196616 | tf_op jit(solution)/shard_map/ppermute | solution.py:437
  74.9 1.4 %collective-permute-start.22 = (f32[128,128]{1,0:T(8,128)S(1)}, f32[128,128]{1,0:T(8,128)S(1)}, u32[]{:S(2)}, u32[]{:S(2)}) collective-permute-start(f32[128,128]{1,0:T(8,128)S(1)} %get-tuple-element.79), channel_id=1, source_target_pairs={{0,5},{1,4},{2,7},{3,6},{4,1},{5,0},{6,3},{7,2},{8,13},{9,12},{10,... | collective-permute-start | bytes 196616 | tf_op jit(solution)/shard_map/ppermute | solution.py:437
  76.3 3.1 %collective-permute-start.23 = (f32[128,128]{1,0:T(8,128)S(1)}, f32[128,128]{1,0:T(8,128)S(1)}, u32[]{:S(2)}, u32[]{:S(2)}) collective-permute-start(f32[128,128]{1,0:T(8,128)S(1)} %get-tuple-element.80), channel_id=1, source_target_pairs={{0,6},{1,7},{2,4},{3,5},{4,2},{5,3},{6,0},{7,1},{8,14},{9,15},{10,... | collective-permute-start | bytes 196616 | tf_op jit(solution)/shard_map/ppermute | solution.py:437
  79.4 1.8 %collective-permute-start.24 = (f32[128,128]{1,0:T(8,128)S(1)}, f32[128,128]{1,0:T(8,128)S(1)}, u32[]{:S(2)}, u32[]{:S(2)}) collective-permute-start(f32[128,128]{1,0:T(8,128)S(1)} %get-tuple-element.81), channel_id=1, source_target_pairs={{0,7},{1,6},{2,5},{3,4},{4,3},{5,2},{6,1},{7,0},{8,15},{9,14},{10,... | collective-permute-start | bytes 196616 | tf_op jit(solution)/shard_map/ppermute | solution.py:437
  81.2 0.3 shard_map.163
  81.5 0.8 collective-permute-done.22.rest_5_
  82.3 1.3 %collective-permute-done.23.rest_6_ = f32[128,128]{1,0:T(8,128)S(1)} collective-permute-done((f32[128,128]{1,0:T(8,128)S(1)}, f32[128,128]{1,0:T(8,128)S(1)}, u32[]{:S(2)}, u32[]{:S(2)}) %collective-permute-start.23) | collective-permute-done | bytes 65568 | tf_op jit(solution)/shard_map/ppermute | solution.py:437
  83.7 2.8 %collective-permute-done.24.rest_7_ = f32[128,128]{1,0:T(8,128)S(1)} collective-permute-done((f32[128,128]{1,0:T(8,128)S(1)}, f32[128,128]{1,0:T(8,128)S(1)}, u32[]{:S(2)}, u32[]{:S(2)}) %collective-permute-start.24) | collective-permute-done | bytes 65568 | tf_op jit(solution)/shard_map/ppermute | solution.py:437
  86.5 1.7 %shard_map.164 = (f32[136,128]{1,0:T(8,128)S(1)}, f32[136,128]{1,0:T(8,128)S(1)}, f32[136,128]{1,0:T(8,128)S(1)}, f32[136,128]{1,0:T(8,128)S(1)}, f32[136,128]{1...) custom-call(s32[2]{0:T(128)S(1)} %pad_add_fusion.place, ...), custom_call_target="tpu_custom_call" | custom-call | flops 1000000000 | bytes 2363400 | tf_op jit(solution)/shard_map/pallas_call | solution.py:415
  88.2 0.9 collective-permute-start.25
  89.1 1.7 %collective-permute-start.26 = (f32[136,128]{1,0:T(8,128)S(1)}, f32[136,128]{1,0:T(8,128)S(1)}, u32[]{:S(2)}, u32[]{:S(2)}) collective-permute-start(f32[136,128]{1,0:T(8,128)S(1)} %get-tuple-element.88), channel_id=1, source_target_pairs={{0,2},{1,3},{2,0},{3,1},{4,6},{5,7},{6,4},{7,5},{8,10},{9,11},{10,... | collective-permute-start | bytes 208904 | tf_op jit(solution)/shard_map/ppermute | solution.py:437
  90.8 1.9 %collective-permute-start.27 = (f32[136,128]{1,0:T(8,128)S(1)}, f32[136,128]{1,0:T(8,128)S(1)}, u32[]{:S(2)}, u32[]{:S(2)}) collective-permute-start(f32[136,128]{1,0:T(8,128)S(1)} %get-tuple-element.89), channel_id=1, source_target_pairs={{0,3},{1,2},{2,1},{3,0},{4,7},{5,6},{6,5},{7,4},{8,11},{9,10},{10,... | collective-permute-start | bytes 208904 | tf_op jit(solution)/shard_map/ppermute | solution.py:437
  92.7 3.1 %collective-permute-start.28 = (f32[136,128]{1,0:T(8,128)S(1)}, f32[136,128]{1,0:T(8,128)S(1)}, u32[]{:S(2)}, u32[]{:S(2)}) collective-permute-start(f32[136,128]{1,0:T(8,128)S(1)} %get-tuple-element.90), channel_id=1, source_target_pairs={{0,4},{1,5},{2,6},{3,7},{4,0},{5,1},{6,2},{7,3},{8,12},{9,13},{10,... | collective-permute-start | bytes 208904 | tf_op jit(solution)/shard_map/ppermute | solution.py:437
  95.8 1.2 collective-permute-start.29
  97.0 3.3 %collective-permute-start.30 = (f32[136,128]{1,0:T(8,128)S(1)}, f32[136,128]{1,0:T(8,128)S(1)}, u32[]{:S(2)}, u32[]{:S(2)}) collective-permute-start(f32[136,128]{1,0:T(8,128)S(1)} %get-tuple-element.92), channel_id=1, source_target_pairs={{0,6},{1,7},{2,4},{3,5},{4,2},{5,3},{6,0},{7,1},{8,14},{9,15},{10,... | collective-permute-start | bytes 208904 | tf_op jit(solution)/shard_map/ppermute | solution.py:437
  100.3 1.5 %collective-permute-start.31 = (f32[136,128]{1,0:T(8,128)S(1)}, f32[136,128]{1,0:T(8,128)S(1)}, u32[]{:S(2)}, u32[]{:S(2)}) collective-permute-start(f32[136,128]{1,0:T(8,128)S(1)} %get-tuple-element.93), channel_id=1, source_target_pairs={{0,7},{1,6},{2,5},{3,4},{4,3},{5,2},{6,1},{7,0},{8,15},{9,14},{10,... | collective-permute-start | bytes 208904 | tf_op jit(solution)/shard_map/ppermute | solution.py:437
  101.9 2.3 %collective-permute-done.29.rest_5_ = f32[136,128]{1,0:T(8,128)S(1)} collective-permute-done((f32[136,128]{1,0:T(8,128)S(1)}, f32[136,128]{1,0:T(8,128)S(1)}, u32[]{:S(2)}, u32[]{:S(2)}) %collective-permute-start.29) | collective-permute-done | bytes 69664 | tf_op jit(solution)/shard_map/ppermute | solution.py:437
  104.2 1.6 %collective-permute-done.30.rest_6_ = f32[136,128]{1,0:T(8,128)S(1)} collective-permute-done((f32[136,128]{1,0:T(8,128)S(1)}, f32[136,128]{1,0:T(8,128)S(1)}, u32[]{:S(2)}, u32[]{:S(2)}) %collective-permute-start.30) | collective-permute-done | bytes 69664 | tf_op jit(solution)/shard_map/ppermute | solution.py:437
  105.8 2.8 %collective-permute-done.31.rest_7_ = f32[136,128]{1,0:T(8,128)S(1)} collective-permute-done((f32[136,128]{1,0:T(8,128)S(1)}, f32[136,128]{1,0:T(8,128)S(1)}, u32[]{:S(2)}, u32[]{:S(2)}) %collective-permute-start.31) | collective-permute-done | bytes 69664 | tf_op jit(solution)/shard_map/ppermute | solution.py:437
  108.6 0.8 shard_map.165
  109.4 14.4 %all_to_all.5.sums = f32[32,8,128]{2,1,0:T(8,128)S(1)} all-to-all(f32[32,8,128]{2,1,0:T(8,128)S(1)} %get-tuple-element.95), channel_id=1, replica_groups=mesh['rows'=32,'cols'=8] {'rows'}, dimensions={0} | all-to-all | bytes 262144 | tf_op jit(solution)/shard_map/all_to_all | solution.py:541
  123.8 1.3 %shard_map.166 = (f32[64,2048]{1,0:T(8,128)}, f32[64,2048]{1,0:T(8,128)}, f32[64,2048]{1,0:T(8,128)}) custom-call(f32[32,8,128]{2,1,0:T(8,128)S(1)} %all_to_all.5.sums, f32[64,2176]{1,0:T(8,128)S(1)} %get-tuple-element.69.search, f32[64,2048]{1,0:T(8,128)S(1)} %get-tuple-element.82.grad, f32[64,2048]{1,0:T(8,128)S(1)} %get-tuple-element.94.rest_8_.image, ...), custom_call_target="tpu_custom_call" | custom-call | flops 1000000 | bytes 3833856 | tf_op jit(solution)/shard_map/pallas_call | solution.py:415
  (42 shorter events, 0.1 us)
Async XLA Ops:
  0.6 5.1 %copy-start.13 = (bf16[64,192]{1,0:T(8,128)(2,1)S(1)}, bf16[64,192]{1,0:T(8,128)(2,1)}, u32[]{:S(2)}) copy-start(bf16[64,192]{1,0:T(8,128)(2,1)} %constant.47.clone.basis) | copy-start | bytes 73732
  1.5 8.6 %collective-permute-start.1 = (f32[2,2048]{1,0:T(2,128)S(1)}, f32[2,2048]{1,0:T(2,128)S(1)}, u32[]{:S(2)}, u32[]{:S(2)}) collective-permute-start(f32[2,2048]{1,0:T(2,128)S(1)} %get-tuple-element.97), channel_id=1, source_target_pairs={{8,16},{24,32},{40,48},{56,64},{72,80},{88,96},{104,112},{120,128}... | collective-permute-start | bytes 49160 | tf_op jit(solution)/shard_map/ppermute | solution.py:443
  5.5 4.6 %collective-permute-start = (f32[2,2048]{1,0:T(2,128)S(1)}, f32[2,2048]{1,0:T(2,128)S(1)}, u32[]{:S(2)}, u32[]{:S(2)}) collective-permute-start(f32[2,2048]{1,0:T(2,128)S(1)} %get-tuple-element.98), channel_id=1, source_target_pairs={{0,8},{8,0},{16,24},{24,16},{32,40},{40,32},{48,56},{56,48},{64,72... | collective-permute-start | bytes 49160 | tf_op jit(solution)/shard_map/ppermute | solution.py:443
  5.7 1.0 copy-start.2
  6.8 1.0 copy-start.3
  7.8 1.0 copy-start.4
  8.9 1.3 %copy-start.1 = (bf16[64,48]{1,0:T(8,128)(2,1)S(1)}, bf16[64,48]{1,0:T(8,128)(2,1)}, u32[]{:S(2)}) copy-start(bf16[64,48]{1,0:T(8,128)(2,1)} %constant.48.clone.basis) | copy-start | bytes 18436
  8.9 27.0 %copy-start.9 = (f32[2,72,128]{2,1,0:T(8,128)S(1)}, f32[2,72,128]{2,1,0:T(8,128)}, u32[]{:S(2)}) copy-start(f32[2,72,128]{2,1,0:T(8,128)} %constant.53.clone.rest_16_) | copy-start | bytes 221188
  8.9 27.0 %copy-start.11 = (f32[72,128]{1,0:T(8,128)S(1)}, f32[72,128]{1,0:T(8,128)}, u32[]{:S(2)}) copy-start(f32[72,128]{1,0:T(8,128)} %constant.56.clone.rest_11_) | copy-start | bytes 110596
  8.9 27.0 %copy-start.12 = (f32[64,128]{1,0:T(8,128)S(1)}, f32[64,128]{1,0:T(8,128)}, u32[]{:S(2)}) copy-start(f32[64,128]{1,0:T(8,128)} %constant.50.clone.rest_9_) | copy-start | bytes 98308
  10.2 25.7 %copy-start.5 = (bf16[384,256]{1,0:T(8,128)(2,1)S(1)}, bf16[384,256]{1,0:T(8,128)(2,1)}, u32[]{:S(2)}) copy-start(bf16[384,256]{1,0:T(8,128)(2,1)} %constant.55.clone.rest_15_) | copy-start | bytes 589828
  10.2 25.7 %copy-start.6 = (bf16[256,256]{1,0:T(8,128)(2,1)S(1)}, bf16[256,256]{1,0:T(8,128)(2,1)}, u32[]{:S(2)}) copy-start(bf16[256,256]{1,0:T(8,128)(2,1)} %constant.54.clone.rest_14_) | copy-start | bytes 393220
  10.2 25.7 %copy-start.7 = (bf16[128,432]{1,0:T(8,128)(2,1)S(1)}, bf16[128,432]{1,0:T(8,128)(2,1)}, u32[]{:S(2)}) copy-start(bf16[128,432]{1,0:T(8,128)(2,1)} %constant.52.clone.rest_13_) | copy-start | bytes 331780
  10.2 25.7 %copy-start.8 = (bf16[144,384]{1,0:T(8,128)(2,1)S(1)}, bf16[144,384]{1,0:T(8,128)(2,1)}, u32[]{:S(2)}) copy-start(bf16[144,384]{1,0:T(8,128)(2,1)} %constant.51.clone.rest_12_) | copy-start | bytes 331780
  10.2 25.7 %copy-start.10 = (f32[72,128]{1,0:T(8,128)S(1)}, f32[72,128]{1,0:T(8,128)}, u32[]{:S(2)}) copy-start(f32[72,128]{1,0:T(8,128)} %constant.57.clone.rest_10_) | copy-start | bytes 110596
  11.2 11.7 %collective-permute-start.2 = (f32[136,128]{1,0:T(8,128)S(1)}, f32[136,128]{1,0:T(8,128)S(1)}, u32[]{:S(2)}, u32[]{:S(2)}) collective-permute-start(f32[136,128]{1,0:T(8,128)S(1)} %get-tuple-element.52), channel_id=1, source_target_pairs={{0,1},{1,0},{2,3},{3,2},{4,5},{5,4},{6,7},{7,6},{8,9},{9,8},{10,11... | collective-permute-start | bytes 208904 | tf_op jit(solution)/shard_map/ppermute | solution.py:437
  13.2 14.3 %collective-permute-start.3 = (f32[136,128]{1,0:T(8,128)S(1)}, f32[136,128]{1,0:T(8,128)S(1)}, u32[]{:S(2)}, u32[]{:S(2)}) collective-permute-start(f32[136,128]{1,0:T(8,128)S(1)} %get-tuple-element.53), channel_id=1, source_target_pairs={{0,2},{1,3},{2,0},{3,1},{4,6},{5,7},{6,4},{7,5},{8,10},{9,11},{10,... | collective-permute-start | bytes 208904 | tf_op jit(solution)/shard_map/ppermute | solution.py:437
  16.5 13.9 %collective-permute-start.4 = (f32[136,128]{1,0:T(8,128)S(1)}, f32[136,128]{1,0:T(8,128)S(1)}, u32[]{:S(2)}, u32[]{:S(2)}) collective-permute-start(f32[136,128]{1,0:T(8,128)S(1)} %get-tuple-element.54), channel_id=1, source_target_pairs={{0,3},{1,2},{2,1},{3,0},{4,7},{5,6},{6,5},{7,4},{8,11},{9,10},{10,... | collective-permute-start | bytes 208904 | tf_op jit(solution)/shard_map/ppermute | solution.py:437
  16.5 13.9 %collective-permute-start.5 = (f32[136,128]{1,0:T(8,128)S(1)}, f32[136,128]{1,0:T(8,128)S(1)}, u32[]{:S(2)}, u32[]{:S(2)}) collective-permute-start(f32[136,128]{1,0:T(8,128)S(1)} %get-tuple-element.55), channel_id=1, source_target_pairs={{0,4},{1,5},{2,6},{3,7},{4,0},{5,1},{6,2},{7,3},{8,12},{9,13},{10,... | collective-permute-start | bytes 208904 | tf_op jit(solution)/shard_map/ppermute | solution.py:437
  22.9 9.6 %collective-permute-start.6 = (f32[136,128]{1,0:T(8,128)S(1)}, f32[136,128]{1,0:T(8,128)S(1)}, u32[]{:S(2)}, u32[]{:S(2)}) collective-permute-start(f32[136,128]{1,0:T(8,128)S(1)} %get-tuple-element.56), channel_id=1, source_target_pairs={{0,5},{1,4},{2,7},{3,6},{4,1},{5,0},{6,3},{7,2},{8,13},{9,12},{10,... | collective-permute-start | bytes 208904 | tf_op jit(solution)/shard_map/ppermute | solution.py:437
  22.9 10.4 %collective-permute-start.7 = (f32[136,128]{1,0:T(8,128)S(1)}, f32[136,128]{1,0:T(8,128)S(1)}, u32[]{:S(2)}, u32[]{:S(2)}) collective-permute-start(f32[136,128]{1,0:T(8,128)S(1)} %get-tuple-element.57), channel_id=1, source_target_pairs={{0,6},{1,7},{2,4},{3,5},{4,2},{5,3},{6,0},{7,1},{8,14},{9,15},{10,... | collective-permute-start | bytes 208904 | tf_op jit(solution)/shard_map/ppermute | solution.py:437
  27.5 8.4 %collective-permute-start.8 = (f32[136,128]{1,0:T(8,128)S(1)}, f32[136,128]{1,0:T(8,128)S(1)}, u32[]{:S(2)}, u32[]{:S(2)}) collective-permute-start(f32[136,128]{1,0:T(8,128)S(1)} %get-tuple-element.58), channel_id=1, source_target_pairs={{0,7},{1,6},{2,5},{3,4},{4,3},{5,2},{6,1},{7,0},{8,15},{9,14},{10,... | collective-permute-start | bytes 208904 | tf_op jit(solution)/shard_map/ppermute | solution.py:437
  35.9 22.5 %copy-start = (bf16[64,192]{1,0:T(8,128)(2,1)S(1)}, bf16[64,192]{1,0:T(8,128)(2,1)}, u32[]{:S(2)}) copy-start(bf16[64,192]{1,0:T(8,128)(2,1)} %constant.49.clone.rest_10_.rest_9_) | copy-start | bytes 73732
  37.7 8.6 %collective-permute-start.9 = (f32[136,128]{1,0:T(8,128)S(1)}, f32[136,128]{1,0:T(8,128)S(1)}, u32[]{:S(2)}, u32[]{:S(2)}) collective-permute-start(f32[136,128]{1,0:T(8,128)S(1)} %get-tuple-element.60), channel_id=1, source_target_pairs={{0,1},{1,0},{2,3},{3,2},{4,5},{5,4},{6,7},{7,6},{8,9},{9,8},{10,11... | collective-permute-start | bytes 208904 | tf_op jit(solution)/shard_map/ppermute | solution.py:437
  38.3 11.7 %collective-permute-start.10 = (f32[136,128]{1,0:T(8,128)S(1)}, f32[136,128]{1,0:T(8,128)S(1)}, u32[]{:S(2)}, u32[]{:S(2)}) collective-permute-start(f32[136,128]{1,0:T(8,128)S(1)} %get-tuple-element.61), channel_id=1, source_target_pairs={{0,2},{1,3},{2,0},{3,1},{4,6},{5,7},{6,4},{7,5},{8,10},{9,11},{10,... | collective-permute-start | bytes 208904 | tf_op jit(solution)/shard_map/ppermute | solution.py:437
  40.0 11.3 %collective-permute-start.11 = (f32[136,128]{1,0:T(8,128)S(1)}, f32[136,128]{1,0:T(8,128)S(1)}, u32[]{:S(2)}, u32[]{:S(2)}) collective-permute-start(f32[136,128]{1,0:T(8,128)S(1)} %get-tuple-element.62), channel_id=1, source_target_pairs={{0,3},{1,2},{2,1},{3,0},{4,7},{5,6},{6,5},{7,4},{8,11},{9,10},{10,... | collective-permute-start | bytes 208904 | tf_op jit(solution)/shard_map/ppermute | solution.py:437
  42.2 9.2 %collective-permute-start.12 = (f32[136,128]{1,0:T(8,128)S(1)}, f32[136,128]{1,0:T(8,128)S(1)}, u32[]{:S(2)}, u32[]{:S(2)}) collective-permute-start(f32[136,128]{1,0:T(8,128)S(1)} %get-tuple-element.63), channel_id=1, source_target_pairs={{0,4},{1,5},{2,6},{3,7},{4,0},{5,1},{6,2},{7,3},{8,12},{9,13},{10,... | collective-permute-start | bytes 208904 | tf_op jit(solution)/shard_map/ppermute | solution.py:437
  45.5 8.3 %collective-permute-start.13 = (f32[136,128]{1,0:T(8,128)S(1)}, f32[136,128]{1,0:T(8,128)S(1)}, u32[]{:S(2)}, u32[]{:S(2)}) collective-permute-start(f32[136,128]{1,0:T(8,128)S(1)} %get-tuple-element.64), channel_id=1, source_target_pairs={{0,5},{1,4},{2,7},{3,6},{4,1},{5,0},{6,3},{7,2},{8,13},{9,12},{10,... | collective-permute-start | bytes 208904 | tf_op jit(solution)/shard_map/ppermute | solution.py:437
  46.3 9.1 %collective-permute-start.14 = (f32[136,128]{1,0:T(8,128)S(1)}, f32[136,128]{1,0:T(8,128)S(1)}, u32[]{:S(2)}, u32[]{:S(2)}) collective-permute-start(f32[136,128]{1,0:T(8,128)S(1)} %get-tuple-element.65), channel_id=1, source_target_pairs={{0,6},{1,7},{2,4},{3,5},{4,2},{5,3},{6,0},{7,1},{8,14},{9,15},{10,... | collective-permute-start | bytes 208904 | tf_op jit(solution)/shard_map/ppermute | solution.py:437
  50.1 8.3 %collective-permute-start.15 = (f32[136,128]{1,0:T(8,128)S(1)}, f32[136,128]{1,0:T(8,128)S(1)}, u32[]{:S(2)}, u32[]{:S(2)}) collective-permute-start(f32[136,128]{1,0:T(8,128)S(1)} %get-tuple-element.66), channel_id=1, source_target_pairs={{0,7},{1,6},{2,5},{3,4},{4,3},{5,2},{6,1},{7,0},{8,15},{9,14},{10,... | collective-permute-start | bytes 208904 | tf_op jit(solution)/shard_map/ppermute | solution.py:437
  59.3 5.2 %collective-permute-start.16 = (f32[2,2176]{1,0:T(2,128)S(1)}, f32[2,2176]{1,0:T(2,128)S(1)}, u32[]{:S(2)}, u32[]{:S(2)}) collective-permute-start(f32[2,2176]{1,0:T(2,128)S(1)} %get-tuple-element.72), channel_id=1, source_target_pairs={{0,8},{8,0},{16,24},{24,16},{32,40},{40,32},{48,56},{56,48},{64,72... | collective-permute-start | bytes 52232 | tf_op jit(solution)/shard_map/ppermute | solution.py:443
  59.4 7.2 %collective-permute-start.17 = (f32[2,2176]{1,0:T(2,128)S(1)}, f32[2,2176]{1,0:T(2,128)S(1)}, u32[]{:S(2)}, u32[]{:S(2)}) collective-permute-start(f32[2,2176]{1,0:T(2,128)S(1)} %get-tuple-element.73), channel_id=1, source_target_pairs={{8,16},{24,32},{40,48},{56,64},{72,80},{88,96},{104,112},{120,128}... | collective-permute-start | bytes 52232 | tf_op jit(solution)/shard_map/ppermute | solution.py:443
  67.5 8.8 %collective-permute-start.18 = (f32[128,128]{1,0:T(8,128)S(1)}, f32[128,128]{1,0:T(8,128)S(1)}, u32[]{:S(2)}, u32[]{:S(2)}) collective-permute-start(f32[128,128]{1,0:T(8,128)S(1)} %get-tuple-element.75), channel_id=1, source_target_pairs={{0,1},{1,0},{2,3},{3,2},{4,5},{5,4},{6,7},{7,6},{8,9},{9,8},{10,11... | collective-permute-start | bytes 196616 | tf_op jit(solution)/shard_map/ppermute | solution.py:437
  68.3 11.1 %collective-permute-start.19 = (f32[128,128]{1,0:T(8,128)S(1)}, f32[128,128]{1,0:T(8,128)S(1)}, u32[]{:S(2)}, u32[]{:S(2)}) collective-permute-start(f32[128,128]{1,0:T(8,128)S(1)} %get-tuple-element.76), channel_id=1, source_target_pairs={{0,2},{1,3},{2,0},{3,1},{4,6},{5,7},{6,4},{7,5},{8,10},{9,11},{10,... | collective-permute-start | bytes 196616 | tf_op jit(solution)/shard_map/ppermute | solution.py:437
  69.7 11.8 %collective-permute-start.20 = (f32[128,128]{1,0:T(8,128)S(1)}, f32[128,128]{1,0:T(8,128)S(1)}, u32[]{:S(2)}, u32[]{:S(2)}) collective-permute-start(f32[128,128]{1,0:T(8,128)S(1)} %get-tuple-element.77), channel_id=1, source_target_pairs={{0,3},{1,2},{2,1},{3,0},{4,7},{5,6},{6,5},{7,4},{8,11},{9,10},{10,... | collective-permute-start | bytes 196616 | tf_op jit(solution)/shard_map/ppermute | solution.py:437
  72.0 9.5 %collective-permute-start.21 = (f32[128,128]{1,0:T(8,128)S(1)}, f32[128,128]{1,0:T(8,128)S(1)}, u32[]{:S(2)}, u32[]{:S(2)}) collective-permute-start(f32[128,128]{1,0:T(8,128)S(1)} %get-tuple-element.78), channel_id=1, source_target_pairs={{0,4},{1,5},{2,6},{3,7},{4,0},{5,1},{6,2},{7,3},{8,12},{9,13},{10,... | collective-permute-start | bytes 196616 | tf_op jit(solution)/shard_map/ppermute | solution.py:437
  74.9 7.4 %collective-permute-start.22 = (f32[128,128]{1,0:T(8,128)S(1)}, f32[128,128]{1,0:T(8,128)S(1)}, u32[]{:S(2)}, u32[]{:S(2)}) collective-permute-start(f32[128,128]{1,0:T(8,128)S(1)} %get-tuple-element.79), channel_id=1, source_target_pairs={{0,5},{1,4},{2,7},{3,6},{4,1},{5,0},{6,3},{7,2},{8,13},{9,12},{10,... | collective-permute-start | bytes 196616 | tf_op jit(solution)/shard_map/ppermute | solution.py:437
  76.3 7.4 %collective-permute-start.23 = (f32[128,128]{1,0:T(8,128)S(1)}, f32[128,128]{1,0:T(8,128)S(1)}, u32[]{:S(2)}, u32[]{:S(2)}) collective-permute-start(f32[128,128]{1,0:T(8,128)S(1)} %get-tuple-element.80), channel_id=1, source_target_pairs={{0,6},{1,7},{2,4},{3,5},{4,2},{5,3},{6,0},{7,1},{8,14},{9,15},{10,... | collective-permute-start | bytes 196616 | tf_op jit(solution)/shard_map/ppermute | solution.py:437
  79.4 7.1 %collective-permute-start.24 = (f32[128,128]{1,0:T(8,128)S(1)}, f32[128,128]{1,0:T(8,128)S(1)}, u32[]{:S(2)}, u32[]{:S(2)}) collective-permute-start(f32[128,128]{1,0:T(8,128)S(1)} %get-tuple-element.81), channel_id=1, source_target_pairs={{0,7},{1,6},{2,5},{3,4},{4,3},{5,2},{6,1},{7,0},{8,15},{9,14},{10,... | collective-permute-start | bytes 196616 | tf_op jit(solution)/shard_map/ppermute | solution.py:437
  88.2 8.8 %collective-permute-start.25 = (f32[136,128]{1,0:T(8,128)S(1)}, f32[136,128]{1,0:T(8,128)S(1)}, u32[]{:S(2)}, u32[]{:S(2)}) collective-permute-start(f32[136,128]{1,0:T(8,128)S(1)} %get-tuple-element.87), channel_id=1, source_target_pairs={{0,1},{1,0},{2,3},{3,2},{4,5},{5,4},{6,7},{7,6},{8,9},{9,8},{10,11... | collective-permute-start | bytes 208904 | tf_op jit(solution)/shard_map/ppermute | solution.py:437
  89.1 11.3 %collective-permute-start.26 = (f32[136,128]{1,0:T(8,128)S(1)}, f32[136,128]{1,0:T(8,128)S(1)}, u32[]{:S(2)}, u32[]{:S(2)}) collective-permute-start(f32[136,128]{1,0:T(8,128)S(1)} %get-tuple-element.88), channel_id=1, source_target_pairs={{0,2},{1,3},{2,0},{3,1},{4,6},{5,7},{6,4},{7,5},{8,10},{9,11},{10,... | collective-permute-start | bytes 208904 | tf_op jit(solution)/shard_map/ppermute | solution.py:437
  90.8 11.1 %collective-permute-start.27 = (f32[136,128]{1,0:T(8,128)S(1)}, f32[136,128]{1,0:T(8,128)S(1)}, u32[]{:S(2)}, u32[]{:S(2)}) collective-permute-start(f32[136,128]{1,0:T(8,128)S(1)} %get-tuple-element.89), channel_id=1, source_target_pairs={{0,3},{1,2},{2,1},{3,0},{4,7},{5,6},{6,5},{7,4},{8,11},{9,10},{10,... | collective-permute-start | bytes 208904 | tf_op jit(solution)/shard_map/ppermute | solution.py:437
  92.7 9.2 %collective-permute-start.28 = (f32[136,128]{1,0:T(8,128)S(1)}, f32[136,128]{1,0:T(8,128)S(1)}, u32[]{:S(2)}, u32[]{:S(2)}) collective-permute-start(f32[136,128]{1,0:T(8,128)S(1)} %get-tuple-element.90), channel_id=1, source_target_pairs={{0,4},{1,5},{2,6},{3,7},{4,0},{5,1},{6,2},{7,3},{8,12},{9,13},{10,... | collective-permute-start | bytes 208904 | tf_op jit(solution)/shard_map/ppermute | solution.py:437
  95.8 8.4 %collective-permute-start.29 = (f32[136,128]{1,0:T(8,128)S(1)}, f32[136,128]{1,0:T(8,128)S(1)}, u32[]{:S(2)}, u32[]{:S(2)}) collective-permute-start(f32[136,128]{1,0:T(8,128)S(1)} %get-tuple-element.91), channel_id=1, source_target_pairs={{0,5},{1,4},{2,7},{3,6},{4,1},{5,0},{6,3},{7,2},{8,13},{9,12},{10,... | collective-permute-start | bytes 208904 | tf_op jit(solution)/shard_map/ppermute | solution.py:437
  97.0 8.8 %collective-permute-start.30 = (f32[136,128]{1,0:T(8,128)S(1)}, f32[136,128]{1,0:T(8,128)S(1)}, u32[]{:S(2)}, u32[]{:S(2)}) collective-permute-start(f32[136,128]{1,0:T(8,128)S(1)} %get-tuple-element.92), channel_id=1, source_target_pairs={{0,6},{1,7},{2,4},{3,5},{4,2},{5,3},{6,0},{7,1},{8,14},{9,15},{10,... | collective-permute-start | bytes 208904 | tf_op jit(solution)/shard_map/ppermute | solution.py:437
  100.3 8.2 %collective-permute-start.31 = (f32[136,128]{1,0:T(8,128)S(1)}, f32[136,128]{1,0:T(8,128)S(1)}, u32[]{:S(2)}, u32[]{:S(2)}) collective-permute-start(f32[136,128]{1,0:T(8,128)S(1)} %get-tuple-element.93), channel_id=1, source_target_pairs={{0,7},{1,6},{2,5},{3,4},{4,3},{5,2},{6,1},{7,0},{8,15},{9,14},{10,... | collective-permute-start | bytes 208904 | tf_op jit(solution)/shard_map/ppermute | solution.py:437

commit v3 on v2

--- a/solution.py
+++ b/solution.py
@@ -26,6 +26,8 @@
 half = 72
 kept = 64
 vmem_bytes = 48 * 1024 * 1024
+pieces = 4
+pairwise = (True, True, True, False)
 
 
 def high_low(table):
@@ -174,22 +176,28 @@
 
 
 def store_coefs(place, coefs, buffer, outs, count):
+    target = outs[0] if len(outs) == 1 else buffer
     for part in range(parts):
         for tile in range(count):
-            buffer[part, tile * lines : (tile + 1) * lines, :] = coefs[
+            target[part, tile * lines : (tile + 1) * lines, :] = coefs[
                 part * lines : (part + 1) * lines, tile * lanes : (tile + 1) * lanes
             ]
     store_blocks(place, buffer, outs)
 
 
 def store_blocks(place, buffer, outs):
+    if len(outs) == 1:
+        return
     for mask, out in enumerate(outs):
         out[...] = buffer[place[1] ^ mask]
 
 
 def load_blocks(place, refs, buffer):
+    if len(refs) == 1:
+        return refs[0]
     for mask, ref in enumerate(refs):
         buffer[place[1] ^ mask] = ref[...]
+    return buffer
 
 
 def load_coefs(buffer, count):
@@ -204,23 +212,41 @@
     )
 
 
-def gradient_kernel(latent, counts, exposure, basis, coefs, grad, fisher, pad):
+def gradient_kernel(
+    latent, counts, exposure, basis, coefs, grad, fisher, pad, counts_here, exposure_here, sems
+):
+    fields = ((latent, pad), (exposure, exposure_here), (counts, counts_here))
+    copies = []
+    for which, (there, here) in enumerate(fields):
+        skip = 8 if which == 0 else 0
+        for part in range(pieces):
+            rows = pl.ds(part * (band // pieces), band // pieces)
+            onto = pl.ds(part * (band // pieces) + skip, band // pieces)
+            copies.append(
+                pltpu.make_async_copy(
+                    there.at[rows, :], here.at[onto, :width], sems.at[which, part]
+                )
+            )
+            copies[-1].start()
     pad[0:8, :] = jnp.zeros((8, width + lanes), jnp.float32)
     pad[72:80, :] = jnp.zeros((8, width + lanes), jnp.float32)
-    pad[8:72, :width] = latent[...]
     pad[8:72, width:] = jnp.zeros((band, lanes), jnp.float32)
+    for copy in copies[:pieces]:
+        copy.wait()
     prior = stencil(pad)
-    mean_rate = exposure[...].astype(jnp.float32) * jnp.exp(latent[...])
+    for copy in copies[pieces:]:
+        copy.wait()
+    mean_rate = exposure_here[...].astype(jnp.float32) * jnp.exp(pad[8:72, :width])
     ratio = dispersion / (dispersion + mean_rate)
     fisher[...] = mean_rate * ratio
-    score = (counts[...].astype(jnp.float32) - mean_rate) * ratio
+    score = (counts_here[...].astype(jnp.float32) - mean_rate) * ratio
     inside = score - prior[:, :width]
     grad[...] = inside
     coefs[...] = left_product(basis[...], jnp.concatenate([inside, -prior[:, width:]], 1))
 
 
 def gradient_halo_kernel(place, coefs, swap_a, swap_b, basis, *rest):
-    outs, (added, halo, buffer) = rest[:parts], rest[parts:]
+    *outs, added, halo, buffer = rest
     rows, beside = halo_terms(place, swap_a, swap_b, halo)
     added[...] = -halo_rows(rows, beside)
     whole = coefs[...] - left_product(basis[...], jnp.concatenate([rows, beside], 0))
@@ -229,8 +255,8 @@
     store_coefs(place, jnp.concatenate([whole[:, :width], spill], 1), buffer, outs, tiles + 1)
 
 
-def filter_kernel(place, *rest, edges):
-    blocks_in, rest = rest[:parts], rest[parts:]
+def filter_kernel(place, *rest, edges, taken, given):
+    blocks_in, rest = rest[:taken], rest[taken:]
     (
         sums,
         row_term,
@@ -242,12 +268,16 @@
         inner_inverse,
         twist,
     ) = rest[:9]
-    blocks_out, (incoming, out) = rest[9 : 9 + parts], rest[9 + parts :]
-    load_blocks(place, blocks_in, incoming)
+    blocks_out, (known, incoming, out) = rest[9 : 9 + given], rest[9 + given :]
+    incoming = load_blocks(place, blocks_in, incoming)
+    if given == 1:
+        out = blocks_out[0]
     lane = lane_index((tiles, lanes))
     sub = lax.broadcasted_iota(jnp.int32, (tiles, lanes), 0)
     first = (sub == 0) & (lane < 2)
     last = (sub == tiles - 1) & (lane >= lanes - 2)
+    if edges:
+        known[...] = sums[...]
     line_fields = []
     for line in range(lines):
         blocks = [
@@ -290,10 +320,7 @@
             total = total + piece * scaled[-1]
     if not edges:
         energy = jnp.sum(total, axis=(0, 1), keepdims=True)
-        third = lax.broadcasted_iota(jnp.int32, (8, lanes), 0) == 2
-        known = sums[...] + jnp.where(third, energy, 0.0)
-        for part in range(parts):
-            out[part, tiles * lines :, :] = known
+        known[...] = sums[...] + jnp.where(lane_index((1, lanes)) == 2, energy, 0.0)
     high, low = split(jnp.concatenate(scaled, 0))
     back = dot(jnp.concatenate([high, low], 1), inner_inverse[: 4 * kept, :]) + dot(
         high, inner_inverse[4 * kept :, :]
@@ -334,12 +361,9 @@
 
 
 def search_kernel(place, *rest):
-    blocks, (grad, added, basis, full_grad, search, send_a, send_b, buffer) = (
-        rest[:parts],
-        rest[parts:],
-    )
+    *blocks, grad, added, basis, full_grad, search, send_a, send_b, buffer = rest
     even = place[0] % 2 == 0
-    load_blocks(place, blocks, buffer)
+    buffer = load_blocks(place, blocks, buffer)
     update = left_product(basis[...], load_coefs(buffer, tiles + 1))
     beyond = update[:, width:]
     spill = pltpu.roll(beyond, lanes // 2, 1)
@@ -366,7 +390,7 @@
 
 
 def image_halo_kernel(place, coefs, swap_a, swap_b, basis, *rest):
-    outs, (added, halo, buffer) = rest[:parts], rest[parts:]
+    *outs, added, halo, buffer = rest
     rows, beside = halo_terms(place, swap_a, swap_b, halo)
     added[...] = halo_rows(rows, beside)
     both = jnp.concatenate([rows, beside], 0)[:, :width]
@@ -378,45 +402,69 @@
     result = add_halo_rows(partial[...], added[:, :width])
     image[...] = result
     products = (grad[...] * field, field * result, result * result)
-    for row, product in enumerate(products):
+    lane = lane_index((1, lanes))
+    line = jnp.zeros((1, lanes), jnp.float32)
+    for which, product in enumerate(products):
         total = jnp.sum(product, axis=(0, 1), keepdims=True)
-        sums[row : row + 1, :] = jnp.broadcast_to(total, (1, lanes))
-    sums[3:8, :] = jnp.zeros((5, lanes), jnp.float32)
+        line = line + jnp.where(lane == which, total, 0.0)
+    sums[...] = line
+
+
+def spread_kernel(one, two, three, four, spread):
+    total = (one[...] + two[...]) + (three[...] + four[...])
+    for part in range(parts):
+        spread[part] = total
 
 
 def second_kernel(place, *rest):
-    blocks, (image, basis, second, spread, buffer) = rest[:parts], rest[parts:]
-    load_blocks(place, blocks, buffer)
-    total = buffer[0, tiles * lines :, :]
-    for part in range(1, parts):
-        total = total + buffer[part, tiles * lines :, :]
-    for row in range(spread.shape[0]):
-        spread[row] = total
+    *blocks, image, basis, second, buffer = rest
+    buffer = load_blocks(place, blocks, buffer)
     second[...] = image[...] + left_product(basis[...], load_coefs(buffer, tiles))
 
 
-def final_kernel(sums, search, grad, image, second, step, residual, direction):
+def final_kernel(
+    sums, search, grad, image, second, step, residual, direction, step_here, residual_here, direction_here, sems
+):
     total = jnp.sum(sums[...], axis=0)
     first_product = total[0:1, 0:1]
-    curvature = total[1:2, 0:1]
-    image_product = total[2:3, 0:1]
+    curvature = total[0:1, 1:2]
+    image_product = total[0:1, 2:3]
     step_size = first_product / curvature
     ratio = step_size * (image_product / curvature) - 1.0
-    field = search[:, :width]
-    step[...] = step_size * field
-    residual[...] = grad[...] - step_size * image[...]
-    direction[...] = (field - step_size * second[...]) + ratio * field
-
-
-def call(kernel, shapes, args, scratch=(), flops=0):
-    in_specs = [pl.BlockSpec(memory_space=pltpu.SMEM if a.dtype == jnp.int32 and a.ndim == 1 else pltpu.VMEM) for a in args]
+    copies = []
+    for part in range(pieces):
+        rows = slice(part * (band // pieces), (part + 1) * (band // pieces))
+        field = search[rows, :width]
+        results = (
+            (step_size * field, step_here, step),
+            (grad[rows, :] - step_size * image[rows, :], residual_here, residual),
+            ((field - step_size * second[rows, :]) + ratio * field, direction_here, direction),
+        )
+        for which, (value, here, there) in enumerate(results):
+            here[rows, :] = value
+            copies.append(
+                pltpu.make_async_copy(here.at[rows, :], there.at[rows, :], sems.at[which, part])
+            )
+            copies[-1].start()
+    for copy in copies:
+        copy.wait()
+
+
+def call(kernel, shapes, args, scratch=(), flops=0, far=0, far_out=False):
+    in_specs = [
+        pl.BlockSpec(memory_space=pltpu.HBM if i < far else pltpu.VMEM) for i in range(len(args))
+    ]
+    if args[0].ndim == 1:
+        in_specs[0] = pl.BlockSpec(memory_space=pltpu.SMEM)
     outs = tuple(jax.ShapeDtypeStruct(s, jnp.float32) for s in shapes)
     moved = 4 * (sum(a.size for a in args) + sum(o.size for o in outs))
     return pl.pallas_call(
         kernel,
         out_shape=outs,
         in_specs=in_specs,
-        out_specs=tuple(pl.BlockSpec(memory_space=pltpu.VMEM) for _ in outs),
+        out_specs=tuple(
+            pl.BlockSpec(memory_space=pltpu.HBM if far_out else pltpu.VMEM) for _ in outs
+        ),
         scratch_shapes=list(scratch),
         compiler_params=pltpu.CompilerParams(vmem_limit_bytes=vmem_bytes),
         cost_estimate=pl.CostEstimate(flops=flops, bytes_accessed=moved, transcendentals=0),
@@ -431,6 +479,8 @@
 
 
 def exchange(blocks):
+    if len(blocks) == 1:
+        return [lax.all_to_all(blocks[0], "cols", split_axis=0, concat_axis=0, tiled=True)]
     count = lax.axis_size("cols")
     got = {}
     for mask in (4, 3, 5, 2, 6, 1, 7):
@@ -441,6 +491,17 @@
 def swap_rows(send_a, send_b):
     inner, outer = row_swaps()
     return lax.ppermute(send_a, "rows", inner), lax.ppermute(send_b, "rows", outer)
+
+
+def sum_over_rows(value):
+    count = lax.axis_size("rows")
+
+    def swap(mask):
+        return lax.ppermute(value, "rows", [(i, i ^ mask) for i in range(count)])
+
+    value = value + swap(1)
+    value = value + swap(2) + swap(4) + swap(6)
+    return value, swap(8), swap(16), swap(24)
 
 
 def on_device(latent, counts, exposure):
@@ -455,6 +516,9 @@
     slim = (tiles * lines, lanes)
     wide_buffer = pltpu.VMEM((parts, *wide), jnp.float32)
     slim_buffer = pltpu.VMEM((parts, *slim), jnp.float32)
+    def sent(shape, pairwise):
+        return (shape,) * parts if pairwise else ((parts, *shape),)
+
     block = (band, width)
     extended = (band, full)
     filters = [
@@ -477,22 +541,33 @@
     coefs, grad_part, fisher = call(
         gradient_kernel,
         (extended, block, block),
-        (latent, counts, exposure, tab["row_forward"]),
-        (pad,),
+        (
+            *(pltpu.with_memory_space_constraint(a, pltpu.HBM) for a in (latent, counts, exposure)),
+            tab["row_forward"],
+        ),
+        (
+            pad,
+            pltpu.VMEM(block, jnp.int32),
+            pltpu.VMEM(block, jnp.int32),
+            pltpu.SemaphoreType.DMA((3, pieces)),
+        ),
         flops=10**9,
+        far=3,
     )
     *blocks, added = call(
         gradient_halo_kernel,
-        (wide,) * parts + ((8, full),),
+        sent(wide, pairwise[0]) + ((8, full),),
         (place, coefs, swap_a, swap_b, tab["halo_forward"]),
         (halo, wide_buffer),
         flops=10**7,
     )
     blocks = exchange(blocks)
-    blocks = call(
-        functools.partial(filter_kernel, edges=True),
-        (wide,) * parts,
-        (place, *blocks, jnp.zeros((8, lanes), jnp.float32), *filters),
+    *blocks, _ = call(
+        functools.partial(
+            filter_kernel, edges=True, taken=len(blocks), given=parts if pairwise[1] else 1
+        ),
+        (*sent(wide, pairwise[1]), (1, lanes)),
+        (place, *blocks, jnp.zeros((1, lanes), jnp.float32), *filters),
         (wide_buffer, wide_buffer),
         flops=10**9,
     )
@@ -514,33 +589,41 @@
     )
     *blocks, added = call(
         image_halo_kernel,
-        (slim,) * parts + ((8, full),),
+        sent(slim, pairwise[2]) + ((8, full),),
         (place, coefs, swap_a, swap_b, tab["halo_forward"]),
         (halo, slim_buffer),
         flops=10**7,
     )
     blocks = exchange(blocks)
     image, sums = call(
-        sums_kernel, (block, (8, lanes)), (search, grad, partial, added), flops=10**8
-    )
-    blocks = call(
-        functools.partial(filter_kernel, edges=False),
-        (wide,) * parts,
+        sums_kernel, (block, (1, lanes)), (search, grad, partial, added), flops=10**8
+    )
+    *blocks, known = call(
+        functools.partial(
+            filter_kernel, edges=False, taken=len(blocks), given=parts if pairwise[3] else 1
+        ),
+        (*sent(slim, pairwise[3]), (1, lanes)),
         (place, *blocks, sums, *filters),
-        (slim_buffer, wide_buffer),
+        (slim_buffer, slim_buffer),
         flops=10**9,
     )
     blocks = exchange(blocks)
-    second, spread = call(
+    (spread,) = call(spread_kernel, ((parts, 1, lanes),), sum_over_rows(known))
+    sums = exchange([spread])[0]
+    (second,) = call(
         second_kernel,
-        (block, (lax.axis_size("rows"), 8, lanes)),
+        (block,),
         (place, *blocks, image, tab["row_inverse"]),
-        (wide_buffer,),
+        (slim_buffer,),
         flops=10**8,
     )
-    sums = lax.all_to_all(spread, "rows", split_axis=0, concat_axis=0, tiled=True)
     return call(
-        final_kernel, (block, block, block), (sums, search, grad, image, second), flops=10**6
+        final_kernel,
+        (block, block, block),
+        (sums, search, grad, image, second),
+        (pltpu.VMEM(block, jnp.float32),) * 3 + (pltpu.SemaphoreType.DMA((3, pieces)),),
+        flops=10**6,
+        far_out=True,
     )
 
 

time: 128 us -> 126 us (0.984); the launches traced: 125 us -> 125 us
  blocking collectives: 14.4 us -> 0 us
  waiting for transfers between devices: 26.2 us -> 34.7 us
  starting transfers between devices: 68.3 us -> 74.3 us
  local copies, waits for them, and re-layouts: 3.19 us -> 0.06 us
  Pallas kernels: 11.1 us -> 14.2 us
    all_to_all x1 -> x0, blocking collectives: 14.4 us -> none  [on_device(): lax.all_to_all(spread, 'rows', split_axis=0, concat_axis=0, tiled=True)]
    ppermute x28 -> x21, starting transfers between devices: 60.1 us -> 46.2 us  [exchange(): lax.ppermute(blocks[mask], 'cols', [(i, i ^ mask) for i in range(count)])]
    all_to_all x0 -> x2, starting transfers between devices: none -> 11.1 us  [exchange(): lax.all_to_all(blocks[0], 'cols', split_axis=0, concat_axis=0, tiled=True)]
    ppermute x0 -> x7, starting transfers between devices: none -> 8.39 us  [swap(): return lax.ppermute(value, 'rows', [(i, i ^ mask) for i in range(count)])]
    ppermute x0 -> x7, waiting for transfers between devices: none -> 8.06 us  [swap(): return lax.ppermute(value, 'rows', [(i, i ^ mask) for i in range(count)])]
    all_to_all x0 -> x2, waiting for transfers between devices: none -> 6.8 us  [exchange(): lax.all_to_all(blocks[0], 'cols', split_axis=0, concat_axis=0, tiled=True)]
    ppermute x28 -> x21, waiting for transfers between devices: 24.1 us -> 17.7 us  [exchange(): lax.ppermute(blocks[mask], 'cols', [(i, i ^ mask) for i in range(count)])]
    unnamed x28 -> x22, local copies, waits for them, and re-layouts: 3.19 us -> 0.06 us
  transfers between devices with their start and end apart: 32 -> 34, of which waited for: 13 -> 17; matrix products, arithmetic and copies ran while one was open for 0% -> 0% of each run, Pallas kernels for 2% -> 4%
where the time goes in v3:
time: 126 us; the launch traced here: 125 us
  starting transfers between devices  74.3 us (59%)
  waiting for transfers between devices  34.7 us (28%)
  Pallas kernels  14.2 us (11%)
    ppermute x21, starting transfers between devices, exchange(): lax.ppermute(blocks[mask], 'cols', [(i, i ^ mask) for i in range(count)])  46.2 us
    ppermute x21, waiting for transfers between devices, exchange(): lax.ppermute(blocks[mask], 'cols', [(i, i ^ mask) for i in range(count)])  17.7 us
    pallas_call x11, Pallas kernels, call(): pl.pallas_call(kernel, out_shape=outs, in_specs=in_specs, out_specs=tuple...  14.2 us
    all_to_all x2, starting transfers between devices, exchange(): lax.all_to_all(blocks[0], 'cols', split_axis=0, concat_axis=0, tiled=True)  11.1 us
    ppermute x7, starting transfers between devices, swap(): return lax.ppermute(value, 'rows', [(i, i ^ mask) for i in range(count)])  8.39 us
    ppermute x2, starting transfers between devices, swap_rows(): lax.ppermute(send_b, 'rows', outer)  8.37 us
    ppermute x7, waiting for transfers between devices, swap(): return lax.ppermute(value, 'rows', [(i, i ^ mask) for i in range(count)])  8.06 us
    all_to_all x2, waiting for transfers between devices, exchange(): lax.all_to_all(blocks[0], 'cols', split_axis=0, concat_axis=0, tiled=True)  6.8 us
  transfers between devices with their start and end apart: 34, of which 17 were waited for; matrix products, arithmetic and copies ran while one was open for 0% of the time, Pallas kernels for 4%

profile of v3, /device:TPU:8, one launch (start us, length us, event | category | flops | bytes accessed | tf_op | source)
XLA Modules:
  0.0 125.3 jit_solution(11865342160450084061)
XLA Ops:
  0.6 0.0 copy-start.10
  0.7 0.9 broadcast_select_fusion
  1.5 4.0 %collective-permute-start.1 = (f32[2,2048]{1,0:T(2,128)S(1)}, f32[2,2048]{1,0:T(2,128)S(1)}, u32[]{:S(2)}, u32[]{:S(2)}) collective-permute-start(f32[2,2048]{1,0:T(2,128)S(1)} %get-tuple-element.81), channel_id=1, source_target_pairs={{8,16},{24,32},{40,48},{56,64},{72,80},{88,96},{104,112},{120,128}... | collective-permute-start | bytes 49160 | tf_op jit(solution)/shard_map/ppermute | solution.py:493
  5.5 0.1 collective-permute-start
  5.7 0.1 pad_add_fusion.place
  5.7 0.0 copy-start.9
  5.8 2.6 %shard_map.157 = (f32[64,2176]{1,0:T(8,128)S(1)}, f32[64,2048]{1,0:T(8,128)S(1)}, f32[64,2048]{1,0:T(8,128)S(1)}) custom-call(f32[64,2048]{1,0:T(8,128)} %latent.1, s32[64,2048]{1,0:T(8,128)} %counts.1, s32[64,2048]{1,0:T(8,128)} %exposure.1, bf16[64,192]{1,0:T(8,128)(2,1)S(1)} %copy-done.10), custom_call_target="tpu_custom_call" | custom-call | flops 1000000000 | bytes 3227648 | tf_op jit(solution)/shard_map/pallas_call | solution.py:461
  8.3 0.4 collective-permute-done.1.swap_b
  8.7 0.0 copy-start.3
  8.8 0.0 copy-start.5
  8.8 1.0 shard_map.158
  9.8 2.0 %collective-permute-start.2 = (f32[136,128]{1,0:T(8,128)S(1)}, f32[136,128]{1,0:T(8,128)S(1)}, u32[]{:S(2)}, u32[]{:S(2)}) collective-permute-start(f32[136,128]{1,0:T(8,128)S(1)} %get-tuple-element.44), channel_id=1, source_target_pairs={{0,1},{1,0},{2,3},{3,2},{4,5},{5,4},{6,7},{7,6},{8,9},{9,8},{10,11... | collective-permute-start | bytes 208904 | tf_op jit(solution)/shard_map/ppermute | solution.py:487
  11.8 3.3 %collective-permute-start.3 = (f32[136,128]{1,0:T(8,128)S(1)}, f32[136,128]{1,0:T(8,128)S(1)}, u32[]{:S(2)}, u32[]{:S(2)}) collective-permute-start(f32[136,128]{1,0:T(8,128)S(1)} %get-tuple-element.45), channel_id=1, source_target_pairs={{0,2},{1,3},{2,0},{3,1},{4,6},{5,7},{6,4},{7,5},{8,10},{9,11},{10,... | collective-permute-start | bytes 208904 | tf_op jit(solution)/shard_map/ppermute | solution.py:487
  15.0 6.4 %collective-permute-start.5 = (f32[136,128]{1,0:T(8,128)S(1)}, f32[136,128]{1,0:T(8,128)S(1)}, u32[]{:S(2)}, u32[]{:S(2)}) collective-permute-start(f32[136,128]{1,0:T(8,128)S(1)} %get-tuple-element.47), channel_id=1, source_target_pairs={{0,4},{1,5},{2,6},{3,7},{4,0},{5,1},{6,2},{7,3},{8,12},{9,13},{10,... | collective-permute-start | bytes 208904 | tf_op jit(solution)/shard_map/ppermute | solution.py:487
  21.4 4.6 %collective-permute-start.7 = (f32[136,128]{1,0:T(8,128)S(1)}, f32[136,128]{1,0:T(8,128)S(1)}, u32[]{:S(2)}, u32[]{:S(2)}) collective-permute-start(f32[136,128]{1,0:T(8,128)S(1)} %get-tuple-element.49), channel_id=1, source_target_pairs={{0,6},{1,7},{2,4},{3,5},{4,2},{5,3},{6,0},{7,1},{8,14},{9,15},{10,... | collective-permute-start | bytes 208904 | tf_op jit(solution)/shard_map/ppermute | solution.py:487
  26.0 2.7 %collective-permute-start.8 = (f32[136,128]{1,0:T(8,128)S(1)}, f32[136,128]{1,0:T(8,128)S(1)}, u32[]{:S(2)}, u32[]{:S(2)}) collective-permute-start(f32[136,128]{1,0:T(8,128)S(1)} %get-tuple-element.50), channel_id=1, source_target_pairs={{0,7},{1,6},{2,5},{3,4},{4,3},{5,2},{6,1},{7,0},{8,15},{9,14},{10,... | collective-permute-start | bytes 208904 | tf_op jit(solution)/shard_map/ppermute | solution.py:487
  28.8 1.9 %collective-permute-done.6.rest_5_ = f32[136,128]{1,0:T(8,128)S(1)} collective-permute-done((f32[136,128]{1,0:T(8,128)S(1)}, f32[136,128]{1,0:T(8,128)S(1)}, u32[]{:S(2)}, u32[]{:S(2)}) %collective-permute-start.6) | collective-permute-done | bytes 69664 | tf_op jit(solution)/shard_map/ppermute | solution.py:487
  30.6 1.1 collective-permute-done.7.rest_6_
  31.8 2.5 %collective-permute-done.8.rest_7_ = f32[136,128]{1,0:T(8,128)S(1)} collective-permute-done((f32[136,128]{1,0:T(8,128)S(1)}, f32[136,128]{1,0:T(8,128)S(1)}, u32[]{:S(2)}, u32[]{:S(2)}) %collective-permute-start.8) | collective-permute-done | bytes 69664 | tf_op jit(solution)/shard_map/ppermute | solution.py:487
  34.4 2.2 %shard_map.159 = (f32[136,128]{1,0:T(8,128)S(1)}, f32[136,128]{1,0:T(8,128)S(1)}, f32[136,128]{1,0:T(8,128)S(1)}, f32[136,128]{1,0:T(8,128)S(1)}, f32[136,128]{1...) custom-call(s32[2]{0:T(128)S(1)} %pad_add_fusion.place, ...), custom_call_target="tpu_custom_call" | custom-call | flops 1000000000 | bytes 2393096 | tf_op jit(solution)/shard_map/pallas_call | solution.py:461
  36.5 0.3 collective-permute-start.9
  36.8 1.9 %collective-permute-start.10 = (f32[136,128]{1,0:T(8,128)S(1)}, f32[136,128]{1,0:T(8,128)S(1)}, u32[]{:S(2)}, u32[]{:S(2)}) collective-permute-start(f32[136,128]{1,0:T(8,128)S(1)} %get-tuple-element.53), channel_id=1, source_target_pairs={{0,2},{1,3},{2,0},{3,1},{4,6},{5,7},{6,4},{7,5},{8,10},{9,11},{10,... | collective-permute-start | bytes 208904 | tf_op jit(solution)/shard_map/ppermute | solution.py:487
  38.7 2.3 %collective-permute-start.11 = (f32[136,128]{1,0:T(8,128)S(1)}, f32[136,128]{1,0:T(8,128)S(1)}, u32[]{:S(2)}, u32[]{:S(2)}) collective-permute-start(f32[136,128]{1,0:T(8,128)S(1)} %get-tuple-element.54), channel_id=1, source_target_pairs={{0,3},{1,2},{2,1},{3,0},{4,7},{5,6},{6,5},{7,4},{8,11},{9,10},{10,... | collective-permute-start | bytes 208904 | tf_op jit(solution)/shard_map/ppermute | solution.py:487
  40.9 3.2 %collective-permute-start.12 = (f32[136,128]{1,0:T(8,128)S(1)}, f32[136,128]{1,0:T(8,128)S(1)}, u32[]{:S(2)}, u32[]{:S(2)}) collective-permute-start(f32[136,128]{1,0:T(8,128)S(1)} %get-tuple-element.55), channel_id=1, source_target_pairs={{0,4},{1,5},{2,6},{3,7},{4,0},{5,1},{6,2},{7,3},{8,12},{9,13},{10,... | collective-permute-start | bytes 208904 | tf_op jit(solution)/shard_map/ppermute | solution.py:487
  44.1 0.7 collective-permute-start.13
  44.8 4.0 %collective-permute-start.14 = (f32[136,128]{1,0:T(8,128)S(1)}, f32[136,128]{1,0:T(8,128)S(1)}, u32[]{:S(2)}, u32[]{:S(2)}) collective-permute-start(f32[136,128]{1,0:T(8,128)S(1)} %get-tuple-element.57), channel_id=1, source_target_pairs={{0,6},{1,7},{2,4},{3,5},{4,2},{5,3},{6,0},{7,1},{8,14},{9,15},{10,... | collective-permute-start | bytes 208904 | tf_op jit(solution)/shard_map/ppermute | solution.py:487
  48.8 1.3 %collective-permute-start.15 = (f32[136,128]{1,0:T(8,128)S(1)}, f32[136,128]{1,0:T(8,128)S(1)}, u32[]{:S(2)}, u32[]{:S(2)}) collective-permute-start(f32[136,128]{1,0:T(8,128)S(1)} %get-tuple-element.58), channel_id=1, source_target_pairs={{0,7},{1,6},{2,5},{3,4},{4,3},{5,2},{6,1},{7,0},{8,15},{9,14},{10,... | collective-permute-start | bytes 208904 | tf_op jit(solution)/shard_map/ppermute | solution.py:487
  50.1 0.1 collective-permute-done.12.rest_4_
  50.2 2.2 %collective-permute-done.13.rest_5_ = f32[136,128]{1,0:T(8,128)S(1)} collective-permute-done((f32[136,128]{1,0:T(8,128)S(1)}, f32[136,128]{1,0:T(8,128)S(1)}, u32[]{:S(2)}, u32[]{:S(2)}) %collective-permute-start.13) | collective-permute-done | bytes 69664 | tf_op jit(solution)/shard_map/ppermute | solution.py:487
  52.4 1.5 %collective-permute-done.14.rest_6_ = f32[136,128]{1,0:T(8,128)S(1)} collective-permute-done((f32[136,128]{1,0:T(8,128)S(1)}, f32[136,128]{1,0:T(8,128)S(1)}, u32[]{:S(2)}, u32[]{:S(2)}) %collective-permute-start.14) | collective-permute-done | bytes 69664 | tf_op jit(solution)/shard_map/ppermute | solution.py:487
  53.9 3.2 %collective-permute-done.15.rest_7_ = f32[136,128]{1,0:T(8,128)S(1)} collective-permute-done((f32[136,128]{1,0:T(8,128)S(1)}, f32[136,128]{1,0:T(8,128)S(1)}, u32[]{:S(2)}, u32[]{:S(2)}) %collective-permute-start.15) | collective-permute-done | bytes 69664 | tf_op jit(solution)/shard_map/ppermute | solution.py:487
  57.1 0.9 shard_map.160
  58.1 0.1 collective-permute-start.16
  58.2 4.4 %collective-permute-start.17 = (f32[2,2176]{1,0:T(2,128)S(1)}, f32[2,2176]{1,0:T(2,128)S(1)}, u32[]{:S(2)}, u32[]{:S(2)}) collective-permute-start(f32[2,2176]{1,0:T(2,128)S(1)} %get-tuple-element.65), channel_id=1, source_target_pairs={{8,16},{24,32},{40,48},{56,64},{72,80},{88,96},{104,112},{120,128}... | collective-permute-start | bytes 52232 | tf_op jit(solution)/shard_map/ppermute | solution.py:493
  62.6 1.1 shard_map.161
  63.7 1.7 %collective-permute-done.17.swap_b = f32[2,2176]{1,0:T(2,128)S(1)} collective-permute-done((f32[2,2176]{1,0:T(2,128)S(1)}, f32[2,2176]{1,0:T(2,128)S(1)}, u32[]{:S(2)}, u32[]{:S(2)}) %collective-permute-start.17) | collective-permute-done | bytes 17440 | tf_op jit(solution)/shard_map/ppermute | solution.py:493
  65.3 0.9 shard_map.162
  66.2 0.8 collective-permute-start.18
  67.0 1.3 %collective-permute-start.19 = (f32[128,128]{1,0:T(8,128)S(1)}, f32[128,128]{1,0:T(8,128)S(1)}, u32[]{:S(2)}, u32[]{:S(2)}) collective-permute-start(f32[128,128]{1,0:T(8,128)S(1)} %get-tuple-element.68), channel_id=1, source_target_pairs={{0,2},{1,3},{2,0},{3,1},{4,6},{5,7},{6,4},{7,5},{8,10},{9,11},{10,... | collective-permute-start | bytes 196616 | tf_op jit(solution)/shard_map/ppermute | solution.py:487
  68.3 2.4 %collective-permute-start.20 = (f32[128,128]{1,0:T(8,128)S(1)}, f32[128,128]{1,0:T(8,128)S(1)}, u32[]{:S(2)}, u32[]{:S(2)}) collective-permute-start(f32[128,128]{1,0:T(8,128)S(1)} %get-tuple-element.69), channel_id=1, source_target_pairs={{0,3},{1,2},{2,1},{3,0},{4,7},{5,6},{6,5},{7,4},{8,11},{9,10},{10,... | collective-permute-start | bytes 196616 | tf_op jit(solution)/shard_map/ppermute | solution.py:487
  70.7 2.6 %collective-permute-start.21 = (f32[128,128]{1,0:T(8,128)S(1)}, f32[128,128]{1,0:T(8,128)S(1)}, u32[]{:S(2)}, u32[]{:S(2)}) collective-permute-start(f32[128,128]{1,0:T(8,128)S(1)} %get-tuple-element.70), channel_id=1, source_target_pairs={{0,4},{1,5},{2,6},{3,7},{4,0},{5,1},{6,2},{7,3},{8,12},{9,13},{10,... | collective-permute-start | bytes 196616 | tf_op jit(solution)/shard_map/ppermute | solution.py:487
  73.4 1.6 %collective-permute-start.22 = (f32[128,128]{1,0:T(8,128)S(1)}, f32[128,128]{1,0:T(8,128)S(1)}, u32[]{:S(2)}, u32[]{:S(2)}) collective-permute-start(f32[128,128]{1,0:T(8,128)S(1)} %get-tuple-element.71), channel_id=1, source_target_pairs={{0,5},{1,4},{2,7},{3,6},{4,1},{5,0},{6,3},{7,2},{8,13},{9,12},{10,... | collective-permute-start | bytes 196616 | tf_op jit(solution)/shard_map/ppermute | solution.py:487
  75.0 3.1 %collective-permute-start.23 = (f32[128,128]{1,0:T(8,128)S(1)}, f32[128,128]{1,0:T(8,128)S(1)}, u32[]{:S(2)}, u32[]{:S(2)}) collective-permute-start(f32[128,128]{1,0:T(8,128)S(1)} %get-tuple-element.72), channel_id=1, source_target_pairs={{0,6},{1,7},{2,4},{3,5},{4,2},{5,3},{6,0},{7,1},{8,14},{9,15},{10,... | collective-permute-start | bytes 196616 | tf_op jit(solution)/shard_map/ppermute | solution.py:487
  78.0 1.9 %collective-permute-start.24 = (f32[128,128]{1,0:T(8,128)S(1)}, f32[128,128]{1,0:T(8,128)S(1)}, u32[]{:S(2)}, u32[]{:S(2)}) collective-permute-start(f32[128,128]{1,0:T(8,128)S(1)} %get-tuple-element.73), channel_id=1, source_target_pairs={{0,7},{1,6},{2,5},{3,4},{4,3},{5,2},{6,1},{7,0},{8,15},{9,14},{10,... | collective-permute-start | bytes 196616 | tf_op jit(solution)/shard_map/ppermute | solution.py:487
  79.9 0.3 shard_map.163
  80.3 0.6 collective-permute-done.22.rest_5_
  80.8 1.5 %collective-permute-done.23.rest_6_ = f32[128,128]{1,0:T(8,128)S(1)} collective-permute-done((f32[128,128]{1,0:T(8,128)S(1)}, f32[128,128]{1,0:T(8,128)S(1)}, u32[]{:S(2)}, u32[]{:S(2)}) %collective-permute-start.23) | collective-permute-done | bytes 65568 | tf_op jit(solution)/shard_map/ppermute | solution.py:487
  82.4 3.1 %collective-permute-done.24.rest_7_ = f32[128,128]{1,0:T(8,128)S(1)} collective-permute-done((f32[128,128]{1,0:T(8,128)S(1)}, f32[128,128]{1,0:T(8,128)S(1)}, u32[]{:S(2)}, u32[]{:S(2)}) %collective-permute-start.24) | collective-permute-done | bytes 65568 | tf_op jit(solution)/shard_map/ppermute | solution.py:487
  85.4 2.5 %shard_map.164 = (f32[8,128,128]{2,1,0:T(8,128)}, f32[1,128]{1,0:T(1,128)S(1)}) custom-call(s32[2]{0:T(128)S(1)} %pad_add_fusion.place, f32[128,128]{1,0:T(8,128)S(1)} %get-tuple-element.66.rest_0_, f32[128,128]{1,0:T(8,128)S(1)} %collective-permute-done.18.rest_1_, f32[128,128]{1,0:T(8,128)S(1)} %collective-permute-done.19.rest_2_, ...), custom_call_target="tpu_custom_call" | custom-call | flops 1000000000 | bytes 2327560 | tf_op jit(solution)/shard_map/pallas_call | solution.py:461
  87.9 3.9 %all-to-all-start.1 = ((f32[8,128,128]{2,1,0:T(8,128)}), f32[8,128,128]{2,1,0:T(8,128)S(1)}, u32[]{:S(2)}, u32[]{:S(2)}) async-start(f32[8,128,128]{2,1,0:T(8,128)} %get-tuple-element.80), calls=%async_computation.1 | async-start | bytes 1048576 | tf_op jit(solution)/shard_map/all_to_all | solution.py:483
  91.8 1.1 collective-permute-done.25
  92.9 3.4 %collective-permute-start.28 = (f32[1,128]{1,0:T(1,128)S(1)}, f32[1,128]{1,0:T(1,128)S(1)}, u32[]{:S(2)}, u32[]{:S(2)}) collective-permute-start(f32[1,128]{1,0:T(1,128)S(1)} %add.17), channel_id=1, source_target_pairs={{0,48},{8,56},{16,32},{24,40},{32,16},{40,24},{48,0},{56,8},{64,11... | collective-permute-start | bytes 1544 | tf_op jit(solution)/shard_map/ppermute | solution.py:500
  96.3 0.9 collective-permute-start.26
  97.2 0.7 collective-permute-done.28
  97.8 3.5 %collective-permute-done.27 = f32[1,128]{1,0:T(1,128)S(1)} collective-permute-done((f32[1,128]{1,0:T(1,128)S(1)}, f32[1,128]{1,0:T(1,128)S(1)}, u32[]{:S(2)}, u32[]{:S(2)}) %collective-permute-start.27) | collective-permute-done | bytes 544 | tf_op jit(solution)/shard_map/ppermute | solution.py:500
  101.4 1.9 %collective-permute-start.31 = (f32[1,128]{1,0:T(1,128)S(1)}, f32[1,128]{1,0:T(1,128)S(1)}, u32[]{:S(2)}, u32[]{:S(2)}) collective-permute-start(f32[1,128]{1,0:T(1,128)S(1)} %add_add_fusion.one), channel_id=1, source_target_pairs={{0,192},{8,200},{16,208},{24,216},{32,224},{40,232},{48,240},{56,2... | collective-permute-start | bytes 1544 | tf_op jit(solution)/shard_map/ppermute | solution.py:500
  103.3 0.7 collective-permute-start.30
  104.0 1.6 %collective-permute-start.29 = (f32[1,128]{1,0:T(1,128)S(1)}, f32[1,128]{1,0:T(1,128)S(1)}, u32[]{:S(2)}, u32[]{:S(2)}) collective-permute-start(f32[1,128]{1,0:T(1,128)S(1)} %add_add_fusion.one), channel_id=1, source_target_pairs={{0,64},{8,72},{16,80},{24,88},{32,96},{40,104},{48,112},{56,120},{... | collective-permute-start | bytes 1544 | tf_op jit(solution)/shard_map/ppermute | solution.py:500
  105.5 2.8 %collective-permute-done.30.three = f32[1,128]{1,0:T(1,128)S(1)} collective-permute-done((f32[1,128]{1,0:T(1,128)S(1)}, f32[1,128]{1,0:T(1,128)S(1)}, u32[]{:S(2)}, u32[]{:S(2)}) %collective-permute-start.30) | collective-permute-done | bytes 544 | tf_op jit(solution)/shard_map/ppermute | solution.py:500
  108.3 0.6 shard_map.165
  108.9 7.2 %all-to-all-start = ((f32[8,1,128]{2,1,0:T(1,128)}), f32[8,1,128]{2,1,0:T(1,128)S(1)}, u32[]{:S(2)}, u32[]{:S(2)}) async-start(f32[8,1,128]{2,1,0:T(1,128)} %shard_map.165), calls=%async_computation | async-start | bytes 8192 | tf_op jit(solution)/shard_map/all_to_all | solution.py:483
  116.1 0.8 shard_map.166.second
  116.9 6.8 %all-to-all-done.sums = f32[8,1,128]{2,1,0:T(1,128)S(1)} async-done(((f32[8,1,128]{2,1,0:T(1,128)}), f32[8,1,128]{2,1,0:T(1,128)S(1)}, u32[]{:S(2)}, u32[]{:S(2)}) %all-to-all-start) | async-done | bytes 4128 | tf_op jit(solution)/shard_map/all_to_all | solution.py:483
  123.7 1.4 %shard_map.167 = (f32[64,2048]{1,0:T(8,128)}, f32[64,2048]{1,0:T(8,128)}, f32[64,2048]{1,0:T(8,128)}) custom-call(f32[8,1,128]{2,1,0:T(1,128)S(1)} %all-to-all-done.sums, f32[64,2176]{1,0:T(8,128)S(1)} %get-tuple-element.61.search, f32[64,2048]{1,0:T(8,128)S(1)} %get-tuple-element.74.grad, f32[64,2048]{1,0:T(8,128)S(1)} %get-tuple-element.79.rest_1_.image, ...), custom_call_target="tpu_custom_call" | custom-call | flops 1000000 | bytes 3706880 | tf_op jit(solution)/shard_map/pallas_call | solution.py:461
  (42 shorter events, 0.1 us)
Async XLA Ops:
  0.6 5.1 %copy-start.10 = (bf16[64,192]{1,0:T(8,128)(2,1)S(1)}, bf16[64,192]{1,0:T(8,128)(2,1)}, u32[]{:S(2)}) copy-start(bf16[64,192]{1,0:T(8,128)(2,1)} %constant.47.clone.basis) | copy-start | bytes 73732
  1.5 7.2 %collective-permute-start.1 = (f32[2,2048]{1,0:T(2,128)S(1)}, f32[2,2048]{1,0:T(2,128)S(1)}, u32[]{:S(2)}, u32[]{:S(2)}) collective-permute-start(f32[2,2048]{1,0:T(2,128)S(1)} %get-tuple-element.81), channel_id=1, source_target_pairs={{8,16},{24,32},{40,48},{56,64},{72,80},{88,96},{104,112},{120,128}... | collective-permute-start | bytes 49160 | tf_op jit(solution)/shard_map/ppermute | solution.py:493
  5.5 3.2 %collective-permute-start = (f32[2,2048]{1,0:T(2,128)S(1)}, f32[2,2048]{1,0:T(2,128)S(1)}, u32[]{:S(2)}, u32[]{:S(2)}) collective-permute-start(f32[2,2048]{1,0:T(2,128)S(1)} %get-tuple-element.82), channel_id=1, source_target_pairs={{0,8},{8,0},{16,24},{24,16},{32,40},{40,32},{48,56},{56,48},{64,72... | collective-permute-start | bytes 49160 | tf_op jit(solution)/shard_map/ppermute | solution.py:493
  5.7 3.0 %copy-start.1 = (bf16[64,48]{1,0:T(8,128)(2,1)S(1)}, bf16[64,48]{1,0:T(8,128)(2,1)}, u32[]{:S(2)}) copy-start(bf16[64,48]{1,0:T(8,128)(2,1)} %constant.48.clone.basis) | copy-start | bytes 18436
  5.7 28.6 %copy-start.6 = (f32[2,72,128]{2,1,0:T(8,128)S(1)}, f32[2,72,128]{2,1,0:T(8,128)}, u32[]{:S(2)}) copy-start(f32[2,72,128]{2,1,0:T(8,128)} %constant.53.clone.rest_16_) | copy-start | bytes 221188
  5.7 28.6 %copy-start.8 = (f32[72,128]{1,0:T(8,128)S(1)}, f32[72,128]{1,0:T(8,128)}, u32[]{:S(2)}) copy-start(f32[72,128]{1,0:T(8,128)} %constant.56.clone.rest_11_) | copy-start | bytes 110596
  5.7 28.6 %copy-start.9 = (f32[64,128]{1,0:T(8,128)S(1)}, f32[64,128]{1,0:T(8,128)}, u32[]{:S(2)}) copy-start(f32[64,128]{1,0:T(8,128)} %constant.50.clone.rest_9_) | copy-start | bytes 98308
  8.7 25.6 %copy-start.2 = (bf16[384,256]{1,0:T(8,128)(2,1)S(1)}, bf16[384,256]{1,0:T(8,128)(2,1)}, u32[]{:S(2)}) copy-start(bf16[384,256]{1,0:T(8,128)(2,1)} %constant.55.clone.rest_15_) | copy-start | bytes 589828
  8.7 25.6 %copy-start.3 = (bf16[256,256]{1,0:T(8,128)(2,1)S(1)}, bf16[256,256]{1,0:T(8,128)(2,1)}, u32[]{:S(2)}) copy-start(bf16[256,256]{1,0:T(8,128)(2,1)} %constant.54.clone.rest_14_) | copy-start | bytes 393220
  8.7 25.6 %copy-start.4 = (bf16[128,432]{1,0:T(8,128)(2,1)S(1)}, bf16[128,432]{1,0:T(8,128)(2,1)}, u32[]{:S(2)}) copy-start(bf16[128,432]{1,0:T(8,128)(2,1)} %constant.52.clone.rest_13_) | copy-start | bytes 331780
  8.8 25.6 %copy-start.5 = (bf16[144,384]{1,0:T(8,128)(2,1)S(1)}, bf16[144,384]{1,0:T(8,128)(2,1)}, u32[]{:S(2)}) copy-start(bf16[144,384]{1,0:T(8,128)(2,1)} %constant.51.clone.rest_12_) | copy-start | bytes 331780
  8.8 25.6 %copy-start.7 = (f32[72,128]{1,0:T(8,128)S(1)}, f32[72,128]{1,0:T(8,128)}, u32[]{:S(2)}) copy-start(f32[72,128]{1,0:T(8,128)} %constant.57.clone.rest_10_) | copy-start | bytes 110596
  9.8 11.7 %collective-permute-start.2 = (f32[136,128]{1,0:T(8,128)S(1)}, f32[136,128]{1,0:T(8,128)S(1)}, u32[]{:S(2)}, u32[]{:S(2)}) collective-permute-start(f32[136,128]{1,0:T(8,128)S(1)} %get-tuple-element.44), channel_id=1, source_target_pairs={{0,1},{1,0},{2,3},{3,2},{4,5},{5,4},{6,7},{7,6},{8,9},{9,8},{10,11... | collective-permute-start | bytes 208904 | tf_op jit(solution)/shard_map/ppermute | solution.py:487
  11.8 14.3 %collective-permute-start.3 = (f32[136,128]{1,0:T(8,128)S(1)}, f32[136,128]{1,0:T(8,128)S(1)}, u32[]{:S(2)}, u32[]{:S(2)}) collective-permute-start(f32[136,128]{1,0:T(8,128)S(1)} %get-tuple-element.45), channel_id=1, source_target_pairs={{0,2},{1,3},{2,0},{3,1},{4,6},{5,7},{6,4},{7,5},{8,10},{9,11},{10,... | collective-permute-start | bytes 208904 | tf_op jit(solution)/shard_map/ppermute | solution.py:487
  15.0 13.7 %collective-permute-start.4 = (f32[136,128]{1,0:T(8,128)S(1)}, f32[136,128]{1,0:T(8,128)S(1)}, u32[]{:S(2)}, u32[]{:S(2)}) collective-permute-start(f32[136,128]{1,0:T(8,128)S(1)} %get-tuple-element.46), channel_id=1, source_target_pairs={{0,3},{1,2},{2,1},{3,0},{4,7},{5,6},{6,5},{7,4},{8,11},{9,10},{10,... | collective-permute-start | bytes 208904 | tf_op jit(solution)/shard_map/ppermute | solution.py:487
  15.0 13.7 %collective-permute-start.5 = (f32[136,128]{1,0:T(8,128)S(1)}, f32[136,128]{1,0:T(8,128)S(1)}, u32[]{:S(2)}, u32[]{:S(2)}) collective-permute-start(f32[136,128]{1,0:T(8,128)S(1)} %get-tuple-element.47), channel_id=1, source_target_pairs={{0,4},{1,5},{2,6},{3,7},{4,0},{5,1},{6,2},{7,3},{8,12},{9,13},{10,... | collective-permute-start | bytes 208904 | tf_op jit(solution)/shard_map/ppermute | solution.py:487
  21.4 9.2 %collective-permute-start.6 = (f32[136,128]{1,0:T(8,128)S(1)}, f32[136,128]{1,0:T(8,128)S(1)}, u32[]{:S(2)}, u32[]{:S(2)}) collective-permute-start(f32[136,128]{1,0:T(8,128)S(1)} %get-tuple-element.48), channel_id=1, source_target_pairs={{0,5},{1,4},{2,7},{3,6},{4,1},{5,0},{6,3},{7,2},{8,13},{9,12},{10,... | collective-permute-start | bytes 208904 | tf_op jit(solution)/shard_map/ppermute | solution.py:487
  21.4 10.3 %collective-permute-start.7 = (f32[136,128]{1,0:T(8,128)S(1)}, f32[136,128]{1,0:T(8,128)S(1)}, u32[]{:S(2)}, u32[]{:S(2)}) collective-permute-start(f32[136,128]{1,0:T(8,128)S(1)} %get-tuple-element.49), channel_id=1, source_target_pairs={{0,6},{1,7},{2,4},{3,5},{4,2},{5,3},{6,0},{7,1},{8,14},{9,15},{10,... | collective-permute-start | bytes 208904 | tf_op jit(solution)/shard_map/ppermute | solution.py:487
  26.0 8.2 %collective-permute-start.8 = (f32[136,128]{1,0:T(8,128)S(1)}, f32[136,128]{1,0:T(8,128)S(1)}, u32[]{:S(2)}, u32[]{:S(2)}) collective-permute-start(f32[136,128]{1,0:T(8,128)S(1)} %get-tuple-element.50), channel_id=1, source_target_pairs={{0,7},{1,6},{2,5},{3,4},{4,3},{5,2},{6,1},{7,0},{8,15},{9,14},{10,... | collective-permute-start | bytes 208904 | tf_op jit(solution)/shard_map/ppermute | solution.py:487
  34.3 22.8 %copy-start = (bf16[64,192]{1,0:T(8,128)(2,1)S(1)}, bf16[64,192]{1,0:T(8,128)(2,1)}, u32[]{:S(2)}) copy-start(bf16[64,192]{1,0:T(8,128)(2,1)} %constant.49.clone.rest_10_.rest_2_) | copy-start | bytes 73732
  36.5 8.2 %collective-permute-start.9 = (f32[136,128]{1,0:T(8,128)S(1)}, f32[136,128]{1,0:T(8,128)S(1)}, u32[]{:S(2)}, u32[]{:S(2)}) collective-permute-start(f32[136,128]{1,0:T(8,128)S(1)} %get-tuple-element.52), channel_id=1, source_target_pairs={{0,1},{1,0},{2,3},{3,2},{4,5},{5,4},{6,7},{7,6},{8,9},{9,8},{10,11... | collective-permute-start | bytes 208904 | tf_op jit(solution)/shard_map/ppermute | solution.py:487
  36.8 12.0 %collective-permute-start.10 = (f32[136,128]{1,0:T(8,128)S(1)}, f32[136,128]{1,0:T(8,128)S(1)}, u32[]{:S(2)}, u32[]{:S(2)}) collective-permute-start(f32[136,128]{1,0:T(8,128)S(1)} %get-tuple-element.53), channel_id=1, source_target_pairs={{0,2},{1,3},{2,0},{3,1},{4,6},{5,7},{6,4},{7,5},{8,10},{9,11},{10,... | collective-permute-start | bytes 208904 | tf_op jit(solution)/shard_map/ppermute | solution.py:487
  38.7 11.4 %collective-permute-start.11 = (f32[136,128]{1,0:T(8,128)S(1)}, f32[136,128]{1,0:T(8,128)S(1)}, u32[]{:S(2)}, u32[]{:S(2)}) collective-permute-start(f32[136,128]{1,0:T(8,128)S(1)} %get-tuple-element.54), channel_id=1, source_target_pairs={{0,3},{1,2},{2,1},{3,0},{4,7},{5,6},{6,5},{7,4},{8,11},{9,10},{10,... | collective-permute-start | bytes 208904 | tf_op jit(solution)/shard_map/ppermute | solution.py:487
  40.9 9.3 %collective-permute-start.12 = (f32[136,128]{1,0:T(8,128)S(1)}, f32[136,128]{1,0:T(8,128)S(1)}, u32[]{:S(2)}, u32[]{:S(2)}) collective-permute-start(f32[136,128]{1,0:T(8,128)S(1)} %get-tuple-element.55), channel_id=1, source_target_pairs={{0,4},{1,5},{2,6},{3,7},{4,0},{5,1},{6,2},{7,3},{8,12},{9,13},{10,... | collective-permute-start | bytes 208904 | tf_op jit(solution)/shard_map/ppermute | solution.py:487
  44.1 8.4 %collective-permute-start.13 = (f32[136,128]{1,0:T(8,128)S(1)}, f32[136,128]{1,0:T(8,128)S(1)}, u32[]{:S(2)}, u32[]{:S(2)}) collective-permute-start(f32[136,128]{1,0:T(8,128)S(1)} %get-tuple-element.56), channel_id=1, source_target_pairs={{0,5},{1,4},{2,7},{3,6},{4,1},{5,0},{6,3},{7,2},{8,13},{9,12},{10,... | collective-permute-start | bytes 208904 | tf_op jit(solution)/shard_map/ppermute | solution.py:487
  44.8 9.2 %collective-permute-start.14 = (f32[136,128]{1,0:T(8,128)S(1)}, f32[136,128]{1,0:T(8,128)S(1)}, u32[]{:S(2)}, u32[]{:S(2)}) collective-permute-start(f32[136,128]{1,0:T(8,128)S(1)} %get-tuple-element.57), channel_id=1, source_target_pairs={{0,6},{1,7},{2,4},{3,5},{4,2},{5,3},{6,0},{7,1},{8,14},{9,15},{10,... | collective-permute-start | bytes 208904 | tf_op jit(solution)/shard_map/ppermute | solution.py:487
  48.8 8.3 %collective-permute-start.15 = (f32[136,128]{1,0:T(8,128)S(1)}, f32[136,128]{1,0:T(8,128)S(1)}, u32[]{:S(2)}, u32[]{:S(2)}) collective-permute-start(f32[136,128]{1,0:T(8,128)S(1)} %get-tuple-element.58), channel_id=1, source_target_pairs={{0,7},{1,6},{2,5},{3,4},{4,3},{5,2},{6,1},{7,0},{8,15},{9,14},{10,... | collective-permute-start | bytes 208904 | tf_op jit(solution)/shard_map/ppermute | solution.py:487
  58.1 5.6 %collective-permute-start.16 = (f32[2,2176]{1,0:T(2,128)S(1)}, f32[2,2176]{1,0:T(2,128)S(1)}, u32[]{:S(2)}, u32[]{:S(2)}) collective-permute-start(f32[2,2176]{1,0:T(2,128)S(1)} %get-tuple-element.64), channel_id=1, source_target_pairs={{0,8},{8,0},{16,24},{24,16},{32,40},{40,32},{48,56},{56,48},{64,72... | collective-permute-start | bytes 52232 | tf_op jit(solution)/shard_map/ppermute | solution.py:493
  58.2 7.2 %collective-permute-start.17 = (f32[2,2176]{1,0:T(2,128)S(1)}, f32[2,2176]{1,0:T(2,128)S(1)}, u32[]{:S(2)}, u32[]{:S(2)}) collective-permute-start(f32[2,2176]{1,0:T(2,128)S(1)} %get-tuple-element.65), channel_id=1, source_target_pairs={{8,16},{24,32},{40,48},{56,64},{72,80},{88,96},{104,112},{120,128}... | collective-permute-start | bytes 52232 | tf_op jit(solution)/shard_map/ppermute | solution.py:493
  66.2 8.7 %collective-permute-start.18 = (f32[128,128]{1,0:T(8,128)S(1)}, f32[128,128]{1,0:T(8,128)S(1)}, u32[]{:S(2)}, u32[]{:S(2)}) collective-permute-start(f32[128,128]{1,0:T(8,128)S(1)} %get-tuple-element.67), channel_id=1, source_target_pairs={{0,1},{1,0},{2,3},{3,2},{4,5},{5,4},{6,7},{7,6},{8,9},{9,8},{10,11... | collective-permute-start | bytes 196616 | tf_op jit(solution)/shard_map/ppermute | solution.py:487
  67.0 11.0 %collective-permute-start.19 = (f32[128,128]{1,0:T(8,128)S(1)}, f32[128,128]{1,0:T(8,128)S(1)}, u32[]{:S(2)}, u32[]{:S(2)}) collective-permute-start(f32[128,128]{1,0:T(8,128)S(1)} %get-tuple-element.68), channel_id=1, source_target_pairs={{0,2},{1,3},{2,0},{3,1},{4,6},{5,7},{6,4},{7,5},{8,10},{9,11},{10,... | collective-permute-start | bytes 196616 | tf_op jit(solution)/shard_map/ppermute | solution.py:487
  68.3 12.0 %collective-permute-start.20 = (f32[128,128]{1,0:T(8,128)S(1)}, f32[128,128]{1,0:T(8,128)S(1)}, u32[]{:S(2)}, u32[]{:S(2)}) collective-permute-start(f32[128,128]{1,0:T(8,128)S(1)} %get-tuple-element.69), channel_id=1, source_target_pairs={{0,3},{1,2},{2,1},{3,0},{4,7},{5,6},{6,5},{7,4},{8,11},{9,10},{10,... | collective-permute-start | bytes 196616 | tf_op jit(solution)/shard_map/ppermute | solution.py:487
  70.7 9.5 %collective-permute-start.21 = (f32[128,128]{1,0:T(8,128)S(1)}, f32[128,128]{1,0:T(8,128)S(1)}, u32[]{:S(2)}, u32[]{:S(2)}) collective-permute-start(f32[128,128]{1,0:T(8,128)S(1)} %get-tuple-element.70), channel_id=1, source_target_pairs={{0,4},{1,5},{2,6},{3,7},{4,0},{5,1},{6,2},{7,3},{8,12},{9,13},{10,... | collective-permute-start | bytes 196616 | tf_op jit(solution)/shard_map/ppermute | solution.py:487
  73.4 7.5 %collective-permute-start.22 = (f32[128,128]{1,0:T(8,128)S(1)}, f32[128,128]{1,0:T(8,128)S(1)}, u32[]{:S(2)}, u32[]{:S(2)}) collective-permute-start(f32[128,128]{1,0:T(8,128)S(1)} %get-tuple-element.71), channel_id=1, source_target_pairs={{0,5},{1,4},{2,7},{3,6},{4,1},{5,0},{6,3},{7,2},{8,13},{9,12},{10,... | collective-permute-start | bytes 196616 | tf_op jit(solution)/shard_map/ppermute | solution.py:487
  75.0 7.4 %collective-permute-start.23 = (f32[128,128]{1,0:T(8,128)S(1)}, f32[128,128]{1,0:T(8,128)S(1)}, u32[]{:S(2)}, u32[]{:S(2)}) collective-permute-start(f32[128,128]{1,0:T(8,128)S(1)} %get-tuple-element.72), channel_id=1, source_target_pairs={{0,6},{1,7},{2,4},{3,5},{4,2},{5,3},{6,0},{7,1},{8,14},{9,15},{10,... | collective-permute-start | bytes 196616 | tf_op jit(solution)/shard_map/ppermute | solution.py:487
  78.0 7.4 %collective-permute-start.24 = (f32[128,128]{1,0:T(8,128)S(1)}, f32[128,128]{1,0:T(8,128)S(1)}, u32[]{:S(2)}, u32[]{:S(2)}) collective-permute-start(f32[128,128]{1,0:T(8,128)S(1)} %get-tuple-element.73), channel_id=1, source_target_pairs={{0,7},{1,6},{2,5},{3,4},{4,3},{5,2},{6,1},{7,0},{8,15},{9,14},{10,... | collective-permute-start | bytes 196616 | tf_op jit(solution)/shard_map/ppermute | solution.py:487
  87.9 21.0 %all-to-all-start.1 = ((f32[8,128,128]{2,1,0:T(8,128)}), f32[8,128,128]{2,1,0:T(8,128)S(1)}, u32[]{:S(2)}, u32[]{:S(2)}) async-start(f32[8,128,128]{2,1,0:T(8,128)} %get-tuple-element.80), calls=%async_computation.1 | async-start | bytes 1048576 | tf_op jit(solution)/shard_map/all_to_all | solution.py:483
  91.8 1.1 collective-permute-start.25
  92.9 4.9 %collective-permute-start.28 = (f32[1,128]{1,0:T(1,128)S(1)}, f32[1,128]{1,0:T(1,128)S(1)}, u32[]{:S(2)}, u32[]{:S(2)}) collective-permute-start(f32[1,128]{1,0:T(1,128)S(1)} %add.17), channel_id=1, source_target_pairs={{0,48},{8,56},{16,32},{24,40},{32,16},{40,24},{48,0},{56,8},{64,11... | collective-permute-start | bytes 1544 | tf_op jit(solution)/shard_map/ppermute | solution.py:500
  96.3 5.0 %collective-permute-start.27 = (f32[1,128]{1,0:T(1,128)S(1)}, f32[1,128]{1,0:T(1,128)S(1)}, u32[]{:S(2)}, u32[]{:S(2)}) collective-permute-start(f32[1,128]{1,0:T(1,128)S(1)} %add.17), channel_id=1, source_target_pairs={{0,32},{8,40},{16,48},{24,56},{32,0},{40,8},{48,16},{56,24},{64,96... | collective-permute-start | bytes 1544 | tf_op jit(solution)/shard_map/ppermute | solution.py:500
  96.3 5.0 %collective-permute-start.26 = (f32[1,128]{1,0:T(1,128)S(1)}, f32[1,128]{1,0:T(1,128)S(1)}, u32[]{:S(2)}, u32[]{:S(2)}) collective-permute-start(f32[1,128]{1,0:T(1,128)S(1)} %add.17), channel_id=1, source_target_pairs={{0,16},{8,24},{16,0},{24,8},{32,48},{40,56},{48,32},{56,40},{64,80... | collective-permute-start | bytes 1544 | tf_op jit(solution)/shard_map/ppermute | solution.py:500
  101.4 4.2 %collective-permute-start.31 = (f32[1,128]{1,0:T(1,128)S(1)}, f32[1,128]{1,0:T(1,128)S(1)}, u32[]{:S(2)}, u32[]{:S(2)}) collective-permute-start(f32[1,128]{1,0:T(1,128)S(1)} %add_add_fusion.one), channel_id=1, source_target_pairs={{0,192},{8,200},{16,208},{24,216},{32,224},{40,232},{48,240},{56,2... | collective-permute-start | bytes 1544 | tf_op jit(solution)/shard_map/ppermute | solution.py:500
  103.3 5.0 %collective-permute-start.30 = (f32[1,128]{1,0:T(1,128)S(1)}, f32[1,128]{1,0:T(1,128)S(1)}, u32[]{:S(2)}, u32[]{:S(2)}) collective-permute-start(f32[1,128]{1,0:T(1,128)S(1)} %add_add_fusion.one), channel_id=1, source_target_pairs={{0,128},{8,136},{16,144},{24,152},{32,160},{40,168},{48,176},{56,1... | collective-permute-start | bytes 1544 | tf_op jit(solution)/shard_map/ppermute | solution.py:500
  104.0 4.3 %collective-permute-start.29 = (f32[1,128]{1,0:T(1,128)S(1)}, f32[1,128]{1,0:T(1,128)S(1)}, u32[]{:S(2)}, u32[]{:S(2)}) collective-permute-start(f32[1,128]{1,0:T(1,128)S(1)} %add_add_fusion.one), channel_id=1, source_target_pairs={{0,64},{8,72},{16,80},{24,88},{32,96},{40,104},{48,112},{56,120},{... | collective-permute-start | bytes 1544 | tf_op jit(solution)/shard_map/ppermute | solution.py:500
  108.9 14.8 %all-to-all-start = ((f32[8,1,128]{2,1,0:T(1,128)}), f32[8,1,128]{2,1,0:T(1,128)S(1)}, u32[]{:S(2)}, u32[]{:S(2)}) async-start(f32[8,1,128]{2,1,0:T(1,128)} %shard_map.165), calls=%async_computation | async-start | bytes 8192 | tf_op jit(solution)/shard_map/all_to_all | solution.py:483

commit v4 on v3

--- a/solution.py
+++ b/solution.py
@@ -27,7 +27,6 @@
 kept = 64
 vmem_bytes = 48 * 1024 * 1024
 pieces = 4
-pairwise = (True, True, True, False)
 
 
 def high_low(table):
@@ -255,29 +254,11 @@
     store_coefs(place, jnp.concatenate([whole[:, :width], spill], 1), buffer, outs, tiles + 1)
 
 
-def filter_kernel(place, *rest, edges, taken, given):
-    blocks_in, rest = rest[:taken], rest[taken:]
-    (
-        sums,
-        row_term,
-        col_term,
-        weight,
-        outer_forward,
-        outer_inverse,
-        inner_forward,
-        inner_inverse,
-        twist,
-    ) = rest[:9]
-    blocks_out, (known, incoming, out) = rest[9 : 9 + given], rest[9 + given :]
-    incoming = load_blocks(place, blocks_in, incoming)
-    if given == 1:
-        out = blocks_out[0]
+def gather_lines(incoming, edges):
     lane = lane_index((tiles, lanes))
     sub = lax.broadcasted_iota(jnp.int32, (tiles, lanes), 0)
     first = (sub == 0) & (lane < 2)
     last = (sub == tiles - 1) & (lane >= lanes - 2)
-    if edges:
-        known[...] = sums[...]
     line_fields = []
     for line in range(lines):
         blocks = [
@@ -294,7 +275,10 @@
                 if part < parts - 1:
                     blocks[part] = blocks[part] + jnp.where(last, spill[part + 1], 0.0)
         line_fields.append(jnp.concatenate(blocks, 0))
-    field = jnp.concatenate(line_fields, 1)
+    return jnp.concatenate(line_fields, 1)
+
+
+def columns_forward(field, outer_forward, inner_forward, twist):
     section = left_product(outer_forward[...], field)
     cosine, sine = twist[0], twist[1]
     turned = []
@@ -306,7 +290,10 @@
         turned.append(jnp.concatenate([real, imag], 1))
     high, low = split(jnp.concatenate(turned, 0))
     both = dot(high, inner_forward[...])
-    spectrum = both[:, : 2 * kept] + both[:, 2 * kept :] + dot(low, inner_forward[:, : 2 * kept])
+    return both[:, : 2 * kept] + both[:, 2 * kept :] + dot(low, inner_forward[:, : 2 * kept])
+
+
+def scale_spectrum(place, spectrum, row_term, col_term, weight):
     row_line = row_term[pl.ds(pl.multiple_of(place[1] * lines, lines), lines), :]
     scaled = []
     total = jnp.zeros((half, 2 * kept), jnp.float32)
@@ -316,15 +303,16 @@
         gain = -quad / (quad + weight_shift) * weight[...]
         piece = spectrum[line * half : (line + 1) * half, :]
         scaled.append(piece * gain)
-        if not edges:
-            total = total + piece * scaled[-1]
-    if not edges:
-        energy = jnp.sum(total, axis=(0, 1), keepdims=True)
-        known[...] = sums[...] + jnp.where(lane_index((1, lanes)) == 2, energy, 0.0)
-    high, low = split(jnp.concatenate(scaled, 0))
+        total = total + piece * scaled[-1]
+    return jnp.concatenate(scaled, 0), total
+
+
+def columns_inverse(scaled, outer_inverse, inner_inverse, twist):
+    high, low = split(scaled)
     back = dot(jnp.concatenate([high, low], 1), inner_inverse[: 4 * kept, :]) + dot(
         high, inner_inverse[4 * kept :, :]
     )
+    cosine, sine = twist[0], twist[1]
     reals, imags = [], []
     for line in range(lines):
         rows = slice(line * half, (line + 1) * half)
@@ -332,32 +320,68 @@
         reals.append(real * cosine - imag * sine)
         imags.append(imag * cosine + real * sine)
     folded = jnp.concatenate([jnp.concatenate(reals, 1), jnp.concatenate(imags, 1)], 0)
-    result = left_product(outer_inverse[...], folded)
+    return left_product(outer_inverse[...], folded)
+
+
+def store_lines(result, out):
+    for line in range(lines):
+        for part in range(parts):
+            out[part, pl.ds(line, tiles, stride=lines), :] = result[
+                part * tiles : (part + 1) * tiles, line * lanes : (line + 1) * lanes
+            ]
+
+
+def filter_kernel(place, *rest):
+    blocks_in, rest = rest[:parts], rest[parts:]
+    row_term, col_term, weight, outer_forward, inner_forward, twist, outer_inverse, inner_inverse = (
+        rest[:8]
+    )
+    blocks_out, (incoming, out) = rest[8 : 8 + parts], rest[8 + parts :]
+    incoming = load_blocks(place, blocks_in, incoming)
+    field = gather_lines(incoming, True)
+    spectrum = columns_forward(field, outer_forward, inner_forward, twist)
+    scaled, _ = scale_spectrum(place, spectrum, row_term, col_term, weight)
+    result = columns_inverse(scaled, outer_inverse, inner_inverse, twist)
+    store_lines(result, out)
     edge_lane = lane_index((1, lanes))
     nothing = jnp.zeros((1, lanes), jnp.float32)
     for line in range(lines):
         cols = slice(line * lanes, (line + 1) * lanes)
+        spot = tiles * lines + line
         for part in range(parts):
-            out[part, pl.ds(line, tiles, stride=lines), :] = result[
-                part * tiles : (part + 1) * tiles, cols
-            ]
-        if edges:
-            spot = tiles * lines + line
-            for part in range(parts):
-                after, before, from_left, from_right = nothing, nothing, nothing, nothing
-                if part < parts - 1:
-                    row = slice((part + 1) * tiles, (part + 1) * tiles + 1)
-                    after = result[row, cols] + field[row, cols]
-                    from_right = incoming[part + 1, spot : spot + 1, :]
-                if part > 0:
-                    row = slice(part * tiles - 1, part * tiles)
-                    before = result[row, cols] + field[row, cols]
-                    from_left = incoming[part - 1, spot : spot + 1, :]
-                middle = jnp.where(edge_lane >= lanes // 2, from_left, from_right)
-                out[part, spot : spot + 1, :] = jnp.where(
-                    edge_lane < 2, after, jnp.where(edge_lane >= lanes - 2, before, middle)
-                )
+            after, before, from_left, from_right = nothing, nothing, nothing, nothing
+            if part < parts - 1:
+                row = slice((part + 1) * tiles, (part + 1) * tiles + 1)
+                after = result[row, cols] + field[row, cols]
+                from_right = incoming[part + 1, spot : spot + 1, :]
+            if part > 0:
+                row = slice(part * tiles - 1, part * tiles)
+                before = result[row, cols] + field[row, cols]
+                from_left = incoming[part - 1, spot : spot + 1, :]
+            middle = jnp.where(edge_lane >= lanes // 2, from_left, from_right)
+            out[part, spot : spot + 1, :] = jnp.where(
+                edge_lane < 2, after, jnp.where(edge_lane >= lanes - 2, before, middle)
+            )
     store_blocks(place, out, blocks_out)
+
+
+def front_kernel(place, *rest):
+    blocks_in, rest = rest[:parts], rest[parts:]
+    sums, row_term, col_term, weight, outer_forward, inner_forward, twist = rest[:7]
+    spectrum_out, known, incoming = rest[7:]
+    incoming = load_blocks(place, blocks_in, incoming)
+    field = gather_lines(incoming, False)
+    spectrum = columns_forward(field, outer_forward, inner_forward, twist)
+    scaled, total = scale_spectrum(place, spectrum, row_term, col_term, weight)
+    spectrum_out[...] = scaled
+    energy = jnp.sum(total, axis=(0, 1), keepdims=True)
+    line = sums[...] + jnp.where(lane_index((1, lanes)) == 2, energy, 0.0)
+    for part in range(parts):
+        known[part] = line
+
+
+def back_kernel(scaled, twist, outer_inverse, inner_inverse, out):
+    store_lines(columns_inverse(scaled[...], outer_inverse, inner_inverse, twist), out)
 
 
 def search_kernel(place, *rest):
@@ -408,12 +432,6 @@
         total = jnp.sum(product, axis=(0, 1), keepdims=True)
         line = line + jnp.where(lane == which, total, 0.0)
     sums[...] = line
-
-
-def spread_kernel(one, two, three, four, spread):
-    total = (one[...] + two[...]) + (three[...] + four[...])
-    for part in range(parts):
-        spread[part] = total
 
 
 def second_kernel(place, *rest):
@@ -493,15 +511,9 @@
     return lax.ppermute(send_a, "rows", inner), lax.ppermute(send_b, "rows", outer)
 
 
-def sum_over_rows(value):
+def row_swap(value, mask):
     count = lax.axis_size("rows")
-
-    def swap(mask):
-        return lax.ppermute(value, "rows", [(i, i ^ mask) for i in range(count)])
-
-    value = value + swap(1)
-    value = value + swap(2) + swap(4) + swap(6)
-    return value, swap(8), swap(16), swap(24)
+    return lax.ppermute(value, "rows", [(i, i ^ mask) for i in range(count)])
 
 
 def on_device(latent, counts, exposure):
@@ -516,24 +528,13 @@
     slim = (tiles * lines, lanes)
     wide_buffer = pltpu.VMEM((parts, *wide), jnp.float32)
     slim_buffer = pltpu.VMEM((parts, *slim), jnp.float32)
-    def sent(shape, pairwise):
-        return (shape,) * parts if pairwise else ((parts, *shape),)
-
     block = (band, width)
     extended = (band, full)
-    filters = [
+    forward = [
         tab[name]
-        for name in (
-            "row_term",
-            "col_term",
-            "weight",
-            "outer_forward",
-            "outer_inverse",
-            "inner_forward",
-            "inner_inverse",
-            "twist",
-        )
+        for name in ("row_term", "col_term", "weight", "outer_forward", "inner_forward", "twist")
     ]
+    inverse = [tab["outer_inverse"], tab["inner_inverse"]]
 
     even = row_index % 2 == 0
     top, bottom = latent[:2], latent[band - 2 :]
@@ -556,18 +557,16 @@
     )
     *blocks, added = call(
         gradient_halo_kernel,
-        sent(wide, pairwise[0]) + ((8, full),),
+        (wide,) * parts + ((8, full),),
         (place, coefs, swap_a, swap_b, tab["halo_forward"]),
         (halo, wide_buffer),
         flops=10**7,
     )
     blocks = exchange(blocks)
-    *blocks, _ = call(
-        functools.partial(
-            filter_kernel, edges=True, taken=len(blocks), given=parts if pairwise[1] else 1
-        ),
-        (*sent(wide, pairwise[1]), (1, lanes)),
-        (place, *blocks, jnp.zeros((1, lanes), jnp.float32), *filters),
+    blocks = call(
+        filter_kernel,
+        (wide,) * parts,
+        (place, *blocks, *forward, *inverse),
         (wide_buffer, wide_buffer),
         flops=10**9,
     )
@@ -589,7 +588,7 @@
     )
     *blocks, added = call(
         image_halo_kernel,
-        sent(slim, pairwise[2]) + ((8, full),),
+        (slim,) * parts + ((8, full),),
         (place, coefs, swap_a, swap_b, tab["halo_forward"]),
         (halo, slim_buffer),
         flops=10**7,
@@ -598,18 +597,21 @@
     image, sums = call(
         sums_kernel, (block, (1, lanes)), (search, grad, partial, added), flops=10**8
     )
-    *blocks, known = call(
-        functools.partial(
-            filter_kernel, edges=False, taken=len(blocks), given=parts if pairwise[3] else 1
-        ),
-        (*sent(slim, pairwise[3]), (1, lanes)),
-        (place, *blocks, sums, *filters),
-        (slim_buffer, slim_buffer),
-        flops=10**9,
-    )
-    blocks = exchange(blocks)
-    (spread,) = call(spread_kernel, ((parts, 1, lanes),), sum_over_rows(known))
-    sums = exchange([spread])[0]
+    scaled, known = call(
+        front_kernel,
+        ((lines * half, 2 * kept), (parts, 1, lanes)),
+        (place, *blocks, sums, *forward),
+        (slim_buffer,),
+        flops=10**8,
+    )
+    (block_out,) = call(
+        back_kernel, ((parts, *slim),), (scaled, tab["twist"], *inverse), flops=10**9
+    )
+    block_out, known = lax.optimization_barrier((block_out, known + row_swap(known, 1)))
+    blocks = exchange([block_out])
+    known = known + row_swap(known, 2) + row_swap(known, 4) + row_swap(known, 6)
+    known = known + row_swap(known, 8) + row_swap(known, 16) + row_swap(known, 24)
+    sums = exchange([known])[0]
     (second,) = call(
         second_kernel,
         (block,),

time: 126 us -> 125 us (level)
  starting transfers between devices: 74.3 us -> 72.9 us
    all_to_all x2, waiting for transfers between devices: 6.8 us -> 8.81 us  [exchange(): lax.all_to_all(blocks[0], 'cols', split_axis=0, concat_axis=0, tiled=True)]
    all_to_all x2, starting transfers between devices: 11.1 us -> 9.26 us  [exchange(): lax.all_to_all(blocks[0], 'cols', split_axis=0, concat_axis=0, tiled=True)]
  transfers between devices with their start and end apart: 34 -> 34, of which waited for: 17 -> 17; matrix products, arithmetic and copies ran while one was open for 0% -> 1% of each run, Pallas kernels for 4% -> 5%
where the time goes in v4:
time: 125 us
  starting transfers between devices  72.9 us (58%)
  waiting for transfers between devices  35.5 us (28%)
  Pallas kernels  13.5 us (11%)
  other arithmetic  1.58 us (1%)
    ppermute x21, starting transfers between devices, exchange(): lax.ppermute(blocks[mask], 'cols', [(i, i ^ mask) for i in range(count)])  46.4 us
    ppermute x21, waiting for transfers between devices, exchange(): lax.ppermute(blocks[mask], 'cols', [(i, i ^ mask) for i in range(count)])  17.6 us
    pallas_call x11, Pallas kernels, call(): pl.pallas_call(kernel, out_shape=outs, in_specs=in_specs, out_specs=tuple...  13.5 us
    all_to_all x2, starting transfers between devices, exchange(): lax.all_to_all(blocks[0], 'cols', split_axis=0, concat_axis=0, tiled=True)  9.26 us
    all_to_all x2, waiting for transfers between devices, exchange(): lax.all_to_all(blocks[0], 'cols', split_axis=0, concat_axis=0, tiled=True)  8.81 us
    ppermute x7, starting transfers between devices, row_swap(): return lax.ppermute(value, 'rows', [(i, i ^ mask) for i in range(count)])  8.66 us
    ppermute x2, starting transfers between devices, swap_rows(): lax.ppermute(send_b, 'rows', outer)  8.39 us
    ppermute x7, waiting for transfers between devices, row_swap(): return lax.ppermute(value, 'rows', [(i, i ^ mask) for i in range(count)])  7.01 us
  transfers between devices with their start and end apart: 34, of which 17 were waited for; matrix products, arithmetic and copies ran while one was open for 1% of the time, Pallas kernels for 5%

profile of v4, /device:TPU:8, one launch (start us, length us, event | category | flops | bytes accessed | tf_op | source)
XLA Modules:
  0.0 124.6 jit_solution(17354362003253999538)
XLA Ops:
  0.6 0.0 copy-start.10
  0.7 0.9 broadcast_select_fusion
  1.5 4.0 %collective-permute-start.1 = (f32[2,2048]{1,0:T(2,128)S(1)}, f32[2,2048]{1,0:T(2,128)S(1)}, u32[]{:S(2)}, u32[]{:S(2)}) collective-permute-start(f32[2,2048]{1,0:T(2,128)S(1)} %get-tuple-element.85), channel_id=1, source_target_pairs={{8,16},{24,32},{40,48},{56,64},{72,80},{88,96},{104,112},{120,128}... | collective-permute-start | bytes 49160 | tf_op jit(solution)/shard_map/ppermute | solution.py:511
  5.5 0.1 collective-permute-start
  5.7 0.1 pad_add_fusion.place
  5.7 2.6 %shard_map.157 = (f32[64,2176]{1,0:T(8,128)S(1)}, f32[64,2048]{1,0:T(8,128)S(1)}, f32[64,2048]{1,0:T(8,128)S(1)}) custom-call(f32[64,2048]{1,0:T(8,128)} %latent.1, s32[64,2048]{1,0:T(8,128)} %counts.1, s32[64,2048]{1,0:T(8,128)} %exposure.1, bf16[64,192]{1,0:T(8,128)(2,1)S(1)} %copy-done.10), custom_call_target="tpu_custom_call" | custom-call | flops 1000000000 | bytes 3227648 | tf_op jit(solution)/shard_map/pallas_call | solution.py:479
  8.3 0.4 collective-permute-done.1.swap_b
  8.7 0.0 copy-start.2
  8.8 1.0 shard_map.158
  9.8 2.0 %collective-permute-start.2 = (f32[136,128]{1,0:T(8,128)S(1)}, f32[136,128]{1,0:T(8,128)S(1)}, u32[]{:S(2)}, u32[]{:S(2)}) collective-permute-start(f32[136,128]{1,0:T(8,128)S(1)} %get-tuple-element.46), channel_id=1, source_target_pairs={{0,1},{1,0},{2,3},{3,2},{4,5},{5,4},{6,7},{7,6},{8,9},{9,8},{10,11... | collective-permute-start | bytes 208904 | tf_op jit(solution)/shard_map/ppermute | solution.py:505
  11.8 3.3 %collective-permute-start.3 = (f32[136,128]{1,0:T(8,128)S(1)}, f32[136,128]{1,0:T(8,128)S(1)}, u32[]{:S(2)}, u32[]{:S(2)}) collective-permute-start(f32[136,128]{1,0:T(8,128)S(1)} %get-tuple-element.47), channel_id=1, source_target_pairs={{0,2},{1,3},{2,0},{3,1},{4,6},{5,7},{6,4},{7,5},{8,10},{9,11},{10,... | collective-permute-start | bytes 208904 | tf_op jit(solution)/shard_map/ppermute | solution.py:505
  15.1 6.4 %collective-permute-start.5 = (f32[136,128]{1,0:T(8,128)S(1)}, f32[136,128]{1,0:T(8,128)S(1)}, u32[]{:S(2)}, u32[]{:S(2)}) collective-permute-start(f32[136,128]{1,0:T(8,128)S(1)} %get-tuple-element.49), channel_id=1, source_target_pairs={{0,4},{1,5},{2,6},{3,7},{4,0},{5,1},{6,2},{7,3},{8,12},{9,13},{10,... | collective-permute-start | bytes 208904 | tf_op jit(solution)/shard_map/ppermute | solution.py:505
  21.5 4.6 %collective-permute-start.7 = (f32[136,128]{1,0:T(8,128)S(1)}, f32[136,128]{1,0:T(8,128)S(1)}, u32[]{:S(2)}, u32[]{:S(2)}) collective-permute-start(f32[136,128]{1,0:T(8,128)S(1)} %get-tuple-element.51), channel_id=1, source_target_pairs={{0,6},{1,7},{2,4},{3,5},{4,2},{5,3},{6,0},{7,1},{8,14},{9,15},{10,... | collective-permute-start | bytes 208904 | tf_op jit(solution)/shard_map/ppermute | solution.py:505
  26.1 2.8 %collective-permute-start.8 = (f32[136,128]{1,0:T(8,128)S(1)}, f32[136,128]{1,0:T(8,128)S(1)}, u32[]{:S(2)}, u32[]{:S(2)}) collective-permute-start(f32[136,128]{1,0:T(8,128)S(1)} %get-tuple-element.52), channel_id=1, source_target_pairs={{0,7},{1,6},{2,5},{3,4},{4,3},{5,2},{6,1},{7,0},{8,15},{9,14},{10,... | collective-permute-start | bytes 208904 | tf_op jit(solution)/shard_map/ppermute | solution.py:505
  28.9 1.8 %collective-permute-done.6.rest_5_ = f32[136,128]{1,0:T(8,128)S(1)} collective-permute-done((f32[136,128]{1,0:T(8,128)S(1)}, f32[136,128]{1,0:T(8,128)S(1)}, u32[]{:S(2)}, u32[]{:S(2)}) %collective-permute-start.6) | collective-permute-done | bytes 69664 | tf_op jit(solution)/shard_map/ppermute | solution.py:505
  30.6 1.2 collective-permute-done.7.rest_6_
  31.8 2.5 %collective-permute-done.8.rest_7_ = f32[136,128]{1,0:T(8,128)S(1)} collective-permute-done((f32[136,128]{1,0:T(8,128)S(1)}, f32[136,128]{1,0:T(8,128)S(1)}, u32[]{:S(2)}, u32[]{:S(2)}) %collective-permute-start.8) | collective-permute-done | bytes 69664 | tf_op jit(solution)/shard_map/ppermute | solution.py:505
  34.4 1.7 %shard_map.159 = (f32[136,128]{1,0:T(8,128)S(1)}, f32[136,128]{1,0:T(8,128)S(1)}, f32[136,128]{1,0:T(8,128)S(1)}, f32[136,128]{1,0:T(8,128)S(1)}, f32[136,128]{1...) custom-call(s32[2]{0:T(128)S(1)} %pad_add_fusion.place, ...), custom_call_target="tpu_custom_call" | custom-call | flops 1000000000 | bytes 2392072 | tf_op jit(solution)/shard_map/pallas_call | solution.py:479
  36.1 0.3 collective-permute-start.9
  36.5 1.9 %collective-permute-start.10 = (f32[136,128]{1,0:T(8,128)S(1)}, f32[136,128]{1,0:T(8,128)S(1)}, u32[]{:S(2)}, u32[]{:S(2)}) collective-permute-start(f32[136,128]{1,0:T(8,128)S(1)} %get-tuple-element.55), channel_id=1, source_target_pairs={{0,2},{1,3},{2,0},{3,1},{4,6},{5,7},{6,4},{7,5},{8,10},{9,11},{10,... | collective-permute-start | bytes 208904 | tf_op jit(solution)/shard_map/ppermute | solution.py:505
  38.3 2.3 %collective-permute-start.11 = (f32[136,128]{1,0:T(8,128)S(1)}, f32[136,128]{1,0:T(8,128)S(1)}, u32[]{:S(2)}, u32[]{:S(2)}) collective-permute-start(f32[136,128]{1,0:T(8,128)S(1)} %get-tuple-element.56), channel_id=1, source_target_pairs={{0,3},{1,2},{2,1},{3,0},{4,7},{5,6},{6,5},{7,4},{8,11},{9,10},{10,... | collective-permute-start | bytes 208904 | tf_op jit(solution)/shard_map/ppermute | solution.py:505
  40.6 3.2 %collective-permute-start.12 = (f32[136,128]{1,0:T(8,128)S(1)}, f32[136,128]{1,0:T(8,128)S(1)}, u32[]{:S(2)}, u32[]{:S(2)}) collective-permute-start(f32[136,128]{1,0:T(8,128)S(1)} %get-tuple-element.57), channel_id=1, source_target_pairs={{0,4},{1,5},{2,6},{3,7},{4,0},{5,1},{6,2},{7,3},{8,12},{9,13},{10,... | collective-permute-start | bytes 208904 | tf_op jit(solution)/shard_map/ppermute | solution.py:505
  43.8 0.7 collective-permute-start.13
  44.4 4.0 %collective-permute-start.14 = (f32[136,128]{1,0:T(8,128)S(1)}, f32[136,128]{1,0:T(8,128)S(1)}, u32[]{:S(2)}, u32[]{:S(2)}) collective-permute-start(f32[136,128]{1,0:T(8,128)S(1)} %get-tuple-element.59), channel_id=1, source_target_pairs={{0,6},{1,7},{2,4},{3,5},{4,2},{5,3},{6,0},{7,1},{8,14},{9,15},{10,... | collective-permute-start | bytes 208904 | tf_op jit(solution)/shard_map/ppermute | solution.py:505
  48.5 1.3 %collective-permute-start.15 = (f32[136,128]{1,0:T(8,128)S(1)}, f32[136,128]{1,0:T(8,128)S(1)}, u32[]{:S(2)}, u32[]{:S(2)}) collective-permute-start(f32[136,128]{1,0:T(8,128)S(1)} %get-tuple-element.60), channel_id=1, source_target_pairs={{0,7},{1,6},{2,5},{3,4},{4,3},{5,2},{6,1},{7,0},{8,15},{9,14},{10,... | collective-permute-start | bytes 208904 | tf_op jit(solution)/shard_map/ppermute | solution.py:505
  49.8 0.1 collective-permute-done.12.rest_4_
  49.9 2.2 %collective-permute-done.13.rest_5_ = f32[136,128]{1,0:T(8,128)S(1)} collective-permute-done((f32[136,128]{1,0:T(8,128)S(1)}, f32[136,128]{1,0:T(8,128)S(1)}, u32[]{:S(2)}, u32[]{:S(2)}) %collective-permute-start.13) | collective-permute-done | bytes 69664 | tf_op jit(solution)/shard_map/ppermute | solution.py:505
  52.1 1.5 %collective-permute-done.14.rest_6_ = f32[136,128]{1,0:T(8,128)S(1)} collective-permute-done((f32[136,128]{1,0:T(8,128)S(1)}, f32[136,128]{1,0:T(8,128)S(1)}, u32[]{:S(2)}, u32[]{:S(2)}) %collective-permute-start.14) | collective-permute-done | bytes 69664 | tf_op jit(solution)/shard_map/ppermute | solution.py:505
  53.6 3.1 %collective-permute-done.15.rest_7_ = f32[136,128]{1,0:T(8,128)S(1)} collective-permute-done((f32[136,128]{1,0:T(8,128)S(1)}, f32[136,128]{1,0:T(8,128)S(1)}, u32[]{:S(2)}, u32[]{:S(2)}) %collective-permute-start.15) | collective-permute-done | bytes 69664 | tf_op jit(solution)/shard_map/ppermute | solution.py:505
  56.8 0.9 shard_map.160
  57.7 0.1 collective-permute-start.16
  57.8 4.4 %collective-permute-start.17 = (f32[2,2176]{1,0:T(2,128)S(1)}, f32[2,2176]{1,0:T(2,128)S(1)}, u32[]{:S(2)}, u32[]{:S(2)}) collective-permute-start(f32[2,2176]{1,0:T(2,128)S(1)} %get-tuple-element.67), channel_id=1, source_target_pairs={{8,16},{24,32},{40,48},{56,64},{72,80},{88,96},{104,112},{120,128}... | collective-permute-start | bytes 52232 | tf_op jit(solution)/shard_map/ppermute | solution.py:511
  62.2 1.1 shard_map.161
  63.4 1.7 %collective-permute-done.17.swap_b = f32[2,2176]{1,0:T(2,128)S(1)} collective-permute-done((f32[2,2176]{1,0:T(2,128)S(1)}, f32[2,2176]{1,0:T(2,128)S(1)}, u32[]{:S(2)}, u32[]{:S(2)}) %collective-permute-start.17) | collective-permute-done | bytes 17440 | tf_op jit(solution)/shard_map/ppermute | solution.py:511
  65.0 0.9 shard_map.162
  65.9 0.8 collective-permute-start.18
  66.7 1.3 %collective-permute-start.19 = (f32[128,128]{1,0:T(8,128)S(1)}, f32[128,128]{1,0:T(8,128)S(1)}, u32[]{:S(2)}, u32[]{:S(2)}) collective-permute-start(f32[128,128]{1,0:T(8,128)S(1)} %get-tuple-element.70), channel_id=1, source_target_pairs={{0,2},{1,3},{2,0},{3,1},{4,6},{5,7},{6,4},{7,5},{8,10},{9,11},{10,... | collective-permute-start | bytes 196616 | tf_op jit(solution)/shard_map/ppermute | solution.py:505
  68.0 2.4 %collective-permute-start.20 = (f32[128,128]{1,0:T(8,128)S(1)}, f32[128,128]{1,0:T(8,128)S(1)}, u32[]{:S(2)}, u32[]{:S(2)}) collective-permute-start(f32[128,128]{1,0:T(8,128)S(1)} %get-tuple-element.71), channel_id=1, source_target_pairs={{0,3},{1,2},{2,1},{3,0},{4,7},{5,6},{6,5},{7,4},{8,11},{9,10},{10,... | collective-permute-start | bytes 196616 | tf_op jit(solution)/shard_map/ppermute | solution.py:505
  70.4 2.7 %collective-permute-start.21 = (f32[128,128]{1,0:T(8,128)S(1)}, f32[128,128]{1,0:T(8,128)S(1)}, u32[]{:S(2)}, u32[]{:S(2)}) collective-permute-start(f32[128,128]{1,0:T(8,128)S(1)} %get-tuple-element.72), channel_id=1, source_target_pairs={{0,4},{1,5},{2,6},{3,7},{4,0},{5,1},{6,2},{7,3},{8,12},{9,13},{10,... | collective-permute-start | bytes 196616 | tf_op jit(solution)/shard_map/ppermute | solution.py:505
  73.0 1.6 %collective-permute-start.22 = (f32[128,128]{1,0:T(8,128)S(1)}, f32[128,128]{1,0:T(8,128)S(1)}, u32[]{:S(2)}, u32[]{:S(2)}) collective-permute-start(f32[128,128]{1,0:T(8,128)S(1)} %get-tuple-element.73), channel_id=1, source_target_pairs={{0,5},{1,4},{2,7},{3,6},{4,1},{5,0},{6,3},{7,2},{8,13},{9,12},{10,... | collective-permute-start | bytes 196616 | tf_op jit(solution)/shard_map/ppermute | solution.py:505
  74.6 3.2 %collective-permute-start.23 = (f32[128,128]{1,0:T(8,128)S(1)}, f32[128,128]{1,0:T(8,128)S(1)}, u32[]{:S(2)}, u32[]{:S(2)}) collective-permute-start(f32[128,128]{1,0:T(8,128)S(1)} %get-tuple-element.74), channel_id=1, source_target_pairs={{0,6},{1,7},{2,4},{3,5},{4,2},{5,3},{6,0},{7,1},{8,14},{9,15},{10,... | collective-permute-start | bytes 196616 | tf_op jit(solution)/shard_map/ppermute | solution.py:505
  77.8 1.8 %collective-permute-start.24 = (f32[128,128]{1,0:T(8,128)S(1)}, f32[128,128]{1,0:T(8,128)S(1)}, u32[]{:S(2)}, u32[]{:S(2)}) collective-permute-start(f32[128,128]{1,0:T(8,128)S(1)} %get-tuple-element.75), channel_id=1, source_target_pairs={{0,7},{1,6},{2,5},{3,4},{4,3},{5,2},{6,1},{7,0},{8,15},{9,14},{10,... | collective-permute-start | bytes 196616 | tf_op jit(solution)/shard_map/ppermute | solution.py:505
  79.6 0.3 shard_map.163
  79.9 0.5 collective-permute-done.22.rest_5_
  80.4 1.6 %collective-permute-done.23.rest_6_ = f32[128,128]{1,0:T(8,128)S(1)} collective-permute-done((f32[128,128]{1,0:T(8,128)S(1)}, f32[128,128]{1,0:T(8,128)S(1)}, u32[]{:S(2)}, u32[]{:S(2)}) %collective-permute-start.23) | collective-permute-done | bytes 65568 | tf_op jit(solution)/shard_map/ppermute | solution.py:505
  82.1 3.0 %collective-permute-done.24.rest_7_ = f32[128,128]{1,0:T(8,128)S(1)} collective-permute-done((f32[128,128]{1,0:T(8,128)S(1)}, f32[128,128]{1,0:T(8,128)S(1)}, u32[]{:S(2)}, u32[]{:S(2)}) %collective-permute-start.24) | collective-permute-done | bytes 65568 | tf_op jit(solution)/shard_map/ppermute | solution.py:505
  85.1 1.3 %shard_map.164 = (f32[576,128]{1,0:T(8,128)S(1)}, f32[8,1,128]{2,1,0:T(1,128)S(1)}) custom-call(s32[2]{0:T(128)S(1)} %pad_add_fusion.place, f32[128,128]{1,0:T(8,128)S(1)} %get-tuple-element.68.rest_0_, f32[128,128]{1,0:T(8,128)S(1)} %collective-permute-done.18.rest_1_, f32[128,128]{1,0:T(8,128)S(1)} %collective-permute-done.19.rest_2_, ...), custom_call_target="tpu_custom_call" | custom-call | flops 100000000 | bytes 1487368 | tf_op jit(solution)/shard_map/pallas_call | solution.py:479
  86.4 0.1 collective-permute-start.25
  86.5 1.5 %shard_map.165 = f32[8,128,128]{2,1,0:T(8,128)} custom-call(f32[576,128]{1,0:T(8,128)S(1)} %get-tuple-element.80.scaled, f32[2,72,128]{2,1,0:T(8,128)S(1)} %copy-done.3, bf16[128,432]{1,0:T(8,128)(2,1)S(1)} %copy-done.9, bf16[384,256]{1,0:T(8,128)(2,1)S(1)} %copy-done.8), custom_call_target="tpu_custom_call" | custom-call | flops 1000000000 | bytes 1507328 | tf_op jit(solution)/shard_map/pallas_call | solution.py:479
  88.0 4.1 %all-to-all-start.1 = ((f32[8,128,128]{2,1,0:T(8,128)}), f32[8,128,128]{2,1,0:T(8,128)S(1)}, u32[]{:S(2)}, u32[]{:S(2)}) async-start(f32[8,128,128]{2,1,0:T(8,128)} %shard_map.165), calls=%async_computation.1 | async-start | bytes 1048576 | tf_op jit(solution)/shard_map/all_to_all | solution.py:501
  92.1 3.4 %collective-permute-start.28 = (f32[8,1,128]{2,1,0:T(1,128)S(1)}, f32[8,1,128]{2,1,0:T(1,128)S(1)}, u32[]{:S(2)}, u32[]{:S(2)}) collective-permute-start(f32[8,1,128]{2,1,0:T(1,128)S(1)} %add.26), channel_id=1, source_target_pairs={{0,48},{8,56},{16,32},{24,40},{32,16},{40,24},{48,0},{56,8},{64,11... | collective-permute-start | bytes 12296 | tf_op jit(solution)/shard_map/ppermute | solution.py:516
  95.5 0.9 collective-permute-start.26
  96.5 0.6 collective-permute-done.28
  97.1 3.5 %collective-permute-done.27 = f32[8,1,128]{2,1,0:T(1,128)S(1)} collective-permute-done((f32[8,1,128]{2,1,0:T(1,128)S(1)}, f32[8,1,128]{2,1,0:T(1,128)S(1)}, u32[]{:S(2)}, u32[]{:S(2)}) %collective-permute-start.27) | collective-permute-done | bytes 4128 | tf_op jit(solution)/shard_map/ppermute | solution.py:516
  100.6 1.9 %collective-permute-start.31 = (f32[8,1,128]{2,1,0:T(1,128)S(1)}, f32[8,1,128]{2,1,0:T(1,128)S(1)}, u32[]{:S(2)}, u32[]{:S(2)}) collective-permute-start(f32[8,1,128]{2,1,0:T(1,128)S(1)} %bitcast.13), channel_id=1, source_target_pairs={{0,192},{8,200},{16,208},{24,216},{32,224},{40,232},{48,240},{56,2... | collective-permute-start | bytes 12296 | tf_op jit(solution)/shard_map/ppermute | solution.py:516
  102.5 0.7 collective-permute-start.30
  103.2 1.6 %collective-permute-start.29 = (f32[8,1,128]{2,1,0:T(1,128)S(1)}, f32[8,1,128]{2,1,0:T(1,128)S(1)}, u32[]{:S(2)}, u32[]{:S(2)}) collective-permute-start(f32[8,1,128]{2,1,0:T(1,128)S(1)} %bitcast.15), channel_id=1, source_target_pairs={{0,64},{8,72},{16,80},{24,88},{32,96},{40,104},{48,112},{56,120},{... | collective-permute-start | bytes 12296 | tf_op jit(solution)/shard_map/ppermute | solution.py:516
  104.8 2.8 %collective-permute-done.30 = f32[8,1,128]{2,1,0:T(1,128)S(1)} collective-permute-done((f32[8,1,128]{2,1,0:T(1,128)S(1)}, f32[8,1,128]{2,1,0:T(1,128)S(1)}, u32[]{:S(2)}, u32[]{:S(2)}) %collective-permute-start.30) | collective-permute-done | bytes 4128 | tf_op jit(solution)/shard_map/ppermute | solution.py:516
  107.7 0.6 add_add_fusion
  108.3 2.0 %all-to-all-done.1.rest_0_ = f32[8,128,128]{2,1,0:T(8,128)S(1)} async-done(((f32[8,128,128]{2,1,0:T(8,128)}), f32[8,128,128]{2,1,0:T(8,128)S(1)}, u32[]{:S(2)}, u32[]{:S(2)}) %all-to-all-start.1) | async-done | bytes 524320 | tf_op jit(solution)/shard_map/all_to_all | solution.py:501
  110.3 5.2 %all-to-all-start = ((f32[8,1,128]{2,1,0:T(1,128)}), f32[8,1,128]{2,1,0:T(1,128)S(1)}, u32[]{:S(2)}, u32[]{:S(2)}) async-start(f32[8,1,128]{2,1,0:T(1,128)} %bitcast.11), calls=%async_computation | async-start | bytes 8192 | tf_op jit(solution)/shard_map/all_to_all | solution.py:501
  115.5 0.8 shard_map.166.second
  116.3 6.8 %all-to-all-done.sums = f32[8,1,128]{2,1,0:T(1,128)S(1)} async-done(((f32[8,1,128]{2,1,0:T(1,128)}), f32[8,1,128]{2,1,0:T(1,128)S(1)}, u32[]{:S(2)}, u32[]{:S(2)}) %all-to-all-start) | async-done | bytes 4128 | tf_op jit(solution)/shard_map/all_to_all | solution.py:501
  123.1 1.4 %shard_map.167 = (f32[64,2048]{1,0:T(8,128)}, f32[64,2048]{1,0:T(8,128)}, f32[64,2048]{1,0:T(8,128)}) custom-call(f32[8,1,128]{2,1,0:T(1,128)S(1)} %all-to-all-done.sums, f32[64,2176]{1,0:T(8,128)S(1)} %get-tuple-element.63.search, f32[64,2048]{1,0:T(8,128)S(1)} %get-tuple-element.76.grad, f32[64,2048]{1,0:T(8,128)S(1)} %get-tuple-element.83.rest_1_.image, ...), custom_call_target="tpu_custom_call" | custom-call | flops 1000000 | bytes 3706880 | tf_op jit(solution)/shard_map/pallas_call | solution.py:479
  (42 shorter events, 0.1 us)
Async XLA Ops:
  0.6 5.1 %copy-start.10 = (bf16[64,192]{1,0:T(8,128)(2,1)S(1)}, bf16[64,192]{1,0:T(8,128)(2,1)}, u32[]{:S(2)}) copy-start(bf16[64,192]{1,0:T(8,128)(2,1)} %constant.45.clone.basis) | copy-start | bytes 73732
  1.5 7.2 %collective-permute-start.1 = (f32[2,2048]{1,0:T(2,128)S(1)}, f32[2,2048]{1,0:T(2,128)S(1)}, u32[]{:S(2)}, u32[]{:S(2)}) collective-permute-start(f32[2,2048]{1,0:T(2,128)S(1)} %get-tuple-element.85), channel_id=1, source_target_pairs={{8,16},{24,32},{40,48},{56,64},{72,80},{88,96},{104,112},{120,128}... | collective-permute-start | bytes 49160 | tf_op jit(solution)/shard_map/ppermute | solution.py:511
  5.5 3.2 %collective-permute-start = (f32[2,2048]{1,0:T(2,128)S(1)}, f32[2,2048]{1,0:T(2,128)S(1)}, u32[]{:S(2)}, u32[]{:S(2)}) collective-permute-start(f32[2,2048]{1,0:T(2,128)S(1)} %get-tuple-element.86), channel_id=1, source_target_pairs={{0,8},{8,0},{16,24},{24,16},{32,40},{40,32},{48,56},{56,48},{64,72... | collective-permute-start | bytes 49160 | tf_op jit(solution)/shard_map/ppermute | solution.py:511
  5.7 3.0 %copy-start.4 = (bf16[64,48]{1,0:T(8,128)(2,1)S(1)}, bf16[64,48]{1,0:T(8,128)(2,1)}, u32[]{:S(2)}) copy-start(bf16[64,48]{1,0:T(8,128)(2,1)} %constant.46.clone.basis) | copy-start | bytes 18436
  5.7 28.6 %copy-start.9 = (bf16[128,432]{1,0:T(8,128)(2,1)S(1)}, bf16[128,432]{1,0:T(8,128)(2,1)}, u32[]{:S(2)}) copy-start(bf16[128,432]{1,0:T(8,128)(2,1)} %constant.50.clone.rest_14_.outer_inverse) | copy-start | bytes 331780
  8.7 25.6 %copy-start.1 = (bf16[256,256]{1,0:T(8,128)(2,1)S(1)}, bf16[256,256]{1,0:T(8,128)(2,1)}, u32[]{:S(2)}) copy-start(bf16[256,256]{1,0:T(8,128)(2,1)} %constant.52.clone.rest_12_.rest_13_) | copy-start | bytes 393220
  8.7 25.6 %copy-start.2 = (bf16[144,384]{1,0:T(8,128)(2,1)S(1)}, bf16[144,384]{1,0:T(8,128)(2,1)}, u32[]{:S(2)}) copy-start(bf16[144,384]{1,0:T(8,128)(2,1)} %constant.49.clone.rest_11_.rest_12_) | copy-start | bytes 331780
  8.7 25.6 %copy-start.3 = (f32[2,72,128]{2,1,0:T(8,128)S(1)}, f32[2,72,128]{2,1,0:T(8,128)}, u32[]{:S(2)}) copy-start(f32[2,72,128]{2,1,0:T(8,128)} %constant.51.clone.rest_13_.rest_14_.twist) | copy-start | bytes 221188
  8.8 25.6 %copy-start.5 = (f32[72,128]{1,0:T(8,128)S(1)}, f32[72,128]{1,0:T(8,128)}, u32[]{:S(2)}) copy-start(f32[72,128]{1,0:T(8,128)} %constant.55.clone.rest_9_.rest_10_) | copy-start | bytes 110596
  8.8 25.6 %copy-start.6 = (f32[72,128]{1,0:T(8,128)S(1)}, f32[72,128]{1,0:T(8,128)}, u32[]{:S(2)}) copy-start(f32[72,128]{1,0:T(8,128)} %constant.54.clone.rest_10_.rest_11_) | copy-start | bytes 110596
  8.8 25.6 %copy-start.7 = (f32[64,128]{1,0:T(8,128)S(1)}, f32[64,128]{1,0:T(8,128)}, u32[]{:S(2)}) copy-start(f32[64,128]{1,0:T(8,128)} %constant.48.clone.rest_8_.rest_9_) | copy-start | bytes 98308
  8.8 25.6 %copy-start.8 = (bf16[384,256]{1,0:T(8,128)(2,1)S(1)}, bf16[384,256]{1,0:T(8,128)(2,1)}, u32[]{:S(2)}) copy-start(bf16[384,256]{1,0:T(8,128)(2,1)} %constant.53.clone.rest_15_.inner_inverse) | copy-start | bytes 589828
  9.8 11.7 %collective-permute-start.2 = (f32[136,128]{1,0:T(8,128)S(1)}, f32[136,128]{1,0:T(8,128)S(1)}, u32[]{:S(2)}, u32[]{:S(2)}) collective-permute-start(f32[136,128]{1,0:T(8,128)S(1)} %get-tuple-element.46), channel_id=1, source_target_pairs={{0,1},{1,0},{2,3},{3,2},{4,5},{5,4},{6,7},{7,6},{8,9},{9,8},{10,11... | collective-permute-start | bytes 208904 | tf_op jit(solution)/shard_map/ppermute | solution.py:505
  11.8 14.3 %collective-permute-start.3 = (f32[136,128]{1,0:T(8,128)S(1)}, f32[136,128]{1,0:T(8,128)S(1)}, u32[]{:S(2)}, u32[]{:S(2)}) collective-permute-start(f32[136,128]{1,0:T(8,128)S(1)} %get-tuple-element.47), channel_id=1, source_target_pairs={{0,2},{1,3},{2,0},{3,1},{4,6},{5,7},{6,4},{7,5},{8,10},{9,11},{10,... | collective-permute-start | bytes 208904 | tf_op jit(solution)/shard_map/ppermute | solution.py:505
  15.1 13.8 %collective-permute-start.4 = (f32[136,128]{1,0:T(8,128)S(1)}, f32[136,128]{1,0:T(8,128)S(1)}, u32[]{:S(2)}, u32[]{:S(2)}) collective-permute-start(f32[136,128]{1,0:T(8,128)S(1)} %get-tuple-element.48), channel_id=1, source_target_pairs={{0,3},{1,2},{2,1},{3,0},{4,7},{5,6},{6,5},{7,4},{8,11},{9,10},{10,... | collective-permute-start | bytes 208904 | tf_op jit(solution)/shard_map/ppermute | solution.py:505
  15.1 13.8 %collective-permute-start.5 = (f32[136,128]{1,0:T(8,128)S(1)}, f32[136,128]{1,0:T(8,128)S(1)}, u32[]{:S(2)}, u32[]{:S(2)}) collective-permute-start(f32[136,128]{1,0:T(8,128)S(1)} %get-tuple-element.49), channel_id=1, source_target_pairs={{0,4},{1,5},{2,6},{3,7},{4,0},{5,1},{6,2},{7,3},{8,12},{9,13},{10,... | collective-permute-start | bytes 208904 | tf_op jit(solution)/shard_map/ppermute | solution.py:505
  21.4 9.2 %collective-permute-start.6 = (f32[136,128]{1,0:T(8,128)S(1)}, f32[136,128]{1,0:T(8,128)S(1)}, u32[]{:S(2)}, u32[]{:S(2)}) collective-permute-start(f32[136,128]{1,0:T(8,128)S(1)} %get-tuple-element.50), channel_id=1, source_target_pairs={{0,5},{1,4},{2,7},{3,6},{4,1},{5,0},{6,3},{7,2},{8,13},{9,12},{10,... | collective-permute-start | bytes 208904 | tf_op jit(solution)/shard_map/ppermute | solution.py:505
  21.5 10.3 %collective-permute-start.7 = (f32[136,128]{1,0:T(8,128)S(1)}, f32[136,128]{1,0:T(8,128)S(1)}, u32[]{:S(2)}, u32[]{:S(2)}) collective-permute-start(f32[136,128]{1,0:T(8,128)S(1)} %get-tuple-element.51), channel_id=1, source_target_pairs={{0,6},{1,7},{2,4},{3,5},{4,2},{5,3},{6,0},{7,1},{8,14},{9,15},{10,... | collective-permute-start | bytes 208904 | tf_op jit(solution)/shard_map/ppermute | solution.py:505
  26.1 8.2 %collective-permute-start.8 = (f32[136,128]{1,0:T(8,128)S(1)}, f32[136,128]{1,0:T(8,128)S(1)}, u32[]{:S(2)}, u32[]{:S(2)}) collective-permute-start(f32[136,128]{1,0:T(8,128)S(1)} %get-tuple-element.52), channel_id=1, source_target_pairs={{0,7},{1,6},{2,5},{3,4},{4,3},{5,2},{6,1},{7,0},{8,15},{9,14},{10,... | collective-permute-start | bytes 208904 | tf_op jit(solution)/shard_map/ppermute | solution.py:505
  34.4 22.4 %copy-start = (bf16[64,192]{1,0:T(8,128)(2,1)S(1)}, bf16[64,192]{1,0:T(8,128)(2,1)}, u32[]{:S(2)}) copy-start(bf16[64,192]{1,0:T(8,128)(2,1)} %constant.47.clone.rest_10_.rest_2_) | copy-start | bytes 73732
  36.1 8.3 %collective-permute-start.9 = (f32[136,128]{1,0:T(8,128)S(1)}, f32[136,128]{1,0:T(8,128)S(1)}, u32[]{:S(2)}, u32[]{:S(2)}) collective-permute-start(f32[136,128]{1,0:T(8,128)S(1)} %get-tuple-element.54), channel_id=1, source_target_pairs={{0,1},{1,0},{2,3},{3,2},{4,5},{5,4},{6,7},{7,6},{8,9},{9,8},{10,11... | collective-permute-start | bytes 208904 | tf_op jit(solution)/shard_map/ppermute | solution.py:505
  36.5 12.0 %collective-permute-start.10 = (f32[136,128]{1,0:T(8,128)S(1)}, f32[136,128]{1,0:T(8,128)S(1)}, u32[]{:S(2)}, u32[]{:S(2)}) collective-permute-start(f32[136,128]{1,0:T(8,128)S(1)} %get-tuple-element.55), channel_id=1, source_target_pairs={{0,2},{1,3},{2,0},{3,1},{4,6},{5,7},{6,4},{7,5},{8,10},{9,11},{10,... | collective-permute-start | bytes 208904 | tf_op jit(solution)/shard_map/ppermute | solution.py:505
  38.3 11.5 %collective-permute-start.11 = (f32[136,128]{1,0:T(8,128)S(1)}, f32[136,128]{1,0:T(8,128)S(1)}, u32[]{:S(2)}, u32[]{:S(2)}) collective-permute-start(f32[136,128]{1,0:T(8,128)S(1)} %get-tuple-element.56), channel_id=1, source_target_pairs={{0,3},{1,2},{2,1},{3,0},{4,7},{5,6},{6,5},{7,4},{8,11},{9,10},{10,... | collective-permute-start | bytes 208904 | tf_op jit(solution)/shard_map/ppermute | solution.py:505
  40.6 9.3 %collective-permute-start.12 = (f32[136,128]{1,0:T(8,128)S(1)}, f32[136,128]{1,0:T(8,128)S(1)}, u32[]{:S(2)}, u32[]{:S(2)}) collective-permute-start(f32[136,128]{1,0:T(8,128)S(1)} %get-tuple-element.57), channel_id=1, source_target_pairs={{0,4},{1,5},{2,6},{3,7},{4,0},{5,1},{6,2},{7,3},{8,12},{9,13},{10,... | collective-permute-start | bytes 208904 | tf_op jit(solution)/shard_map/ppermute | solution.py:505
  43.8 8.3 %collective-permute-start.13 = (f32[136,128]{1,0:T(8,128)S(1)}, f32[136,128]{1,0:T(8,128)S(1)}, u32[]{:S(2)}, u32[]{:S(2)}) collective-permute-start(f32[136,128]{1,0:T(8,128)S(1)} %get-tuple-element.58), channel_id=1, source_target_pairs={{0,5},{1,4},{2,7},{3,6},{4,1},{5,0},{6,3},{7,2},{8,13},{9,12},{10,... | collective-permute-start | bytes 208904 | tf_op jit(solution)/shard_map/ppermute | solution.py:505
  44.4 9.2 %collective-permute-start.14 = (f32[136,128]{1,0:T(8,128)S(1)}, f32[136,128]{1,0:T(8,128)S(1)}, u32[]{:S(2)}, u32[]{:S(2)}) collective-permute-start(f32[136,128]{1,0:T(8,128)S(1)} %get-tuple-element.59), channel_id=1, source_target_pairs={{0,6},{1,7},{2,4},{3,5},{4,2},{5,3},{6,0},{7,1},{8,14},{9,15},{10,... | collective-permute-start | bytes 208904 | tf_op jit(solution)/shard_map/ppermute | solution.py:505
  48.5 8.3 %collective-permute-start.15 = (f32[136,128]{1,0:T(8,128)S(1)}, f32[136,128]{1,0:T(8,128)S(1)}, u32[]{:S(2)}, u32[]{:S(2)}) collective-permute-start(f32[136,128]{1,0:T(8,128)S(1)} %get-tuple-element.60), channel_id=1, source_target_pairs={{0,7},{1,6},{2,5},{3,4},{4,3},{5,2},{6,1},{7,0},{8,15},{9,14},{10,... | collective-permute-start | bytes 208904 | tf_op jit(solution)/shard_map/ppermute | solution.py:505
  57.7 5.6 %collective-permute-start.16 = (f32[2,2176]{1,0:T(2,128)S(1)}, f32[2,2176]{1,0:T(2,128)S(1)}, u32[]{:S(2)}, u32[]{:S(2)}) collective-permute-start(f32[2,2176]{1,0:T(2,128)S(1)} %get-tuple-element.66), channel_id=1, source_target_pairs={{0,8},{8,0},{16,24},{24,16},{32,40},{40,32},{48,56},{56,48},{64,72... | collective-permute-start | bytes 52232 | tf_op jit(solution)/shard_map/ppermute | solution.py:511
  57.8 7.2 %collective-permute-start.17 = (f32[2,2176]{1,0:T(2,128)S(1)}, f32[2,2176]{1,0:T(2,128)S(1)}, u32[]{:S(2)}, u32[]{:S(2)}) collective-permute-start(f32[2,2176]{1,0:T(2,128)S(1)} %get-tuple-element.67), channel_id=1, source_target_pairs={{8,16},{24,32},{40,48},{56,64},{72,80},{88,96},{104,112},{120,128}... | collective-permute-start | bytes 52232 | tf_op jit(solution)/shard_map/ppermute | solution.py:511
  65.9 8.7 %collective-permute-start.18 = (f32[128,128]{1,0:T(8,128)S(1)}, f32[128,128]{1,0:T(8,128)S(1)}, u32[]{:S(2)}, u32[]{:S(2)}) collective-permute-start(f32[128,128]{1,0:T(8,128)S(1)} %get-tuple-element.69), channel_id=1, source_target_pairs={{0,1},{1,0},{2,3},{3,2},{4,5},{5,4},{6,7},{7,6},{8,9},{9,8},{10,11... | collective-permute-start | bytes 196616 | tf_op jit(solution)/shard_map/ppermute | solution.py:505
  66.7 11.1 %collective-permute-start.19 = (f32[128,128]{1,0:T(8,128)S(1)}, f32[128,128]{1,0:T(8,128)S(1)}, u32[]{:S(2)}, u32[]{:S(2)}) collective-permute-start(f32[128,128]{1,0:T(8,128)S(1)} %get-tuple-element.70), channel_id=1, source_target_pairs={{0,2},{1,3},{2,0},{3,1},{4,6},{5,7},{6,4},{7,5},{8,10},{9,11},{10,... | collective-permute-start | bytes 196616 | tf_op jit(solution)/shard_map/ppermute | solution.py:505
  68.0 11.9 %collective-permute-start.20 = (f32[128,128]{1,0:T(8,128)S(1)}, f32[128,128]{1,0:T(8,128)S(1)}, u32[]{:S(2)}, u32[]{:S(2)}) collective-permute-start(f32[128,128]{1,0:T(8,128)S(1)} %get-tuple-element.71), channel_id=1, source_target_pairs={{0,3},{1,2},{2,1},{3,0},{4,7},{5,6},{6,5},{7,4},{8,11},{9,10},{10,... | collective-permute-start | bytes 196616 | tf_op jit(solution)/shard_map/ppermute | solution.py:505
  70.4 9.5 %collective-permute-start.21 = (f32[128,128]{1,0:T(8,128)S(1)}, f32[128,128]{1,0:T(8,128)S(1)}, u32[]{:S(2)}, u32[]{:S(2)}) collective-permute-start(f32[128,128]{1,0:T(8,128)S(1)} %get-tuple-element.72), channel_id=1, source_target_pairs={{0,4},{1,5},{2,6},{3,7},{4,0},{5,1},{6,2},{7,3},{8,12},{9,13},{10,... | collective-permute-start | bytes 196616 | tf_op jit(solution)/shard_map/ppermute | solution.py:505
  73.0 7.4 %collective-permute-start.22 = (f32[128,128]{1,0:T(8,128)S(1)}, f32[128,128]{1,0:T(8,128)S(1)}, u32[]{:S(2)}, u32[]{:S(2)}) collective-permute-start(f32[128,128]{1,0:T(8,128)S(1)} %get-tuple-element.73), channel_id=1, source_target_pairs={{0,5},{1,4},{2,7},{3,6},{4,1},{5,0},{6,3},{7,2},{8,13},{9,12},{10,... | collective-permute-start | bytes 196616 | tf_op jit(solution)/shard_map/ppermute | solution.py:505
  74.6 7.4 %collective-permute-start.23 = (f32[128,128]{1,0:T(8,128)S(1)}, f32[128,128]{1,0:T(8,128)S(1)}, u32[]{:S(2)}, u32[]{:S(2)}) collective-permute-start(f32[128,128]{1,0:T(8,128)S(1)} %get-tuple-element.74), channel_id=1, source_target_pairs={{0,6},{1,7},{2,4},{3,5},{4,2},{5,3},{6,0},{7,1},{8,14},{9,15},{10,... | collective-permute-start | bytes 196616 | tf_op jit(solution)/shard_map/ppermute | solution.py:505
  77.8 7.3 %collective-permute-start.24 = (f32[128,128]{1,0:T(8,128)S(1)}, f32[128,128]{1,0:T(8,128)S(1)}, u32[]{:S(2)}, u32[]{:S(2)}) collective-permute-start(f32[128,128]{1,0:T(8,128)S(1)} %get-tuple-element.75), channel_id=1, source_target_pairs={{0,7},{1,6},{2,5},{3,4},{4,3},{5,2},{6,1},{7,0},{8,15},{9,14},{10,... | collective-permute-start | bytes 196616 | tf_op jit(solution)/shard_map/ppermute | solution.py:505
  86.4 1.6 %collective-permute-start.25 = (f32[8,1,128]{2,1,0:T(1,128)S(1)}, f32[8,1,128]{2,1,0:T(1,128)S(1)}, u32[]{:S(2)}, u32[]{:S(2)}) collective-permute-start(f32[8,1,128]{2,1,0:T(1,128)S(1)} %get-tuple-element.81), channel_id=1, source_target_pairs={{0,8},{8,0},{16,24},{24,16},{32,40},{40,32},{48,56},{56,48},{64,72... | collective-permute-start | bytes 12296 | tf_op jit(solution)/shard_map/ppermute | solution.py:516
  88.0 22.3 %all-to-all-start.1 = ((f32[8,128,128]{2,1,0:T(8,128)}), f32[8,128,128]{2,1,0:T(8,128)S(1)}, u32[]{:S(2)}, u32[]{:S(2)}) async-start(f32[8,128,128]{2,1,0:T(8,128)} %shard_map.165), calls=%async_computation.1 | async-start | bytes 1048576 | tf_op jit(solution)/shard_map/all_to_all | solution.py:501
  92.1 5.0 %collective-permute-start.28 = (f32[8,1,128]{2,1,0:T(1,128)S(1)}, f32[8,1,128]{2,1,0:T(1,128)S(1)}, u32[]{:S(2)}, u32[]{:S(2)}) collective-permute-start(f32[8,1,128]{2,1,0:T(1,128)S(1)} %add.26), channel_id=1, source_target_pairs={{0,48},{8,56},{16,32},{24,40},{32,16},{40,24},{48,0},{56,8},{64,11... | collective-permute-start | bytes 12296 | tf_op jit(solution)/shard_map/ppermute | solution.py:516
  95.5 5.1 %collective-permute-start.27 = (f32[8,1,128]{2,1,0:T(1,128)S(1)}, f32[8,1,128]{2,1,0:T(1,128)S(1)}, u32[]{:S(2)}, u32[]{:S(2)}) collective-permute-start(f32[8,1,128]{2,1,0:T(1,128)S(1)} %add.26), channel_id=1, source_target_pairs={{0,32},{8,40},{16,48},{24,56},{32,0},{40,8},{48,16},{56,24},{64,96... | collective-permute-start | bytes 12296 | tf_op jit(solution)/shard_map/ppermute | solution.py:516
  95.5 5.1 %collective-permute-start.26 = (f32[8,1,128]{2,1,0:T(1,128)S(1)}, f32[8,1,128]{2,1,0:T(1,128)S(1)}, u32[]{:S(2)}, u32[]{:S(2)}) collective-permute-start(f32[8,1,128]{2,1,0:T(1,128)S(1)} %add.26), channel_id=1, source_target_pairs={{0,16},{8,24},{16,0},{24,8},{32,48},{40,56},{48,32},{56,40},{64,80... | collective-permute-start | bytes 12296 | tf_op jit(solution)/shard_map/ppermute | solution.py:516
  100.6 4.2 %collective-permute-start.31 = (f32[8,1,128]{2,1,0:T(1,128)S(1)}, f32[8,1,128]{2,1,0:T(1,128)S(1)}, u32[]{:S(2)}, u32[]{:S(2)}) collective-permute-start(f32[8,1,128]{2,1,0:T(1,128)S(1)} %bitcast.13), channel_id=1, source_target_pairs={{0,192},{8,200},{16,208},{24,216},{32,224},{40,232},{48,240},{56,2... | collective-permute-start | bytes 12296 | tf_op jit(solution)/shard_map/ppermute | solution.py:516
  102.5 5.1 %collective-permute-start.30 = (f32[8,1,128]{2,1,0:T(1,128)S(1)}, f32[8,1,128]{2,1,0:T(1,128)S(1)}, u32[]{:S(2)}, u32[]{:S(2)}) collective-permute-start(f32[8,1,128]{2,1,0:T(1,128)S(1)} %bitcast.14), channel_id=1, source_target_pairs={{0,128},{8,136},{16,144},{24,152},{32,160},{40,168},{48,176},{56,1... | collective-permute-start | bytes 12296 | tf_op jit(solution)/shard_map/ppermute | solution.py:516
  103.2 4.5 %collective-permute-start.29 = (f32[8,1,128]{2,1,0:T(1,128)S(1)}, f32[8,1,128]{2,1,0:T(1,128)S(1)}, u32[]{:S(2)}, u32[]{:S(2)}) collective-permute-start(f32[8,1,128]{2,1,0:T(1,128)S(1)} %bitcast.15), channel_id=1, source_target_pairs={{0,64},{8,72},{16,80},{24,88},{32,96},{40,104},{48,112},{56,120},{... | collective-permute-start | bytes 12296 | tf_op jit(solution)/shard_map/ppermute | solution.py:516
  110.3 12.8 %all-to-all-start = ((f32[8,1,128]{2,1,0:T(1,128)}), f32[8,1,128]{2,1,0:T(1,128)S(1)}, u32[]{:S(2)}, u32[]{:S(2)}) async-start(f32[8,1,128]{2,1,0:T(1,128)} %bitcast.11), calls=%async_computation | async-start | bytes 8192 | tf_op jit(solution)/shard_map/all_to_all | solution.py:501

commit v5 on v3

--- a/solution.py
+++ b/solution.py
@@ -268,7 +268,7 @@
         inner_inverse,
         twist,
     ) = rest[:9]
-    blocks_out, (known, incoming, out) = rest[9 : 9 + given], rest[9 + given :]
+    blocks_out, (incoming, out) = rest[9 : 9 + given], rest[9 + given :]
     incoming = load_blocks(place, blocks_in, incoming)
     if given == 1:
         out = blocks_out[0]
@@ -276,8 +276,6 @@
     sub = lax.broadcasted_iota(jnp.int32, (tiles, lanes), 0)
     first = (sub == 0) & (lane < 2)
     last = (sub == tiles - 1) & (lane >= lanes - 2)
-    if edges:
-        known[...] = sums[...]
     line_fields = []
     for line in range(lines):
         blocks = [
@@ -320,7 +318,10 @@
             total = total + piece * scaled[-1]
     if not edges:
         energy = jnp.sum(total, axis=(0, 1), keepdims=True)
-        known[...] = sums[...] + jnp.where(lane_index((1, lanes)) == 2, energy, 0.0)
+        third = lax.broadcasted_iota(jnp.int32, (8, lanes), 0) == 2
+        known = sums[...] + jnp.where(third, energy, 0.0)
+        for part in range(parts):
+            out[part, tiles * lines :, :] = known
     high, low = split(jnp.concatenate(scaled, 0))
     back = dot(jnp.concatenate([high, low], 1), inner_inverse[: 4 * kept, :]) + dot(
         high, inner_inverse[4 * kept :, :]
@@ -402,24 +403,24 @@
     result = add_halo_rows(partial[...], added[:, :width])
     image[...] = result
     products = (grad[...] * field, field * result, result * result)
+    for row, product in enumerate(products):
+        total = jnp.sum(product, axis=(0, 1), keepdims=True)
+        sums[row : row + 1, :] = jnp.broadcast_to(total, (1, lanes))
+    sums[3:8, :] = jnp.zeros((5, lanes), jnp.float32)
+
+
+def spread_kernel(block, spread):
+    total = block[0, tiles * lines :, :]
+    for part in range(1, parts):
+        total = total + block[part, tiles * lines :, :]
     lane = lane_index((1, lanes))
-    line = jnp.zeros((1, lanes), jnp.float32)
-    for which, product in enumerate(products):
-        total = jnp.sum(product, axis=(0, 1), keepdims=True)
-        line = line + jnp.where(lane == which, total, 0.0)
-    sums[...] = line
-
-
-def spread_kernel(one, two, three, four, spread):
-    total = (one[...] + two[...]) + (three[...] + four[...])
-    for part in range(parts):
-        spread[part] = total
-
-
-def second_kernel(place, *rest):
-    *blocks, image, basis, second, buffer = rest
-    buffer = load_blocks(place, blocks, buffer)
-    second[...] = image[...] + left_product(basis[...], load_coefs(buffer, tiles))
+    line = jnp.where(lane == 0, total[0:1], jnp.where(lane == 1, total[1:2], total[2:3]))
+    for row in range(spread.shape[0]):
+        spread[row] = line
+
+
+def second_kernel(block, image, basis, second):
+    second[...] = image[...] + left_product(basis[...], load_coefs(block, tiles))
 
 
 def final_kernel(
@@ -493,17 +494,6 @@
     return lax.ppermute(send_a, "rows", inner), lax.ppermute(send_b, "rows", outer)
 
 
-def sum_over_rows(value):
-    count = lax.axis_size("rows")
-
-    def swap(mask):
-        return lax.ppermute(value, "rows", [(i, i ^ mask) for i in range(count)])
-
-    value = value + swap(1)
-    value = value + swap(2) + swap(4) + swap(6)
-    return value, swap(8), swap(16), swap(24)
-
-
 def on_device(latent, counts, exposure):
     consts = tables()
     tab = {name: jnp.asarray(value) for name, value in consts.items()}
@@ -562,12 +552,12 @@
         flops=10**7,
     )
     blocks = exchange(blocks)
-    *blocks, _ = call(
+    blocks = call(
         functools.partial(
             filter_kernel, edges=True, taken=len(blocks), given=parts if pairwise[1] else 1
         ),
-        (*sent(wide, pairwise[1]), (1, lanes)),
-        (place, *blocks, jnp.zeros((1, lanes), jnp.float32), *filters),
+        sent(wide, pairwise[1]),
+        (place, *blocks, jnp.zeros((8, lanes), jnp.float32), *filters),
         (wide_buffer, wide_buffer),
         flops=10**9,
     )
@@ -596,26 +586,22 @@
     )
     blocks = exchange(blocks)
     image, sums = call(
-        sums_kernel, (block, (1, lanes)), (search, grad, partial, added), flops=10**8
-    )
-    *blocks, known = call(
+        sums_kernel, (block, (8, lanes)), (search, grad, partial, added), flops=10**8
+    )
+    blocks = call(
         functools.partial(
             filter_kernel, edges=False, taken=len(blocks), given=parts if pairwise[3] else 1
         ),
-        (*sent(slim, pairwise[3]), (1, lanes)),
+        sent(wide, pairwise[3]),
         (place, *blocks, sums, *filters),
-        (slim_buffer, slim_buffer),
+        (slim_buffer, wide_buffer),
         flops=10**9,
     )
     blocks = exchange(blocks)
-    (spread,) = call(spread_kernel, ((parts, 1, lanes),), sum_over_rows(known))
-    sums = exchange([spread])[0]
+    (spread,) = call(spread_kernel, ((lax.axis_size("rows"), 1, lanes),), blocks)
+    sums = lax.all_to_all(spread, "rows", split_axis=0, concat_axis=0, tiled=True)
     (second,) = call(
-        second_kernel,
-        (block,),
-        (place, *blocks, image, tab["row_inverse"]),
-        (slim_buffer,),
-        flops=10**8,
+        second_kernel, (block,), (*blocks, image, tab["row_inverse"]), flops=10**8
     )
     return call(
         final_kernel,

time: 126 us -> 128 us (1.016); the launches traced: 125 us -> 125 us
  blocking collectives: 0 us -> 21.1 us
  starting transfers between devices: 74.3 us -> 64.1 us
  waiting for transfers between devices: 34.7 us -> 25.7 us
  Pallas kernels: 14.2 us -> 12.5 us
    all_to_all x0 -> x1, blocking collectives: none -> 21.1 us  [exchange(): lax.all_to_all(blocks[0], 'cols', split_axis=0, concat_axis=0, tiled=True)]
    ppermute x7 -> x0, starting transfers between devices: 8.39 us -> none  [swap(): return lax.ppermute(value, 'rows', [(i, i ^ mask) for i in range(count)])]
    ppermute x7 -> x0, waiting for transfers between devices: 8.06 us -> none  [swap(): return lax.ppermute(value, 'rows', [(i, i ^ mask) for i in range(count)])]
    all_to_all x2 -> x1, starting transfers between devices: 11.1 us -> 9.29 us  [on_device(): lax.all_to_all(spread, 'rows', split_axis=0, concat_axis=0, tiled=True)]
    pallas_call x11, Pallas kernels: 14.2 us -> 12.5 us  [call(): pl.pallas_call(kernel, out_shape=outs, in_specs=in_specs, out_specs=tuple...]
    all_to_all x2 -> x1, waiting for transfers between devices: 6.8 us -> 5.84 us  [on_device(): lax.all_to_all(spread, 'rows', split_axis=0, concat_axis=0, tiled=True)]
  transfers between devices with their start and end apart: 34 -> 26, of which waited for: 17 -> 13; matrix products, arithmetic and copies ran while one was open for 0% -> 0% of each run, Pallas kernels for 4% -> 3%
where the time goes in v5:
time: 128 us; the launch traced here: 125 us
  starting transfers between devices  64.1 us (50%)
  waiting for transfers between devices  25.7 us (20%)
  blocking collectives  21.1 us (16%)
  Pallas kernels  12.5 us (10%)
    ppermute x21, starting transfers between devices, exchange(): lax.ppermute(blocks[mask], 'cols', [(i, i ^ mask) for i in range(count)])  46.3 us
    all_to_all x1, blocking collectives, exchange(): lax.all_to_all(blocks[0], 'cols', split_axis=0, concat_axis=0, tiled=True)  21.1 us
    ppermute x21, waiting for transfers between devices, exchange(): lax.ppermute(blocks[mask], 'cols', [(i, i ^ mask) for i in range(count)])  17.7 us
    pallas_call x11, Pallas kernels, call(): pl.pallas_call(kernel, out_shape=outs, in_specs=in_specs, out_specs=tuple...  12.5 us
    all_to_all x1, starting transfers between devices, on_device(): lax.all_to_all(spread, 'rows', split_axis=0, concat_axis=0, tiled=True)  9.29 us
    ppermute x2, starting transfers between devices, swap_rows(): lax.ppermute(send_b, 'rows', outer)  8.35 us
    all_to_all x1, waiting for transfers between devices, on_device(): lax.all_to_all(spread, 'rows', split_axis=0, concat_axis=0, tiled=True)  5.84 us
  transfers between devices with their start and end apart: 26, of which 13 were waited for; matrix products, arithmetic and copies ran while one was open for 0% of the time, Pallas kernels for 3%

profile of v5, /device:TPU:8, one launch (start us, length us, event | category | flops | bytes accessed | tf_op | source)
XLA Modules:
  0.0 125.5 jit_solution(11347771508260978346)
XLA Ops:
  0.6 0.0 copy-start.10
  0.7 0.9 broadcast_select_fusion
  1.5 4.0 %collective-permute-start.1 = (f32[2,2048]{1,0:T(2,128)S(1)}, f32[2,2048]{1,0:T(2,128)S(1)}, u32[]{:S(2)}, u32[]{:S(2)}) collective-permute-start(f32[2,2048]{1,0:T(2,128)S(1)} %get-tuple-element.77), channel_id=1, source_target_pairs={{8,16},{24,32},{40,48},{56,64},{72,80},{88,96},{104,112},{120,128}... | collective-permute-start | bytes 49160 | tf_op jit(solution)/shard_map/ppermute | solution.py:494
  5.5 0.1 collective-permute-start
  5.7 0.1 pad_add_fusion.place
  5.7 0.0 copy-start.9
  5.8 2.6 %shard_map.157 = (f32[64,2176]{1,0:T(8,128)S(1)}, f32[64,2048]{1,0:T(8,128)S(1)}, f32[64,2048]{1,0:T(8,128)S(1)}) custom-call(f32[64,2048]{1,0:T(8,128)} %latent.1, s32[64,2048]{1,0:T(8,128)} %counts.1, s32[64,2048]{1,0:T(8,128)} %exposure.1, bf16[64,192]{1,0:T(8,128)(2,1)S(1)} %copy-done.10), custom_call_target="tpu_custom_call" | custom-call | flops 1000000000 | bytes 3227648 | tf_op jit(solution)/shard_map/pallas_call | solution.py:462
  8.3 0.4 collective-permute-done.1.swap_b
  8.7 0.0 copy-start.3
  8.7 0.0 copy-start.4
  8.8 0.0 copy-start.5
  8.8 0.0 copy-start.7
  8.8 1.0 shard_map.158
  9.8 2.0 %collective-permute-start.2 = (f32[136,128]{1,0:T(8,128)S(1)}, f32[136,128]{1,0:T(8,128)S(1)}, u32[]{:S(2)}, u32[]{:S(2)}) collective-permute-start(f32[136,128]{1,0:T(8,128)S(1)} %get-tuple-element.42), channel_id=1, source_target_pairs={{0,1},{1,0},{2,3},{3,2},{4,5},{5,4},{6,7},{7,6},{8,9},{9,8},{10,11... | collective-permute-start | bytes 208904 | tf_op jit(solution)/shard_map/ppermute | solution.py:488
  11.8 3.3 %collective-permute-start.3 = (f32[136,128]{1,0:T(8,128)S(1)}, f32[136,128]{1,0:T(8,128)S(1)}, u32[]{:S(2)}, u32[]{:S(2)}) collective-permute-start(f32[136,128]{1,0:T(8,128)S(1)} %get-tuple-element.43), channel_id=1, source_target_pairs={{0,2},{1,3},{2,0},{3,1},{4,6},{5,7},{6,4},{7,5},{8,10},{9,11},{10,... | collective-permute-start | bytes 208904 | tf_op jit(solution)/shard_map/ppermute | solution.py:488
  15.0 0.0 collective-permute-start.4
  15.0 6.4 %collective-permute-start.5 = (f32[136,128]{1,0:T(8,128)S(1)}, f32[136,128]{1,0:T(8,128)S(1)}, u32[]{:S(2)}, u32[]{:S(2)}) collective-permute-start(f32[136,128]{1,0:T(8,128)S(1)} %get-tuple-element.45), channel_id=1, source_target_pairs={{0,4},{1,5},{2,6},{3,7},{4,0},{5,1},{6,2},{7,3},{8,12},{9,13},{10,... | collective-permute-start | bytes 208904 | tf_op jit(solution)/shard_map/ppermute | solution.py:488
  21.4 0.0 collective-permute-start.6
  21.4 0.0 collective-permute-done.2.rest_1_
  21.4 4.6 %collective-permute-start.7 = (f32[136,128]{1,0:T(8,128)S(1)}, f32[136,128]{1,0:T(8,128)S(1)}, u32[]{:S(2)}, u32[]{:S(2)}) collective-permute-start(f32[136,128]{1,0:T(8,128)S(1)} %get-tuple-element.47), channel_id=1, source_target_pairs={{0,6},{1,7},{2,4},{3,5},{4,2},{5,3},{6,0},{7,1},{8,14},{9,15},{10,... | collective-permute-start | bytes 208904 | tf_op jit(solution)/shard_map/ppermute | solution.py:488
  26.0 2.7 %collective-permute-start.8 = (f32[136,128]{1,0:T(8,128)S(1)}, f32[136,128]{1,0:T(8,128)S(1)}, u32[]{:S(2)}, u32[]{:S(2)}) collective-permute-start(f32[136,128]{1,0:T(8,128)S(1)} %get-tuple-element.48), channel_id=1, source_target_pairs={{0,7},{1,6},{2,5},{3,4},{4,3},{5,2},{6,1},{7,0},{8,15},{9,14},{10,... | collective-permute-start | bytes 208904 | tf_op jit(solution)/shard_map/ppermute | solution.py:488
  28.7 0.0 collective-permute-done.4.rest_3_
  28.8 1.9 %collective-permute-done.6.rest_5_ = f32[136,128]{1,0:T(8,128)S(1)} collective-permute-done((f32[136,128]{1,0:T(8,128)S(1)}, f32[136,128]{1,0:T(8,128)S(1)}, u32[]{:S(2)}, u32[]{:S(2)}) %collective-permute-start.6) | collective-permute-done | bytes 69664 | tf_op jit(solution)/shard_map/ppermute | solution.py:488
  30.6 1.1 collective-permute-done.7.rest_6_
  31.8 2.5 %collective-permute-done.8.rest_7_ = f32[136,128]{1,0:T(8,128)S(1)} collective-permute-done((f32[136,128]{1,0:T(8,128)S(1)}, f32[136,128]{1,0:T(8,128)S(1)}, u32[]{:S(2)}, u32[]{:S(2)}) %collective-permute-start.8) | collective-permute-done | bytes 69664 | tf_op jit(solution)/shard_map/ppermute | solution.py:488
  34.3 0.0 copy-start
  34.4 1.7 %shard_map.159 = (f32[136,128]{1,0:T(8,128)S(1)}, f32[136,128]{1,0:T(8,128)S(1)}, f32[136,128]{1,0:T(8,128)S(1)}, f32[136,128]{1,0:T(8,128)S(1)}, f32[136,128]{1...) custom-call(s32[2]{0:T(128)S(1)} %pad_add_fusion.place, ...), custom_call_target="tpu_custom_call" | custom-call | flops 1000000000 | bytes 2396168 | tf_op jit(solution)/shard_map/pallas_call | solution.py:462
  36.1 0.4 collective-permute-start.9
  36.5 1.9 %collective-permute-start.10 = (f32[136,128]{1,0:T(8,128)S(1)}, f32[136,128]{1,0:T(8,128)S(1)}, u32[]{:S(2)}, u32[]{:S(2)}) collective-permute-start(f32[136,128]{1,0:T(8,128)S(1)} %get-tuple-element.51), channel_id=1, source_target_pairs={{0,2},{1,3},{2,0},{3,1},{4,6},{5,7},{6,4},{7,5},{8,10},{9,11},{10,... | collective-permute-start | bytes 208904 | tf_op jit(solution)/shard_map/ppermute | solution.py:488
  38.3 2.3 %collective-permute-start.11 = (f32[136,128]{1,0:T(8,128)S(1)}, f32[136,128]{1,0:T(8,128)S(1)}, u32[]{:S(2)}, u32[]{:S(2)}) collective-permute-start(f32[136,128]{1,0:T(8,128)S(1)} %get-tuple-element.52), channel_id=1, source_target_pairs={{0,3},{1,2},{2,1},{3,0},{4,7},{5,6},{6,5},{7,4},{8,11},{9,10},{10,... | collective-permute-start | bytes 208904 | tf_op jit(solution)/shard_map/ppermute | solution.py:488
  40.6 3.2 %collective-permute-start.12 = (f32[136,128]{1,0:T(8,128)S(1)}, f32[136,128]{1,0:T(8,128)S(1)}, u32[]{:S(2)}, u32[]{:S(2)}) collective-permute-start(f32[136,128]{1,0:T(8,128)S(1)} %get-tuple-element.53), channel_id=1, source_target_pairs={{0,4},{1,5},{2,6},{3,7},{4,0},{5,1},{6,2},{7,3},{8,12},{9,13},{10,... | collective-permute-start | bytes 208904 | tf_op jit(solution)/shard_map/ppermute | solution.py:488
  43.8 0.7 collective-permute-start.13
  44.4 0.0 collective-permute-done.9.rest_1_
  44.4 4.0 %collective-permute-start.14 = (f32[136,128]{1,0:T(8,128)S(1)}, f32[136,128]{1,0:T(8,128)S(1)}, u32[]{:S(2)}, u32[]{:S(2)}) collective-permute-start(f32[136,128]{1,0:T(8,128)S(1)} %get-tuple-element.55), channel_id=1, source_target_pairs={{0,6},{1,7},{2,4},{3,5},{4,2},{5,3},{6,0},{7,1},{8,14},{9,15},{10,... | collective-permute-start | bytes 208904 | tf_op jit(solution)/shard_map/ppermute | solution.py:488
  48.4 0.0 collective-permute-done.10.rest_2_
  48.4 1.3 %collective-permute-start.15 = (f32[136,128]{1,0:T(8,128)S(1)}, f32[136,128]{1,0:T(8,128)S(1)}, u32[]{:S(2)}, u32[]{:S(2)}) collective-permute-start(f32[136,128]{1,0:T(8,128)S(1)} %get-tuple-element.56), channel_id=1, source_target_pairs={{0,7},{1,6},{2,5},{3,4},{4,3},{5,2},{6,1},{7,0},{8,15},{9,14},{10,... | collective-permute-start | bytes 208904 | tf_op jit(solution)/shard_map/ppermute | solution.py:488
  49.8 0.1 collective-permute-done.12.rest_4_
  49.9 2.2 %collective-permute-done.13.rest_5_ = f32[136,128]{1,0:T(8,128)S(1)} collective-permute-done((f32[136,128]{1,0:T(8,128)S(1)}, f32[136,128]{1,0:T(8,128)S(1)}, u32[]{:S(2)}, u32[]{:S(2)}) %collective-permute-start.13) | collective-permute-done | bytes 69664 | tf_op jit(solution)/shard_map/ppermute | solution.py:488
  52.1 1.6 %collective-permute-done.14.rest_6_ = f32[136,128]{1,0:T(8,128)S(1)} collective-permute-done((f32[136,128]{1,0:T(8,128)S(1)}, f32[136,128]{1,0:T(8,128)S(1)}, u32[]{:S(2)}, u32[]{:S(2)}) %collective-permute-start.14) | collective-permute-done | bytes 69664 | tf_op jit(solution)/shard_map/ppermute | solution.py:488
  53.6 3.2 %collective-permute-done.15.rest_7_ = f32[136,128]{1,0:T(8,128)S(1)} collective-permute-done((f32[136,128]{1,0:T(8,128)S(1)}, f32[136,128]{1,0:T(8,128)S(1)}, u32[]{:S(2)}, u32[]{:S(2)}) %collective-permute-start.15) | collective-permute-done | bytes 69664 | tf_op jit(solution)/shard_map/ppermute | solution.py:488
  56.8 0.9 shard_map.160
  57.7 0.1 collective-permute-start.16
  57.8 4.4 %collective-permute-start.17 = (f32[2,2176]{1,0:T(2,128)S(1)}, f32[2,2176]{1,0:T(2,128)S(1)}, u32[]{:S(2)}, u32[]{:S(2)}) collective-permute-start(f32[2,2176]{1,0:T(2,128)S(1)} %get-tuple-element.63), channel_id=1, source_target_pairs={{8,16},{24,32},{40,48},{56,64},{72,80},{88,96},{104,112},{120,128}... | collective-permute-start | bytes 52232 | tf_op jit(solution)/shard_map/ppermute | solution.py:494
  62.2 1.1 shard_map.161
  63.3 1.7 %collective-permute-done.17.swap_b = f32[2,2176]{1,0:T(2,128)S(1)} collective-permute-done((f32[2,2176]{1,0:T(2,128)S(1)}, f32[2,2176]{1,0:T(2,128)S(1)}, u32[]{:S(2)}, u32[]{:S(2)}) %collective-permute-start.17) | collective-permute-done | bytes 17440 | tf_op jit(solution)/shard_map/ppermute | solution.py:494
  65.0 0.9 shard_map.162
  65.9 0.8 collective-permute-start.18
  66.7 1.3 %collective-permute-start.19 = (f32[128,128]{1,0:T(8,128)S(1)}, f32[128,128]{1,0:T(8,128)S(1)}, u32[]{:S(2)}, u32[]{:S(2)}) collective-permute-start(f32[128,128]{1,0:T(8,128)S(1)} %get-tuple-element.66), channel_id=1, source_target_pairs={{0,2},{1,3},{2,0},{3,1},{4,6},{5,7},{6,4},{7,5},{8,10},{9,11},{10,... | collective-permute-start | bytes 196616 | tf_op jit(solution)/shard_map/ppermute | solution.py:488
  68.0 2.4 %collective-permute-start.20 = (f32[128,128]{1,0:T(8,128)S(1)}, f32[128,128]{1,0:T(8,128)S(1)}, u32[]{:S(2)}, u32[]{:S(2)}) collective-permute-start(f32[128,128]{1,0:T(8,128)S(1)} %get-tuple-element.67), channel_id=1, source_target_pairs={{0,3},{1,2},{2,1},{3,0},{4,7},{5,6},{6,5},{7,4},{8,11},{9,10},{10,... | collective-permute-start | bytes 196616 | tf_op jit(solution)/shard_map/ppermute | solution.py:488
  70.4 2.6 %collective-permute-start.21 = (f32[128,128]{1,0:T(8,128)S(1)}, f32[128,128]{1,0:T(8,128)S(1)}, u32[]{:S(2)}, u32[]{:S(2)}) collective-permute-start(f32[128,128]{1,0:T(8,128)S(1)} %get-tuple-element.68), channel_id=1, source_target_pairs={{0,4},{1,5},{2,6},{3,7},{4,0},{5,1},{6,2},{7,3},{8,12},{9,13},{10,... | collective-permute-start | bytes 196616 | tf_op jit(solution)/shard_map/ppermute | solution.py:488
  73.0 1.6 %collective-permute-start.22 = (f32[128,128]{1,0:T(8,128)S(1)}, f32[128,128]{1,0:T(8,128)S(1)}, u32[]{:S(2)}, u32[]{:S(2)}) collective-permute-start(f32[128,128]{1,0:T(8,128)S(1)} %get-tuple-element.69), channel_id=1, source_target_pairs={{0,5},{1,4},{2,7},{3,6},{4,1},{5,0},{6,3},{7,2},{8,13},{9,12},{10,... | collective-permute-start | bytes 196616 | tf_op jit(solution)/shard_map/ppermute | solution.py:488
  74.7 3.1 %collective-permute-start.23 = (f32[128,128]{1,0:T(8,128)S(1)}, f32[128,128]{1,0:T(8,128)S(1)}, u32[]{:S(2)}, u32[]{:S(2)}) collective-permute-start(f32[128,128]{1,0:T(8,128)S(1)} %get-tuple-element.70), channel_id=1, source_target_pairs={{0,6},{1,7},{2,4},{3,5},{4,2},{5,3},{6,0},{7,1},{8,14},{9,15},{10,... | collective-permute-start | bytes 196616 | tf_op jit(solution)/shard_map/ppermute | solution.py:488
  77.8 1.8 %collective-permute-start.24 = (f32[128,128]{1,0:T(8,128)S(1)}, f32[128,128]{1,0:T(8,128)S(1)}, u32[]{:S(2)}, u32[]{:S(2)}) collective-permute-start(f32[128,128]{1,0:T(8,128)S(1)} %get-tuple-element.71), channel_id=1, source_target_pairs={{0,7},{1,6},{2,5},{3,4},{4,3},{5,2},{6,1},{7,0},{8,15},{9,14},{10,... | collective-permute-start | bytes 196616 | tf_op jit(solution)/shard_map/ppermute | solution.py:488
  79.6 0.3 shard_map.163
  79.9 0.5 collective-permute-done.22.rest_5_
  80.5 1.6 %collective-permute-done.23.rest_6_ = f32[128,128]{1,0:T(8,128)S(1)} collective-permute-done((f32[128,128]{1,0:T(8,128)S(1)}, f32[128,128]{1,0:T(8,128)S(1)}, u32[]{:S(2)}, u32[]{:S(2)}) %collective-permute-start.23) | collective-permute-done | bytes 65568 | tf_op jit(solution)/shard_map/ppermute | solution.py:488
  82.1 3.0 %collective-permute-done.24.rest_7_ = f32[128,128]{1,0:T(8,128)S(1)} collective-permute-done((f32[128,128]{1,0:T(8,128)S(1)}, f32[128,128]{1,0:T(8,128)S(1)}, u32[]{:S(2)}, u32[]{:S(2)}) %collective-permute-start.24) | collective-permute-done | bytes 65568 | tf_op jit(solution)/shard_map/ppermute | solution.py:488
  85.1 1.7 %shard_map.164 = f32[8,136,128]{2,1,0:T(8,128)S(1)} custom-call(s32[2]{0:T(128)S(1)} %pad_add_fusion.place, f32[128,128]{1,0:T(8,128)S(1)} %get-tuple-element.64.rest_0_, f32[128,128]{1,0:T(8,128)S(1)} %collective-permute-done.18.rest_1_, f32[128,128]{1,0:T(8,128)S(1)} %collective-permute-done.19.rest_2_, f32[128,128]{1,0:T(8,128)S(1)} %collective-permute-done.20.rest_3_, ...), custom_call_target="tpu_custom_call" | custom-call | flops 1000000000 | bytes 2363400 | tf_op jit(solution)/shard_map/pallas_call | solution.py:462
  86.8 21.1 %all_to_all.10.block = f32[8,136,128]{2,1,0:T(8,128)S(1)} all-to-all(f32[8,136,128]{2,1,0:T(8,128)S(1)} %shard_map.164), channel_id=1, replica_groups=mesh['rows'=32,'cols'=8] {'cols'}, dimensions={0} | all-to-all | bytes 1114112 | tf_op jit(solution)/shard_map/all_to_all | solution.py:484
  107.9 0.6 shard_map.165
  108.5 9.3 %all-to-all-start.1 = ((f32[32,1,128]{2,1,0:T(1,128)}), f32[32,1,128]{2,1,0:T(1,128)S(1)}, u32[]{:S(2)}, u32[]{:S(2)}) async-start(f32[32,1,128]{2,1,0:T(1,128)} %shard_map.165), calls=%async_computation.1 | async-start | bytes 32768 | tf_op jit(solution)/shard_map/all_to_all | solution.py:602
  117.8 0.3 shard_map.166.second
  118.0 5.8 %all-to-all-done.1.sums = f32[32,1,128]{2,1,0:T(1,128)S(1)} async-done(((f32[32,1,128]{2,1,0:T(1,128)}), f32[32,1,128]{2,1,0:T(1,128)S(1)}, u32[]{:S(2)}, u32[]{:S(2)}) %all-to-all-start.1) | async-done | bytes 16416 | tf_op jit(solution)/shard_map/all_to_all | solution.py:602
  123.9 1.4 %shard_map.167 = (f32[64,2048]{1,0:T(8,128)}, f32[64,2048]{1,0:T(8,128)}, f32[64,2048]{1,0:T(8,128)}) custom-call(f32[32,1,128]{2,1,0:T(1,128)S(1)} %all-to-all-done.1.sums, f32[64,2176]{1,0:T(8,128)S(1)} %get-tuple-element.59.search, f32[64,2048]{1,0:T(8,128)S(1)} %get-tuple-element.72.grad, f32[64,2048]{1,0:T(8,128)S(1)} %get-tuple-element.76.image, ...), custom_call_target="tpu_custom_call" | custom-call | flops 1000000 | bytes 3719168 | tf_op jit(solution)/shard_map/pallas_call | solution.py:462
  (25 shorter events, 0.1 us)
Async XLA Ops:
  0.6 5.1 %copy-start.10 = (bf16[64,192]{1,0:T(8,128)(2,1)S(1)}, bf16[64,192]{1,0:T(8,128)(2,1)}, u32[]{:S(2)}) copy-start(bf16[64,192]{1,0:T(8,128)(2,1)} %constant.47.clone.basis) | copy-start | bytes 73732
  1.5 7.2 %collective-permute-start.1 = (f32[2,2048]{1,0:T(2,128)S(1)}, f32[2,2048]{1,0:T(2,128)S(1)}, u32[]{:S(2)}, u32[]{:S(2)}) collective-permute-start(f32[2,2048]{1,0:T(2,128)S(1)} %get-tuple-element.77), channel_id=1, source_target_pairs={{8,16},{24,32},{40,48},{56,64},{72,80},{88,96},{104,112},{120,128}... | collective-permute-start | bytes 49160 | tf_op jit(solution)/shard_map/ppermute | solution.py:494
  5.5 3.2 %collective-permute-start = (f32[2,2048]{1,0:T(2,128)S(1)}, f32[2,2048]{1,0:T(2,128)S(1)}, u32[]{:S(2)}, u32[]{:S(2)}) collective-permute-start(f32[2,2048]{1,0:T(2,128)S(1)} %get-tuple-element.78), channel_id=1, source_target_pairs={{0,8},{8,0},{16,24},{24,16},{32,40},{40,32},{48,56},{56,48},{64,72... | collective-permute-start | bytes 49160 | tf_op jit(solution)/shard_map/ppermute | solution.py:494
  5.7 3.0 %copy-start.1 = (bf16[64,48]{1,0:T(8,128)(2,1)S(1)}, bf16[64,48]{1,0:T(8,128)(2,1)}, u32[]{:S(2)}) copy-start(bf16[64,48]{1,0:T(8,128)(2,1)} %constant.48.clone.basis) | copy-start | bytes 18436
  5.7 28.6 %copy-start.6 = (f32[2,72,128]{2,1,0:T(8,128)S(1)}, f32[2,72,128]{2,1,0:T(8,128)}, u32[]{:S(2)}) copy-start(f32[2,72,128]{2,1,0:T(8,128)} %constant.53.clone.rest_16_) | copy-start | bytes 221188
  5.7 28.6 %copy-start.8 = (f32[72,128]{1,0:T(8,128)S(1)}, f32[72,128]{1,0:T(8,128)}, u32[]{:S(2)}) copy-start(f32[72,128]{1,0:T(8,128)} %constant.56.clone.rest_11_) | copy-start | bytes 110596
  5.7 28.6 %copy-start.9 = (f32[64,128]{1,0:T(8,128)S(1)}, f32[64,128]{1,0:T(8,128)}, u32[]{:S(2)}) copy-start(f32[64,128]{1,0:T(8,128)} %constant.50.clone.rest_9_) | copy-start | bytes 98308
  8.7 25.6 %copy-start.2 = (bf16[384,256]{1,0:T(8,128)(2,1)S(1)}, bf16[384,256]{1,0:T(8,128)(2,1)}, u32[]{:S(2)}) copy-start(bf16[384,256]{1,0:T(8,128)(2,1)} %constant.55.clone.rest_15_) | copy-start | bytes 589828
  8.7 25.6 %copy-start.3 = (bf16[256,256]{1,0:T(8,128)(2,1)S(1)}, bf16[256,256]{1,0:T(8,128)(2,1)}, u32[]{:S(2)}) copy-start(bf16[256,256]{1,0:T(8,128)(2,1)} %constant.54.clone.rest_14_) | copy-start | bytes 393220
  8.7 25.6 %copy-start.4 = (bf16[128,432]{1,0:T(8,128)(2,1)S(1)}, bf16[128,432]{1,0:T(8,128)(2,1)}, u32[]{:S(2)}) copy-start(bf16[128,432]{1,0:T(8,128)(2,1)} %constant.52.clone.rest_13_) | copy-start | bytes 331780
  8.8 25.6 %copy-start.5 = (bf16[144,384]{1,0:T(8,128)(2,1)S(1)}, bf16[144,384]{1,0:T(8,128)(2,1)}, u32[]{:S(2)}) copy-start(bf16[144,384]{1,0:T(8,128)(2,1)} %constant.51.clone.rest_12_) | copy-start | bytes 331780
  8.8 25.6 %copy-start.7 = (f32[72,128]{1,0:T(8,128)S(1)}, f32[72,128]{1,0:T(8,128)}, u32[]{:S(2)}) copy-start(f32[72,128]{1,0:T(8,128)} %constant.57.clone.rest_10_) | copy-start | bytes 110596
  9.8 11.7 %collective-permute-start.2 = (f32[136,128]{1,0:T(8,128)S(1)}, f32[136,128]{1,0:T(8,128)S(1)}, u32[]{:S(2)}, u32[]{:S(2)}) collective-permute-start(f32[136,128]{1,0:T(8,128)S(1)} %get-tuple-element.42), channel_id=1, source_target_pairs={{0,1},{1,0},{2,3},{3,2},{4,5},{5,4},{6,7},{7,6},{8,9},{9,8},{10,11... | collective-permute-start | bytes 208904 | tf_op jit(solution)/shard_map/ppermute | solution.py:488
  11.8 14.3 %collective-permute-start.3 = (f32[136,128]{1,0:T(8,128)S(1)}, f32[136,128]{1,0:T(8,128)S(1)}, u32[]{:S(2)}, u32[]{:S(2)}) collective-permute-start(f32[136,128]{1,0:T(8,128)S(1)} %get-tuple-element.43), channel_id=1, source_target_pairs={{0,2},{1,3},{2,0},{3,1},{4,6},{5,7},{6,4},{7,5},{8,10},{9,11},{10,... | collective-permute-start | bytes 208904 | tf_op jit(solution)/shard_map/ppermute | solution.py:488
  15.0 13.7 %collective-permute-start.4 = (f32[136,128]{1,0:T(8,128)S(1)}, f32[136,128]{1,0:T(8,128)S(1)}, u32[]{:S(2)}, u32[]{:S(2)}) collective-permute-start(f32[136,128]{1,0:T(8,128)S(1)} %get-tuple-element.44), channel_id=1, source_target_pairs={{0,3},{1,2},{2,1},{3,0},{4,7},{5,6},{6,5},{7,4},{8,11},{9,10},{10,... | collective-permute-start | bytes 208904 | tf_op jit(solution)/shard_map/ppermute | solution.py:488
  15.0 13.7 %collective-permute-start.5 = (f32[136,128]{1,0:T(8,128)S(1)}, f32[136,128]{1,0:T(8,128)S(1)}, u32[]{:S(2)}, u32[]{:S(2)}) collective-permute-start(f32[136,128]{1,0:T(8,128)S(1)} %get-tuple-element.45), channel_id=1, source_target_pairs={{0,4},{1,5},{2,6},{3,7},{4,0},{5,1},{6,2},{7,3},{8,12},{9,13},{10,... | collective-permute-start | bytes 208904 | tf_op jit(solution)/shard_map/ppermute | solution.py:488
  21.4 9.2 %collective-permute-start.6 = (f32[136,128]{1,0:T(8,128)S(1)}, f32[136,128]{1,0:T(8,128)S(1)}, u32[]{:S(2)}, u32[]{:S(2)}) collective-permute-start(f32[136,128]{1,0:T(8,128)S(1)} %get-tuple-element.46), channel_id=1, source_target_pairs={{0,5},{1,4},{2,7},{3,6},{4,1},{5,0},{6,3},{7,2},{8,13},{9,12},{10,... | collective-permute-start | bytes 208904 | tf_op jit(solution)/shard_map/ppermute | solution.py:488
  21.4 10.3 %collective-permute-start.7 = (f32[136,128]{1,0:T(8,128)S(1)}, f32[136,128]{1,0:T(8,128)S(1)}, u32[]{:S(2)}, u32[]{:S(2)}) collective-permute-start(f32[136,128]{1,0:T(8,128)S(1)} %get-tuple-element.47), channel_id=1, source_target_pairs={{0,6},{1,7},{2,4},{3,5},{4,2},{5,3},{6,0},{7,1},{8,14},{9,15},{10,... | collective-permute-start | bytes 208904 | tf_op jit(solution)/shard_map/ppermute | solution.py:488
  26.0 8.2 %collective-permute-start.8 = (f32[136,128]{1,0:T(8,128)S(1)}, f32[136,128]{1,0:T(8,128)S(1)}, u32[]{:S(2)}, u32[]{:S(2)}) collective-permute-start(f32[136,128]{1,0:T(8,128)S(1)} %get-tuple-element.48), channel_id=1, source_target_pairs={{0,7},{1,6},{2,5},{3,4},{4,3},{5,2},{6,1},{7,0},{8,15},{9,14},{10,... | collective-permute-start | bytes 208904 | tf_op jit(solution)/shard_map/ppermute | solution.py:488
  34.3 22.4 %copy-start = (bf16[64,192]{1,0:T(8,128)(2,1)S(1)}, bf16[64,192]{1,0:T(8,128)(2,1)}, u32[]{:S(2)}) copy-start(bf16[64,192]{1,0:T(8,128)(2,1)} %constant.49.clone.rest_10_.basis) | copy-start | bytes 73732
  36.1 8.3 %collective-permute-start.9 = (f32[136,128]{1,0:T(8,128)S(1)}, f32[136,128]{1,0:T(8,128)S(1)}, u32[]{:S(2)}, u32[]{:S(2)}) collective-permute-start(f32[136,128]{1,0:T(8,128)S(1)} %get-tuple-element.50), channel_id=1, source_target_pairs={{0,1},{1,0},{2,3},{3,2},{4,5},{5,4},{6,7},{7,6},{8,9},{9,8},{10,11... | collective-permute-start | bytes 208904 | tf_op jit(solution)/shard_map/ppermute | solution.py:488
  36.5 12.0 %collective-permute-start.10 = (f32[136,128]{1,0:T(8,128)S(1)}, f32[136,128]{1,0:T(8,128)S(1)}, u32[]{:S(2)}, u32[]{:S(2)}) collective-permute-start(f32[136,128]{1,0:T(8,128)S(1)} %get-tuple-element.51), channel_id=1, source_target_pairs={{0,2},{1,3},{2,0},{3,1},{4,6},{5,7},{6,4},{7,5},{8,10},{9,11},{10,... | collective-permute-start | bytes 208904 | tf_op jit(solution)/shard_map/ppermute | solution.py:488
  38.3 11.4 %collective-permute-start.11 = (f32[136,128]{1,0:T(8,128)S(1)}, f32[136,128]{1,0:T(8,128)S(1)}, u32[]{:S(2)}, u32[]{:S(2)}) collective-permute-start(f32[136,128]{1,0:T(8,128)S(1)} %get-tuple-element.52), channel_id=1, source_target_pairs={{0,3},{1,2},{2,1},{3,0},{4,7},{5,6},{6,5},{7,4},{8,11},{9,10},{10,... | collective-permute-start | bytes 208904 | tf_op jit(solution)/shard_map/ppermute | solution.py:488
  40.6 9.3 %collective-permute-start.12 = (f32[136,128]{1,0:T(8,128)S(1)}, f32[136,128]{1,0:T(8,128)S(1)}, u32[]{:S(2)}, u32[]{:S(2)}) collective-permute-start(f32[136,128]{1,0:T(8,128)S(1)} %get-tuple-element.53), channel_id=1, source_target_pairs={{0,4},{1,5},{2,6},{3,7},{4,0},{5,1},{6,2},{7,3},{8,12},{9,13},{10,... | collective-permute-start | bytes 208904 | tf_op jit(solution)/shard_map/ppermute | solution.py:488
  43.8 8.3 %collective-permute-start.13 = (f32[136,128]{1,0:T(8,128)S(1)}, f32[136,128]{1,0:T(8,128)S(1)}, u32[]{:S(2)}, u32[]{:S(2)}) collective-permute-start(f32[136,128]{1,0:T(8,128)S(1)} %get-tuple-element.54), channel_id=1, source_target_pairs={{0,5},{1,4},{2,7},{3,6},{4,1},{5,0},{6,3},{7,2},{8,13},{9,12},{10,... | collective-permute-start | bytes 208904 | tf_op jit(solution)/shard_map/ppermute | solution.py:488
  44.4 9.2 %collective-permute-start.14 = (f32[136,128]{1,0:T(8,128)S(1)}, f32[136,128]{1,0:T(8,128)S(1)}, u32[]{:S(2)}, u32[]{:S(2)}) collective-permute-start(f32[136,128]{1,0:T(8,128)S(1)} %get-tuple-element.55), channel_id=1, source_target_pairs={{0,6},{1,7},{2,4},{3,5},{4,2},{5,3},{6,0},{7,1},{8,14},{9,15},{10,... | collective-permute-start | bytes 208904 | tf_op jit(solution)/shard_map/ppermute | solution.py:488
  48.4 8.3 %collective-permute-start.15 = (f32[136,128]{1,0:T(8,128)S(1)}, f32[136,128]{1,0:T(8,128)S(1)}, u32[]{:S(2)}, u32[]{:S(2)}) collective-permute-start(f32[136,128]{1,0:T(8,128)S(1)} %get-tuple-element.56), channel_id=1, source_target_pairs={{0,7},{1,6},{2,5},{3,4},{4,3},{5,2},{6,1},{7,0},{8,15},{9,14},{10,... | collective-permute-start | bytes 208904 | tf_op jit(solution)/shard_map/ppermute | solution.py:488
  57.7 5.6 %collective-permute-start.16 = (f32[2,2176]{1,0:T(2,128)S(1)}, f32[2,2176]{1,0:T(2,128)S(1)}, u32[]{:S(2)}, u32[]{:S(2)}) collective-permute-start(f32[2,2176]{1,0:T(2,128)S(1)} %get-tuple-element.62), channel_id=1, source_target_pairs={{0,8},{8,0},{16,24},{24,16},{32,40},{40,32},{48,56},{56,48},{64,72... | collective-permute-start | bytes 52232 | tf_op jit(solution)/shard_map/ppermute | solution.py:494
  57.8 7.2 %collective-permute-start.17 = (f32[2,2176]{1,0:T(2,128)S(1)}, f32[2,2176]{1,0:T(2,128)S(1)}, u32[]{:S(2)}, u32[]{:S(2)}) collective-permute-start(f32[2,2176]{1,0:T(2,128)S(1)} %get-tuple-element.63), channel_id=1, source_target_pairs={{8,16},{24,32},{40,48},{56,64},{72,80},{88,96},{104,112},{120,128}... | collective-permute-start | bytes 52232 | tf_op jit(solution)/shard_map/ppermute | solution.py:494
  65.9 8.7 %collective-permute-start.18 = (f32[128,128]{1,0:T(8,128)S(1)}, f32[128,128]{1,0:T(8,128)S(1)}, u32[]{:S(2)}, u32[]{:S(2)}) collective-permute-start(f32[128,128]{1,0:T(8,128)S(1)} %get-tuple-element.65), channel_id=1, source_target_pairs={{0,1},{1,0},{2,3},{3,2},{4,5},{5,4},{6,7},{7,6},{8,9},{9,8},{10,11... | collective-permute-start | bytes 196616 | tf_op jit(solution)/shard_map/ppermute | solution.py:488
  66.7 11.1 %collective-permute-start.19 = (f32[128,128]{1,0:T(8,128)S(1)}, f32[128,128]{1,0:T(8,128)S(1)}, u32[]{:S(2)}, u32[]{:S(2)}) collective-permute-start(f32[128,128]{1,0:T(8,128)S(1)} %get-tuple-element.66), channel_id=1, source_target_pairs={{0,2},{1,3},{2,0},{3,1},{4,6},{5,7},{6,4},{7,5},{8,10},{9,11},{10,... | collective-permute-start | bytes 196616 | tf_op jit(solution)/shard_map/ppermute | solution.py:488
  68.0 11.9 %collective-permute-start.20 = (f32[128,128]{1,0:T(8,128)S(1)}, f32[128,128]{1,0:T(8,128)S(1)}, u32[]{:S(2)}, u32[]{:S(2)}) collective-permute-start(f32[128,128]{1,0:T(8,128)S(1)} %get-tuple-element.67), channel_id=1, source_target_pairs={{0,3},{1,2},{2,1},{3,0},{4,7},{5,6},{6,5},{7,4},{8,11},{9,10},{10,... | collective-permute-start | bytes 196616 | tf_op jit(solution)/shard_map/ppermute | solution.py:488
  70.4 9.5 %collective-permute-start.21 = (f32[128,128]{1,0:T(8,128)S(1)}, f32[128,128]{1,0:T(8,128)S(1)}, u32[]{:S(2)}, u32[]{:S(2)}) collective-permute-start(f32[128,128]{1,0:T(8,128)S(1)} %get-tuple-element.68), channel_id=1, source_target_pairs={{0,4},{1,5},{2,6},{3,7},{4,0},{5,1},{6,2},{7,3},{8,12},{9,13},{10,... | collective-permute-start | bytes 196616 | tf_op jit(solution)/shard_map/ppermute | solution.py:488
  73.0 7.4 %collective-permute-start.22 = (f32[128,128]{1,0:T(8,128)S(1)}, f32[128,128]{1,0:T(8,128)S(1)}, u32[]{:S(2)}, u32[]{:S(2)}) collective-permute-start(f32[128,128]{1,0:T(8,128)S(1)} %get-tuple-element.69), channel_id=1, source_target_pairs={{0,5},{1,4},{2,7},{3,6},{4,1},{5,0},{6,3},{7,2},{8,13},{9,12},{10,... | collective-permute-start | bytes 196616 | tf_op jit(solution)/shard_map/ppermute | solution.py:488
  74.7 7.4 %collective-permute-start.23 = (f32[128,128]{1,0:T(8,128)S(1)}, f32[128,128]{1,0:T(8,128)S(1)}, u32[]{:S(2)}, u32[]{:S(2)}) collective-permute-start(f32[128,128]{1,0:T(8,128)S(1)} %get-tuple-element.70), channel_id=1, source_target_pairs={{0,6},{1,7},{2,4},{3,5},{4,2},{5,3},{6,0},{7,1},{8,14},{9,15},{10,... | collective-permute-start | bytes 196616 | tf_op jit(solution)/shard_map/ppermute | solution.py:488
  77.8 7.3 %collective-permute-start.24 = (f32[128,128]{1,0:T(8,128)S(1)}, f32[128,128]{1,0:T(8,128)S(1)}, u32[]{:S(2)}, u32[]{:S(2)}) collective-permute-start(f32[128,128]{1,0:T(8,128)S(1)} %get-tuple-element.71), channel_id=1, source_target_pairs={{0,7},{1,6},{2,5},{3,4},{4,3},{5,2},{6,1},{7,0},{8,15},{9,14},{10,... | collective-permute-start | bytes 196616 | tf_op jit(solution)/shard_map/ppermute | solution.py:488
  108.5 15.4 %all-to-all-start.1 = ((f32[32,1,128]{2,1,0:T(1,128)}), f32[32,1,128]{2,1,0:T(1,128)S(1)}, u32[]{:S(2)}, u32[]{:S(2)}) async-start(f32[32,1,128]{2,1,0:T(1,128)} %shard_map.165), calls=%async_computation.1 | async-start | bytes 32768 | tf_op jit(solution)/shard_map/all_to_all | solution.py:602

commit v6 on v4

--- a/solution.py
+++ b/solution.py
@@ -501,7 +501,7 @@
         return [lax.all_to_all(blocks[0], "cols", split_axis=0, concat_axis=0, tiled=True)]
     count = lax.axis_size("cols")
     got = {}
-    for mask in (4, 3, 5, 2, 6, 1, 7):
+    for mask in (1, 4, 2, 6, 3, 5, 7):
         got[mask] = lax.ppermute(blocks[mask], "cols", [(i, i ^ mask) for i in range(count)])
     return [blocks[0]] + [got[mask] for mask in range(1, parts)]
 

time: 125 us -> 125 us (level)
  no operation moved by 1% of the time
where the time goes in v6:
time: 125 us
  starting transfers between devices  72.9 us (58%)
  waiting for transfers between devices  35.5 us (28%)
  Pallas kernels  13.5 us (11%)
  other arithmetic  1.58 us (1%)
    ppermute x21, starting transfers between devices, exchange(): lax.ppermute(blocks[mask], 'cols', [(i, i ^ mask) for i in range(count)])  46.4 us
    ppermute x21, waiting for transfers between devices, exchange(): lax.ppermute(blocks[mask], 'cols', [(i, i ^ mask) for i in range(count)])  17.6 us
    pallas_call x11, Pallas kernels, call(): pl.pallas_call(kernel, out_shape=outs, in_specs=in_specs, out_specs=tuple...  13.5 us
    all_to_all x2, starting transfers between devices, exchange(): lax.all_to_all(blocks[0], 'cols', split_axis=0, concat_axis=0, tiled=True)  9.26 us
    all_to_all x2, waiting for transfers between devices, exchange(): lax.all_to_all(blocks[0], 'cols', split_axis=0, concat_axis=0, tiled=True)  8.81 us
    ppermute x7, starting transfers between devices, row_swap(): return lax.ppermute(value, 'rows', [(i, i ^ mask) for i in range(count)])  8.66 us
    ppermute x2, starting transfers between devices, swap_rows(): lax.ppermute(send_b, 'rows', outer)  8.39 us
    ppermute x7, waiting for transfers between devices, row_swap(): return lax.ppermute(value, 'rows', [(i, i ^ mask) for i in range(count)])  7.01 us
  transfers between devices with their start and end apart: 34, of which 17 were waited for; matrix products, arithmetic and copies ran while one was open for 1% of the time, Pallas kernels for 5%

profile of v6, /device:TPU:8, one launch (start us, length us, event | category | flops | bytes accessed | tf_op | source)
XLA Modules:
  0.0 124.6 jit_solution(17354362003253999538)
XLA Ops:
  0.6 0.0 copy-start.10
  0.7 0.9 broadcast_select_fusion
  1.5 4.0 %collective-permute-start.1 = (f32[2,2048]{1,0:T(2,128)S(1)}, f32[2,2048]{1,0:T(2,128)S(1)}, u32[]{:S(2)}, u32[]{:S(2)}) collective-permute-start(f32[2,2048]{1,0:T(2,128)S(1)} %get-tuple-element.85), channel_id=1, source_target_pairs={{8,16},{24,32},{40,48},{56,64},{72,80},{88,96},{104,112},{120,128}... | collective-permute-start | bytes 49160 | tf_op jit(solution)/shard_map/ppermute | solution.py:511
  5.5 0.1 collective-permute-start
  5.7 0.1 pad_add_fusion.place
  5.7 2.6 %shard_map.157 = (f32[64,2176]{1,0:T(8,128)S(1)}, f32[64,2048]{1,0:T(8,128)S(1)}, f32[64,2048]{1,0:T(8,128)S(1)}) custom-call(f32[64,2048]{1,0:T(8,128)} %latent.1, s32[64,2048]{1,0:T(8,128)} %counts.1, s32[64,2048]{1,0:T(8,128)} %exposure.1, bf16[64,192]{1,0:T(8,128)(2,1)S(1)} %copy-done.10), custom_call_target="tpu_custom_call" | custom-call | flops 1000000000 | bytes 3227648 | tf_op jit(solution)/shard_map/pallas_call | solution.py:479
  8.3 0.4 collective-permute-done.1.swap_b
  8.7 0.0 copy-start.2
  8.8 1.0 shard_map.158
  9.8 2.0 %collective-permute-start.2 = (f32[136,128]{1,0:T(8,128)S(1)}, f32[136,128]{1,0:T(8,128)S(1)}, u32[]{:S(2)}, u32[]{:S(2)}) collective-permute-start(f32[136,128]{1,0:T(8,128)S(1)} %get-tuple-element.46), channel_id=1, source_target_pairs={{0,1},{1,0},{2,3},{3,2},{4,5},{5,4},{6,7},{7,6},{8,9},{9,8},{10,11... | collective-permute-start | bytes 208904 | tf_op jit(solution)/shard_map/ppermute | solution.py:505
  11.8 3.3 %collective-permute-start.3 = (f32[136,128]{1,0:T(8,128)S(1)}, f32[136,128]{1,0:T(8,128)S(1)}, u32[]{:S(2)}, u32[]{:S(2)}) collective-permute-start(f32[136,128]{1,0:T(8,128)S(1)} %get-tuple-element.47), channel_id=1, source_target_pairs={{0,2},{1,3},{2,0},{3,1},{4,6},{5,7},{6,4},{7,5},{8,10},{9,11},{10,... | collective-permute-start | bytes 208904 | tf_op jit(solution)/shard_map/ppermute | solution.py:505
  15.1 6.4 %collective-permute-start.5 = (f32[136,128]{1,0:T(8,128)S(1)}, f32[136,128]{1,0:T(8,128)S(1)}, u32[]{:S(2)}, u32[]{:S(2)}) collective-permute-start(f32[136,128]{1,0:T(8,128)S(1)} %get-tuple-element.49), channel_id=1, source_target_pairs={{0,4},{1,5},{2,6},{3,7},{4,0},{5,1},{6,2},{7,3},{8,12},{9,13},{10,... | collective-permute-start | bytes 208904 | tf_op jit(solution)/shard_map/ppermute | solution.py:505
  21.5 4.6 %collective-permute-start.7 = (f32[136,128]{1,0:T(8,128)S(1)}, f32[136,128]{1,0:T(8,128)S(1)}, u32[]{:S(2)}, u32[]{:S(2)}) collective-permute-start(f32[136,128]{1,0:T(8,128)S(1)} %get-tuple-element.51), channel_id=1, source_target_pairs={{0,6},{1,7},{2,4},{3,5},{4,2},{5,3},{6,0},{7,1},{8,14},{9,15},{10,... | collective-permute-start | bytes 208904 | tf_op jit(solution)/shard_map/ppermute | solution.py:505
  26.1 2.8 %collective-permute-start.8 = (f32[136,128]{1,0:T(8,128)S(1)}, f32[136,128]{1,0:T(8,128)S(1)}, u32[]{:S(2)}, u32[]{:S(2)}) collective-permute-start(f32[136,128]{1,0:T(8,128)S(1)} %get-tuple-element.52), channel_id=1, source_target_pairs={{0,7},{1,6},{2,5},{3,4},{4,3},{5,2},{6,1},{7,0},{8,15},{9,14},{10,... | collective-permute-start | bytes 208904 | tf_op jit(solution)/shard_map/ppermute | solution.py:505
  28.9 1.8 %collective-permute-done.6.rest_5_ = f32[136,128]{1,0:T(8,128)S(1)} collective-permute-done((f32[136,128]{1,0:T(8,128)S(1)}, f32[136,128]{1,0:T(8,128)S(1)}, u32[]{:S(2)}, u32[]{:S(2)}) %collective-permute-start.6) | collective-permute-done | bytes 69664 | tf_op jit(solution)/shard_map/ppermute | solution.py:505
  30.6 1.2 collective-permute-done.7.rest_6_
  31.8 2.5 %collective-permute-done.8.rest_7_ = f32[136,128]{1,0:T(8,128)S(1)} collective-permute-done((f32[136,128]{1,0:T(8,128)S(1)}, f32[136,128]{1,0:T(8,128)S(1)}, u32[]{:S(2)}, u32[]{:S(2)}) %collective-permute-start.8) | collective-permute-done | bytes 69664 | tf_op jit(solution)/shard_map/ppermute | solution.py:505
  34.4 1.7 %shard_map.159 = (f32[136,128]{1,0:T(8,128)S(1)}, f32[136,128]{1,0:T(8,128)S(1)}, f32[136,128]{1,0:T(8,128)S(1)}, f32[136,128]{1,0:T(8,128)S(1)}, f32[136,128]{1...) custom-call(s32[2]{0:T(128)S(1)} %pad_add_fusion.place, ...), custom_call_target="tpu_custom_call" | custom-call | flops 1000000000 | bytes 2392072 | tf_op jit(solution)/shard_map/pallas_call | solution.py:479
  36.1 0.3 collective-permute-start.9
  36.5 1.9 %collective-permute-start.10 = (f32[136,128]{1,0:T(8,128)S(1)}, f32[136,128]{1,0:T(8,128)S(1)}, u32[]{:S(2)}, u32[]{:S(2)}) collective-permute-start(f32[136,128]{1,0:T(8,128)S(1)} %get-tuple-element.55), channel_id=1, source_target_pairs={{0,2},{1,3},{2,0},{3,1},{4,6},{5,7},{6,4},{7,5},{8,10},{9,11},{10,... | collective-permute-start | bytes 208904 | tf_op jit(solution)/shard_map/ppermute | solution.py:505
  38.3 2.3 %collective-permute-start.11 = (f32[136,128]{1,0:T(8,128)S(1)}, f32[136,128]{1,0:T(8,128)S(1)}, u32[]{:S(2)}, u32[]{:S(2)}) collective-permute-start(f32[136,128]{1,0:T(8,128)S(1)} %get-tuple-element.56), channel_id=1, source_target_pairs={{0,3},{1,2},{2,1},{3,0},{4,7},{5,6},{6,5},{7,4},{8,11},{9,10},{10,... | collective-permute-start | bytes 208904 | tf_op jit(solution)/shard_map/ppermute | solution.py:505
  40.6 3.2 %collective-permute-start.12 = (f32[136,128]{1,0:T(8,128)S(1)}, f32[136,128]{1,0:T(8,128)S(1)}, u32[]{:S(2)}, u32[]{:S(2)}) collective-permute-start(f32[136,128]{1,0:T(8,128)S(1)} %get-tuple-element.57), channel_id=1, source_target_pairs={{0,4},{1,5},{2,6},{3,7},{4,0},{5,1},{6,2},{7,3},{8,12},{9,13},{10,... | collective-permute-start | bytes 208904 | tf_op jit(solution)/shard_map/ppermute | solution.py:505
  43.8 0.7 collective-permute-start.13
  44.4 4.0 %collective-permute-start.14 = (f32[136,128]{1,0:T(8,128)S(1)}, f32[136,128]{1,0:T(8,128)S(1)}, u32[]{:S(2)}, u32[]{:S(2)}) collective-permute-start(f32[136,128]{1,0:T(8,128)S(1)} %get-tuple-element.59), channel_id=1, source_target_pairs={{0,6},{1,7},{2,4},{3,5},{4,2},{5,3},{6,0},{7,1},{8,14},{9,15},{10,... | collective-permute-start | bytes 208904 | tf_op jit(solution)/shard_map/ppermute | solution.py:505
  48.5 1.3 %collective-permute-start.15 = (f32[136,128]{1,0:T(8,128)S(1)}, f32[136,128]{1,0:T(8,128)S(1)}, u32[]{:S(2)}, u32[]{:S(2)}) collective-permute-start(f32[136,128]{1,0:T(8,128)S(1)} %get-tuple-element.60), channel_id=1, source_target_pairs={{0,7},{1,6},{2,5},{3,4},{4,3},{5,2},{6,1},{7,0},{8,15},{9,14},{10,... | collective-permute-start | bytes 208904 | tf_op jit(solution)/shard_map/ppermute | solution.py:505
  49.8 0.1 collective-permute-done.12.rest_4_
  49.9 2.2 %collective-permute-done.13.rest_5_ = f32[136,128]{1,0:T(8,128)S(1)} collective-permute-done((f32[136,128]{1,0:T(8,128)S(1)}, f32[136,128]{1,0:T(8,128)S(1)}, u32[]{:S(2)}, u32[]{:S(2)}) %collective-permute-start.13) | collective-permute-done | bytes 69664 | tf_op jit(solution)/shard_map/ppermute | solution.py:505
  52.1 1.5 %collective-permute-done.14.rest_6_ = f32[136,128]{1,0:T(8,128)S(1)} collective-permute-done((f32[136,128]{1,0:T(8,128)S(1)}, f32[136,128]{1,0:T(8,128)S(1)}, u32[]{:S(2)}, u32[]{:S(2)}) %collective-permute-start.14) | collective-permute-done | bytes 69664 | tf_op jit(solution)/shard_map/ppermute | solution.py:505
  53.6 3.1 %collective-permute-done.15.rest_7_ = f32[136,128]{1,0:T(8,128)S(1)} collective-permute-done((f32[136,128]{1,0:T(8,128)S(1)}, f32[136,128]{1,0:T(8,128)S(1)}, u32[]{:S(2)}, u32[]{:S(2)}) %collective-permute-start.15) | collective-permute-done | bytes 69664 | tf_op jit(solution)/shard_map/ppermute | solution.py:505
  56.8 0.9 shard_map.160
  57.7 0.1 collective-permute-start.16
  57.8 4.4 %collective-permute-start.17 = (f32[2,2176]{1,0:T(2,128)S(1)}, f32[2,2176]{1,0:T(2,128)S(1)}, u32[]{:S(2)}, u32[]{:S(2)}) collective-permute-start(f32[2,2176]{1,0:T(2,128)S(1)} %get-tuple-element.67), channel_id=1, source_target_pairs={{8,16},{24,32},{40,48},{56,64},{72,80},{88,96},{104,112},{120,128}... | collective-permute-start | bytes 52232 | tf_op jit(solution)/shard_map/ppermute | solution.py:511
  62.2 1.1 shard_map.161
  63.4 1.7 %collective-permute-done.17.swap_b = f32[2,2176]{1,0:T(2,128)S(1)} collective-permute-done((f32[2,2176]{1,0:T(2,128)S(1)}, f32[2,2176]{1,0:T(2,128)S(1)}, u32[]{:S(2)}, u32[]{:S(2)}) %collective-permute-start.17) | collective-permute-done | bytes 17440 | tf_op jit(solution)/shard_map/ppermute | solution.py:511
  65.0 0.9 shard_map.162
  65.9 0.8 collective-permute-start.18
  66.7 1.3 %collective-permute-start.19 = (f32[128,128]{1,0:T(8,128)S(1)}, f32[128,128]{1,0:T(8,128)S(1)}, u32[]{:S(2)}, u32[]{:S(2)}) collective-permute-start(f32[128,128]{1,0:T(8,128)S(1)} %get-tuple-element.70), channel_id=1, source_target_pairs={{0,2},{1,3},{2,0},{3,1},{4,6},{5,7},{6,4},{7,5},{8,10},{9,11},{10,... | collective-permute-start | bytes 196616 | tf_op jit(solution)/shard_map/ppermute | solution.py:505
  68.0 2.4 %collective-permute-start.20 = (f32[128,128]{1,0:T(8,128)S(1)}, f32[128,128]{1,0:T(8,128)S(1)}, u32[]{:S(2)}, u32[]{:S(2)}) collective-permute-start(f32[128,128]{1,0:T(8,128)S(1)} %get-tuple-element.71), channel_id=1, source_target_pairs={{0,3},{1,2},{2,1},{3,0},{4,7},{5,6},{6,5},{7,4},{8,11},{9,10},{10,... | collective-permute-start | bytes 196616 | tf_op jit(solution)/shard_map/ppermute | solution.py:505
  70.4 2.7 %collective-permute-start.21 = (f32[128,128]{1,0:T(8,128)S(1)}, f32[128,128]{1,0:T(8,128)S(1)}, u32[]{:S(2)}, u32[]{:S(2)}) collective-permute-start(f32[128,128]{1,0:T(8,128)S(1)} %get-tuple-element.72), channel_id=1, source_target_pairs={{0,4},{1,5},{2,6},{3,7},{4,0},{5,1},{6,2},{7,3},{8,12},{9,13},{10,... | collective-permute-start | bytes 196616 | tf_op jit(solution)/shard_map/ppermute | solution.py:505
  73.0 1.6 %collective-permute-start.22 = (f32[128,128]{1,0:T(8,128)S(1)}, f32[128,128]{1,0:T(8,128)S(1)}, u32[]{:S(2)}, u32[]{:S(2)}) collective-permute-start(f32[128,128]{1,0:T(8,128)S(1)} %get-tuple-element.73), channel_id=1, source_target_pairs={{0,5},{1,4},{2,7},{3,6},{4,1},{5,0},{6,3},{7,2},{8,13},{9,12},{10,... | collective-permute-start | bytes 196616 | tf_op jit(solution)/shard_map/ppermute | solution.py:505
  74.6 3.2 %collective-permute-start.23 = (f32[128,128]{1,0:T(8,128)S(1)}, f32[128,128]{1,0:T(8,128)S(1)}, u32[]{:S(2)}, u32[]{:S(2)}) collective-permute-start(f32[128,128]{1,0:T(8,128)S(1)} %get-tuple-element.74), channel_id=1, source_target_pairs={{0,6},{1,7},{2,4},{3,5},{4,2},{5,3},{6,0},{7,1},{8,14},{9,15},{10,... | collective-permute-start | bytes 196616 | tf_op jit(solution)/shard_map/ppermute | solution.py:505
  77.8 1.8 %collective-permute-start.24 = (f32[128,128]{1,0:T(8,128)S(1)}, f32[128,128]{1,0:T(8,128)S(1)}, u32[]{:S(2)}, u32[]{:S(2)}) collective-permute-start(f32[128,128]{1,0:T(8,128)S(1)} %get-tuple-element.75), channel_id=1, source_target_pairs={{0,7},{1,6},{2,5},{3,4},{4,3},{5,2},{6,1},{7,0},{8,15},{9,14},{10,... | collective-permute-start | bytes 196616 | tf_op jit(solution)/shard_map/ppermute | solution.py:505
  79.6 0.3 shard_map.163
  79.9 0.5 collective-permute-done.22.rest_5_
  80.4 1.6 %collective-permute-done.23.rest_6_ = f32[128,128]{1,0:T(8,128)S(1)} collective-permute-done((f32[128,128]{1,0:T(8,128)S(1)}, f32[128,128]{1,0:T(8,128)S(1)}, u32[]{:S(2)}, u32[]{:S(2)}) %collective-permute-start.23) | collective-permute-done | bytes 65568 | tf_op jit(solution)/shard_map/ppermute | solution.py:505
  82.1 3.0 %collective-permute-done.24.rest_7_ = f32[128,128]{1,0:T(8,128)S(1)} collective-permute-done((f32[128,128]{1,0:T(8,128)S(1)}, f32[128,128]{1,0:T(8,128)S(1)}, u32[]{:S(2)}, u32[]{:S(2)}) %collective-permute-start.24) | collective-permute-done | bytes 65568 | tf_op jit(solution)/shard_map/ppermute | solution.py:505
  85.1 1.3 %shard_map.164 = (f32[576,128]{1,0:T(8,128)S(1)}, f32[8,1,128]{2,1,0:T(1,128)S(1)}) custom-call(s32[2]{0:T(128)S(1)} %pad_add_fusion.place, f32[128,128]{1,0:T(8,128)S(1)} %get-tuple-element.68.rest_0_, f32[128,128]{1,0:T(8,128)S(1)} %collective-permute-done.18.rest_1_, f32[128,128]{1,0:T(8,128)S(1)} %collective-permute-done.19.rest_2_, ...), custom_call_target="tpu_custom_call" | custom-call | flops 100000000 | bytes 1487368 | tf_op jit(solution)/shard_map/pallas_call | solution.py:479
  86.4 0.1 collective-permute-start.25
  86.5 1.5 %shard_map.165 = f32[8,128,128]{2,1,0:T(8,128)} custom-call(f32[576,128]{1,0:T(8,128)S(1)} %get-tuple-element.80.scaled, f32[2,72,128]{2,1,0:T(8,128)S(1)} %copy-done.3, bf16[128,432]{1,0:T(8,128)(2,1)S(1)} %copy-done.9, bf16[384,256]{1,0:T(8,128)(2,1)S(1)} %copy-done.8), custom_call_target="tpu_custom_call" | custom-call | flops 1000000000 | bytes 1507328 | tf_op jit(solution)/shard_map/pallas_call | solution.py:479
  88.0 4.1 %all-to-all-start.1 = ((f32[8,128,128]{2,1,0:T(8,128)}), f32[8,128,128]{2,1,0:T(8,128)S(1)}, u32[]{:S(2)}, u32[]{:S(2)}) async-start(f32[8,128,128]{2,1,0:T(8,128)} %shard_map.165), calls=%async_computation.1 | async-start | bytes 1048576 | tf_op jit(solution)/shard_map/all_to_all | solution.py:501
  92.1 3.4 %collective-permute-start.28 = (f32[8,1,128]{2,1,0:T(1,128)S(1)}, f32[8,1,128]{2,1,0:T(1,128)S(1)}, u32[]{:S(2)}, u32[]{:S(2)}) collective-permute-start(f32[8,1,128]{2,1,0:T(1,128)S(1)} %add.26), channel_id=1, source_target_pairs={{0,48},{8,56},{16,32},{24,40},{32,16},{40,24},{48,0},{56,8},{64,11... | collective-permute-start | bytes 12296 | tf_op jit(solution)/shard_map/ppermute | solution.py:516
  95.5 0.9 collective-permute-start.26
  96.5 0.6 collective-permute-done.28
  97.1 3.5 %collective-permute-done.27 = f32[8,1,128]{2,1,0:T(1,128)S(1)} collective-permute-done((f32[8,1,128]{2,1,0:T(1,128)S(1)}, f32[8,1,128]{2,1,0:T(1,128)S(1)}, u32[]{:S(2)}, u32[]{:S(2)}) %collective-permute-start.27) | collective-permute-done | bytes 4128 | tf_op jit(solution)/shard_map/ppermute | solution.py:516
  100.6 1.9 %collective-permute-start.31 = (f32[8,1,128]{2,1,0:T(1,128)S(1)}, f32[8,1,128]{2,1,0:T(1,128)S(1)}, u32[]{:S(2)}, u32[]{:S(2)}) collective-permute-start(f32[8,1,128]{2,1,0:T(1,128)S(1)} %bitcast.13), channel_id=1, source_target_pairs={{0,192},{8,200},{16,208},{24,216},{32,224},{40,232},{48,240},{56,2... | collective-permute-start | bytes 12296 | tf_op jit(solution)/shard_map/ppermute | solution.py:516
  102.5 0.7 collective-permute-start.30
  103.2 1.6 %collective-permute-start.29 = (f32[8,1,128]{2,1,0:T(1,128)S(1)}, f32[8,1,128]{2,1,0:T(1,128)S(1)}, u32[]{:S(2)}, u32[]{:S(2)}) collective-permute-start(f32[8,1,128]{2,1,0:T(1,128)S(1)} %bitcast.15), channel_id=1, source_target_pairs={{0,64},{8,72},{16,80},{24,88},{32,96},{40,104},{48,112},{56,120},{... | collective-permute-start | bytes 12296 | tf_op jit(solution)/shard_map/ppermute | solution.py:516
  104.8 2.8 %collective-permute-done.30 = f32[8,1,128]{2,1,0:T(1,128)S(1)} collective-permute-done((f32[8,1,128]{2,1,0:T(1,128)S(1)}, f32[8,1,128]{2,1,0:T(1,128)S(1)}, u32[]{:S(2)}, u32[]{:S(2)}) %collective-permute-start.30) | collective-permute-done | bytes 4128 | tf_op jit(solution)/shard_map/ppermute | solution.py:516
  107.7 0.6 add_add_fusion
  108.3 2.0 %all-to-all-done.1.rest_0_ = f32[8,128,128]{2,1,0:T(8,128)S(1)} async-done(((f32[8,128,128]{2,1,0:T(8,128)}), f32[8,128,128]{2,1,0:T(8,128)S(1)}, u32[]{:S(2)}, u32[]{:S(2)}) %all-to-all-start.1) | async-done | bytes 524320 | tf_op jit(solution)/shard_map/all_to_all | solution.py:501
  110.3 5.2 %all-to-all-start = ((f32[8,1,128]{2,1,0:T(1,128)}), f32[8,1,128]{2,1,0:T(1,128)S(1)}, u32[]{:S(2)}, u32[]{:S(2)}) async-start(f32[8,1,128]{2,1,0:T(1,128)} %bitcast.11), calls=%async_computation | async-start | bytes 8192 | tf_op jit(solution)/shard_map/all_to_all | solution.py:501
  115.5 0.8 shard_map.166.second
  116.3 6.8 %all-to-all-done.sums = f32[8,1,128]{2,1,0:T(1,128)S(1)} async-done(((f32[8,1,128]{2,1,0:T(1,128)}), f32[8,1,128]{2,1,0:T(1,128)S(1)}, u32[]{:S(2)}, u32[]{:S(2)}) %all-to-all-start) | async-done | bytes 4128 | tf_op jit(solution)/shard_map/all_to_all | solution.py:501
  123.1 1.4 %shard_map.167 = (f32[64,2048]{1,0:T(8,128)}, f32[64,2048]{1,0:T(8,128)}, f32[64,2048]{1,0:T(8,128)}) custom-call(f32[8,1,128]{2,1,0:T(1,128)S(1)} %all-to-all-done.sums, f32[64,2176]{1,0:T(8,128)S(1)} %get-tuple-element.63.search, f32[64,2048]{1,0:T(8,128)S(1)} %get-tuple-element.76.grad, f32[64,2048]{1,0:T(8,128)S(1)} %get-tuple-element.83.rest_1_.image, ...), custom_call_target="tpu_custom_call" | custom-call | flops 1000000 | bytes 3706880 | tf_op jit(solution)/shard_map/pallas_call | solution.py:479
  (42 shorter events, 0.1 us)
Async XLA Ops:
  0.6 5.1 %copy-start.10 = (bf16[64,192]{1,0:T(8,128)(2,1)S(1)}, bf16[64,192]{1,0:T(8,128)(2,1)}, u32[]{:S(2)}) copy-start(bf16[64,192]{1,0:T(8,128)(2,1)} %constant.45.clone.basis) | copy-start | bytes 73732
  1.5 7.2 %collective-permute-start.1 = (f32[2,2048]{1,0:T(2,128)S(1)}, f32[2,2048]{1,0:T(2,128)S(1)}, u32[]{:S(2)}, u32[]{:S(2)}) collective-permute-start(f32[2,2048]{1,0:T(2,128)S(1)} %get-tuple-element.85), channel_id=1, source_target_pairs={{8,16},{24,32},{40,48},{56,64},{72,80},{88,96},{104,112},{120,128}... | collective-permute-start | bytes 49160 | tf_op jit(solution)/shard_map/ppermute | solution.py:511
  5.5 3.2 %collective-permute-start = (f32[2,2048]{1,0:T(2,128)S(1)}, f32[2,2048]{1,0:T(2,128)S(1)}, u32[]{:S(2)}, u32[]{:S(2)}) collective-permute-start(f32[2,2048]{1,0:T(2,128)S(1)} %get-tuple-element.86), channel_id=1, source_target_pairs={{0,8},{8,0},{16,24},{24,16},{32,40},{40,32},{48,56},{56,48},{64,72... | collective-permute-start | bytes 49160 | tf_op jit(solution)/shard_map/ppermute | solution.py:511
  5.7 3.0 %copy-start.4 = (bf16[64,48]{1,0:T(8,128)(2,1)S(1)}, bf16[64,48]{1,0:T(8,128)(2,1)}, u32[]{:S(2)}) copy-start(bf16[64,48]{1,0:T(8,128)(2,1)} %constant.46.clone.basis) | copy-start | bytes 18436
  5.7 28.6 %copy-start.9 = (bf16[128,432]{1,0:T(8,128)(2,1)S(1)}, bf16[128,432]{1,0:T(8,128)(2,1)}, u32[]{:S(2)}) copy-start(bf16[128,432]{1,0:T(8,128)(2,1)} %constant.50.clone.rest_14_.outer_inverse) | copy-start | bytes 331780
  8.7 25.6 %copy-start.1 = (bf16[256,256]{1,0:T(8,128)(2,1)S(1)}, bf16[256,256]{1,0:T(8,128)(2,1)}, u32[]{:S(2)}) copy-start(bf16[256,256]{1,0:T(8,128)(2,1)} %constant.52.clone.rest_12_.rest_13_) | copy-start | bytes 393220
  8.7 25.6 %copy-start.2 = (bf16[144,384]{1,0:T(8,128)(2,1)S(1)}, bf16[144,384]{1,0:T(8,128)(2,1)}, u32[]{:S(2)}) copy-start(bf16[144,384]{1,0:T(8,128)(2,1)} %constant.49.clone.rest_11_.rest_12_) | copy-start | bytes 331780
  8.7 25.6 %copy-start.3 = (f32[2,72,128]{2,1,0:T(8,128)S(1)}, f32[2,72,128]{2,1,0:T(8,128)}, u32[]{:S(2)}) copy-start(f32[2,72,128]{2,1,0:T(8,128)} %constant.51.clone.rest_13_.rest_14_.twist) | copy-start | bytes 221188
  8.8 25.6 %copy-start.5 = (f32[72,128]{1,0:T(8,128)S(1)}, f32[72,128]{1,0:T(8,128)}, u32[]{:S(2)}) copy-start(f32[72,128]{1,0:T(8,128)} %constant.55.clone.rest_9_.rest_10_) | copy-start | bytes 110596
  8.8 25.6 %copy-start.6 = (f32[72,128]{1,0:T(8,128)S(1)}, f32[72,128]{1,0:T(8,128)}, u32[]{:S(2)}) copy-start(f32[72,128]{1,0:T(8,128)} %constant.54.clone.rest_10_.rest_11_) | copy-start | bytes 110596
  8.8 25.6 %copy-start.7 = (f32[64,128]{1,0:T(8,128)S(1)}, f32[64,128]{1,0:T(8,128)}, u32[]{:S(2)}) copy-start(f32[64,128]{1,0:T(8,128)} %constant.48.clone.rest_8_.rest_9_) | copy-start | bytes 98308
  8.8 25.6 %copy-start.8 = (bf16[384,256]{1,0:T(8,128)(2,1)S(1)}, bf16[384,256]{1,0:T(8,128)(2,1)}, u32[]{:S(2)}) copy-start(bf16[384,256]{1,0:T(8,128)(2,1)} %constant.53.clone.rest_15_.inner_inverse) | copy-start | bytes 589828
  9.8 11.7 %collective-permute-start.2 = (f32[136,128]{1,0:T(8,128)S(1)}, f32[136,128]{1,0:T(8,128)S(1)}, u32[]{:S(2)}, u32[]{:S(2)}) collective-permute-start(f32[136,128]{1,0:T(8,128)S(1)} %get-tuple-element.46), channel_id=1, source_target_pairs={{0,1},{1,0},{2,3},{3,2},{4,5},{5,4},{6,7},{7,6},{8,9},{9,8},{10,11... | collective-permute-start | bytes 208904 | tf_op jit(solution)/shard_map/ppermute | solution.py:505
  11.8 14.3 %collective-permute-start.3 = (f32[136,128]{1,0:T(8,128)S(1)}, f32[136,128]{1,0:T(8,128)S(1)}, u32[]{:S(2)}, u32[]{:S(2)}) collective-permute-start(f32[136,128]{1,0:T(8,128)S(1)} %get-tuple-element.47), channel_id=1, source_target_pairs={{0,2},{1,3},{2,0},{3,1},{4,6},{5,7},{6,4},{7,5},{8,10},{9,11},{10,... | collective-permute-start | bytes 208904 | tf_op jit(solution)/shard_map/ppermute | solution.py:505
  15.1 13.8 %collective-permute-start.4 = (f32[136,128]{1,0:T(8,128)S(1)}, f32[136,128]{1,0:T(8,128)S(1)}, u32[]{:S(2)}, u32[]{:S(2)}) collective-permute-start(f32[136,128]{1,0:T(8,128)S(1)} %get-tuple-element.48), channel_id=1, source_target_pairs={{0,3},{1,2},{2,1},{3,0},{4,7},{5,6},{6,5},{7,4},{8,11},{9,10},{10,... | collective-permute-start | bytes 208904 | tf_op jit(solution)/shard_map/ppermute | solution.py:505
  15.1 13.8 %collective-permute-start.5 = (f32[136,128]{1,0:T(8,128)S(1)}, f32[136,128]{1,0:T(8,128)S(1)}, u32[]{:S(2)}, u32[]{:S(2)}) collective-permute-start(f32[136,128]{1,0:T(8,128)S(1)} %get-tuple-element.49), channel_id=1, source_target_pairs={{0,4},{1,5},{2,6},{3,7},{4,0},{5,1},{6,2},{7,3},{8,12},{9,13},{10,... | collective-permute-start | bytes 208904 | tf_op jit(solution)/shard_map/ppermute | solution.py:505
  21.4 9.2 %collective-permute-start.6 = (f32[136,128]{1,0:T(8,128)S(1)}, f32[136,128]{1,0:T(8,128)S(1)}, u32[]{:S(2)}, u32[]{:S(2)}) collective-permute-start(f32[136,128]{1,0:T(8,128)S(1)} %get-tuple-element.50), channel_id=1, source_target_pairs={{0,5},{1,4},{2,7},{3,6},{4,1},{5,0},{6,3},{7,2},{8,13},{9,12},{10,... | collective-permute-start | bytes 208904 | tf_op jit(solution)/shard_map/ppermute | solution.py:505
  21.5 10.3 %collective-permute-start.7 = (f32[136,128]{1,0:T(8,128)S(1)}, f32[136,128]{1,0:T(8,128)S(1)}, u32[]{:S(2)}, u32[]{:S(2)}) collective-permute-start(f32[136,128]{1,0:T(8,128)S(1)} %get-tuple-element.51), channel_id=1, source_target_pairs={{0,6},{1,7},{2,4},{3,5},{4,2},{5,3},{6,0},{7,1},{8,14},{9,15},{10,... | collective-permute-start | bytes 208904 | tf_op jit(solution)/shard_map/ppermute | solution.py:505
  26.1 8.2 %collective-permute-start.8 = (f32[136,128]{1,0:T(8,128)S(1)}, f32[136,128]{1,0:T(8,128)S(1)}, u32[]{:S(2)}, u32[]{:S(2)}) collective-permute-start(f32[136,128]{1,0:T(8,128)S(1)} %get-tuple-element.52), channel_id=1, source_target_pairs={{0,7},{1,6},{2,5},{3,4},{4,3},{5,2},{6,1},{7,0},{8,15},{9,14},{10,... | collective-permute-start | bytes 208904 | tf_op jit(solution)/shard_map/ppermute | solution.py:505
  34.4 22.4 %copy-start = (bf16[64,192]{1,0:T(8,128)(2,1)S(1)}, bf16[64,192]{1,0:T(8,128)(2,1)}, u32[]{:S(2)}) copy-start(bf16[64,192]{1,0:T(8,128)(2,1)} %constant.47.clone.rest_10_.rest_2_) | copy-start | bytes 73732
  36.1 8.3 %collective-permute-start.9 = (f32[136,128]{1,0:T(8,128)S(1)}, f32[136,128]{1,0:T(8,128)S(1)}, u32[]{:S(2)}, u32[]{:S(2)}) collective-permute-start(f32[136,128]{1,0:T(8,128)S(1)} %get-tuple-element.54), channel_id=1, source_target_pairs={{0,1},{1,0},{2,3},{3,2},{4,5},{5,4},{6,7},{7,6},{8,9},{9,8},{10,11... | collective-permute-start | bytes 208904 | tf_op jit(solution)/shard_map/ppermute | solution.py:505
  36.5 12.0 %collective-permute-start.10 = (f32[136,128]{1,0:T(8,128)S(1)}, f32[136,128]{1,0:T(8,128)S(1)}, u32[]{:S(2)}, u32[]{:S(2)}) collective-permute-start(f32[136,128]{1,0:T(8,128)S(1)} %get-tuple-element.55), channel_id=1, source_target_pairs={{0,2},{1,3},{2,0},{3,1},{4,6},{5,7},{6,4},{7,5},{8,10},{9,11},{10,... | collective-permute-start | bytes 208904 | tf_op jit(solution)/shard_map/ppermute | solution.py:505
  38.3 11.5 %collective-permute-start.11 = (f32[136,128]{1,0:T(8,128)S(1)}, f32[136,128]{1,0:T(8,128)S(1)}, u32[]{:S(2)}, u32[]{:S(2)}) collective-permute-start(f32[136,128]{1,0:T(8,128)S(1)} %get-tuple-element.56), channel_id=1, source_target_pairs={{0,3},{1,2},{2,1},{3,0},{4,7},{5,6},{6,5},{7,4},{8,11},{9,10},{10,... | collective-permute-start | bytes 208904 | tf_op jit(solution)/shard_map/ppermute | solution.py:505
  40.6 9.3 %collective-permute-start.12 = (f32[136,128]{1,0:T(8,128)S(1)}, f32[136,128]{1,0:T(8,128)S(1)}, u32[]{:S(2)}, u32[]{:S(2)}) collective-permute-start(f32[136,128]{1,0:T(8,128)S(1)} %get-tuple-element.57), channel_id=1, source_target_pairs={{0,4},{1,5},{2,6},{3,7},{4,0},{5,1},{6,2},{7,3},{8,12},{9,13},{10,... | collective-permute-start | bytes 208904 | tf_op jit(solution)/shard_map/ppermute | solution.py:505
  43.8 8.3 %collective-permute-start.13 = (f32[136,128]{1,0:T(8,128)S(1)}, f32[136,128]{1,0:T(8,128)S(1)}, u32[]{:S(2)}, u32[]{:S(2)}) collective-permute-start(f32[136,128]{1,0:T(8,128)S(1)} %get-tuple-element.58), channel_id=1, source_target_pairs={{0,5},{1,4},{2,7},{3,6},{4,1},{5,0},{6,3},{7,2},{8,13},{9,12},{10,... | collective-permute-start | bytes 208904 | tf_op jit(solution)/shard_map/ppermute | solution.py:505
  44.4 9.2 %collective-permute-start.14 = (f32[136,128]{1,0:T(8,128)S(1)}, f32[136,128]{1,0:T(8,128)S(1)}, u32[]{:S(2)}, u32[]{:S(2)}) collective-permute-start(f32[136,128]{1,0:T(8,128)S(1)} %get-tuple-element.59), channel_id=1, source_target_pairs={{0,6},{1,7},{2,4},{3,5},{4,2},{5,3},{6,0},{7,1},{8,14},{9,15},{10,... | collective-permute-start | bytes 208904 | tf_op jit(solution)/shard_map/ppermute | solution.py:505
  48.5 8.3 %collective-permute-start.15 = (f32[136,128]{1,0:T(8,128)S(1)}, f32[136,128]{1,0:T(8,128)S(1)}, u32[]{:S(2)}, u32[]{:S(2)}) collective-permute-start(f32[136,128]{1,0:T(8,128)S(1)} %get-tuple-element.60), channel_id=1, source_target_pairs={{0,7},{1,6},{2,5},{3,4},{4,3},{5,2},{6,1},{7,0},{8,15},{9,14},{10,... | collective-permute-start | bytes 208904 | tf_op jit(solution)/shard_map/ppermute | solution.py:505
  57.7 5.6 %collective-permute-start.16 = (f32[2,2176]{1,0:T(2,128)S(1)}, f32[2,2176]{1,0:T(2,128)S(1)}, u32[]{:S(2)}, u32[]{:S(2)}) collective-permute-start(f32[2,2176]{1,0:T(2,128)S(1)} %get-tuple-element.66), channel_id=1, source_target_pairs={{0,8},{8,0},{16,24},{24,16},{32,40},{40,32},{48,56},{56,48},{64,72... | collective-permute-start | bytes 52232 | tf_op jit(solution)/shard_map/ppermute | solution.py:511
  57.8 7.2 %collective-permute-start.17 = (f32[2,2176]{1,0:T(2,128)S(1)}, f32[2,2176]{1,0:T(2,128)S(1)}, u32[]{:S(2)}, u32[]{:S(2)}) collective-permute-start(f32[2,2176]{1,0:T(2,128)S(1)} %get-tuple-element.67), channel_id=1, source_target_pairs={{8,16},{24,32},{40,48},{56,64},{72,80},{88,96},{104,112},{120,128}... | collective-permute-start | bytes 52232 | tf_op jit(solution)/shard_map/ppermute | solution.py:511
  65.9 8.7 %collective-permute-start.18 = (f32[128,128]{1,0:T(8,128)S(1)}, f32[128,128]{1,0:T(8,128)S(1)}, u32[]{:S(2)}, u32[]{:S(2)}) collective-permute-start(f32[128,128]{1,0:T(8,128)S(1)} %get-tuple-element.69), channel_id=1, source_target_pairs={{0,1},{1,0},{2,3},{3,2},{4,5},{5,4},{6,7},{7,6},{8,9},{9,8},{10,11... | collective-permute-start | bytes 196616 | tf_op jit(solution)/shard_map/ppermute | solution.py:505
  66.7 11.1 %collective-permute-start.19 = (f32[128,128]{1,0:T(8,128)S(1)}, f32[128,128]{1,0:T(8,128)S(1)}, u32[]{:S(2)}, u32[]{:S(2)}) collective-permute-start(f32[128,128]{1,0:T(8,128)S(1)} %get-tuple-element.70), channel_id=1, source_target_pairs={{0,2},{1,3},{2,0},{3,1},{4,6},{5,7},{6,4},{7,5},{8,10},{9,11},{10,... | collective-permute-start | bytes 196616 | tf_op jit(solution)/shard_map/ppermute | solution.py:505
  68.0 11.9 %collective-permute-start.20 = (f32[128,128]{1,0:T(8,128)S(1)}, f32[128,128]{1,0:T(8,128)S(1)}, u32[]{:S(2)}, u32[]{:S(2)}) collective-permute-start(f32[128,128]{1,0:T(8,128)S(1)} %get-tuple-element.71), channel_id=1, source_target_pairs={{0,3},{1,2},{2,1},{3,0},{4,7},{5,6},{6,5},{7,4},{8,11},{9,10},{10,... | collective-permute-start | bytes 196616 | tf_op jit(solution)/shard_map/ppermute | solution.py:505
  70.4 9.5 %collective-permute-start.21 = (f32[128,128]{1,0:T(8,128)S(1)}, f32[128,128]{1,0:T(8,128)S(1)}, u32[]{:S(2)}, u32[]{:S(2)}) collective-permute-start(f32[128,128]{1,0:T(8,128)S(1)} %get-tuple-element.72), channel_id=1, source_target_pairs={{0,4},{1,5},{2,6},{3,7},{4,0},{5,1},{6,2},{7,3},{8,12},{9,13},{10,... | collective-permute-start | bytes 196616 | tf_op jit(solution)/shard_map/ppermute | solution.py:505
  73.0 7.4 %collective-permute-start.22 = (f32[128,128]{1,0:T(8,128)S(1)}, f32[128,128]{1,0:T(8,128)S(1)}, u32[]{:S(2)}, u32[]{:S(2)}) collective-permute-start(f32[128,128]{1,0:T(8,128)S(1)} %get-tuple-element.73), channel_id=1, source_target_pairs={{0,5},{1,4},{2,7},{3,6},{4,1},{5,0},{6,3},{7,2},{8,13},{9,12},{10,... | collective-permute-start | bytes 196616 | tf_op jit(solution)/shard_map/ppermute | solution.py:505
  74.6 7.4 %collective-permute-start.23 = (f32[128,128]{1,0:T(8,128)S(1)}, f32[128,128]{1,0:T(8,128)S(1)}, u32[]{:S(2)}, u32[]{:S(2)}) collective-permute-start(f32[128,128]{1,0:T(8,128)S(1)} %get-tuple-element.74), channel_id=1, source_target_pairs={{0,6},{1,7},{2,4},{3,5},{4,2},{5,3},{6,0},{7,1},{8,14},{9,15},{10,... | collective-permute-start | bytes 196616 | tf_op jit(solution)/shard_map/ppermute | solution.py:505
  77.8 7.3 %collective-permute-start.24 = (f32[128,128]{1,0:T(8,128)S(1)}, f32[128,128]{1,0:T(8,128)S(1)}, u32[]{:S(2)}, u32[]{:S(2)}) collective-permute-start(f32[128,128]{1,0:T(8,128)S(1)} %get-tuple-element.75), channel_id=1, source_target_pairs={{0,7},{1,6},{2,5},{3,4},{4,3},{5,2},{6,1},{7,0},{8,15},{9,14},{10,... | collective-permute-start | bytes 196616 | tf_op jit(solution)/shard_map/ppermute | solution.py:505
  86.4 1.6 %collective-permute-start.25 = (f32[8,1,128]{2,1,0:T(1,128)S(1)}, f32[8,1,128]{2,1,0:T(1,128)S(1)}, u32[]{:S(2)}, u32[]{:S(2)}) collective-permute-start(f32[8,1,128]{2,1,0:T(1,128)S(1)} %get-tuple-element.81), channel_id=1, source_target_pairs={{0,8},{8,0},{16,24},{24,16},{32,40},{40,32},{48,56},{56,48},{64,72... | collective-permute-start | bytes 12296 | tf_op jit(solution)/shard_map/ppermute | solution.py:516
  88.0 22.3 %all-to-all-start.1 = ((f32[8,128,128]{2,1,0:T(8,128)}), f32[8,128,128]{2,1,0:T(8,128)S(1)}, u32[]{:S(2)}, u32[]{:S(2)}) async-start(f32[8,128,128]{2,1,0:T(8,128)} %shard_map.165), calls=%async_computation.1 | async-start | bytes 1048576 | tf_op jit(solution)/shard_map/all_to_all | solution.py:501
  92.1 5.0 %collective-permute-start.28 = (f32[8,1,128]{2,1,0:T(1,128)S(1)}, f32[8,1,128]{2,1,0:T(1,128)S(1)}, u32[]{:S(2)}, u32[]{:S(2)}) collective-permute-start(f32[8,1,128]{2,1,0:T(1,128)S(1)} %add.26), channel_id=1, source_target_pairs={{0,48},{8,56},{16,32},{24,40},{32,16},{40,24},{48,0},{56,8},{64,11... | collective-permute-start | bytes 12296 | tf_op jit(solution)/shard_map/ppermute | solution.py:516
  95.5 5.1 %collective-permute-start.27 = (f32[8,1,128]{2,1,0:T(1,128)S(1)}, f32[8,1,128]{2,1,0:T(1,128)S(1)}, u32[]{:S(2)}, u32[]{:S(2)}) collective-permute-start(f32[8,1,128]{2,1,0:T(1,128)S(1)} %add.26), channel_id=1, source_target_pairs={{0,32},{8,40},{16,48},{24,56},{32,0},{40,8},{48,16},{56,24},{64,96... | collective-permute-start | bytes 12296 | tf_op jit(solution)/shard_map/ppermute | solution.py:516
  95.5 5.1 %collective-permute-start.26 = (f32[8,1,128]{2,1,0:T(1,128)S(1)}, f32[8,1,128]{2,1,0:T(1,128)S(1)}, u32[]{:S(2)}, u32[]{:S(2)}) collective-permute-start(f32[8,1,128]{2,1,0:T(1,128)S(1)} %add.26), channel_id=1, source_target_pairs={{0,16},{8,24},{16,0},{24,8},{32,48},{40,56},{48,32},{56,40},{64,80... | collective-permute-start | bytes 12296 | tf_op jit(solution)/shard_map/ppermute | solution.py:516
  100.6 4.2 %collective-permute-start.31 = (f32[8,1,128]{2,1,0:T(1,128)S(1)}, f32[8,1,128]{2,1,0:T(1,128)S(1)}, u32[]{:S(2)}, u32[]{:S(2)}) collective-permute-start(f32[8,1,128]{2,1,0:T(1,128)S(1)} %bitcast.13), channel_id=1, source_target_pairs={{0,192},{8,200},{16,208},{24,216},{32,224},{40,232},{48,240},{56,2... | collective-permute-start | bytes 12296 | tf_op jit(solution)/shard_map/ppermute | solution.py:516
  102.5 5.1 %collective-permute-start.30 = (f32[8,1,128]{2,1,0:T(1,128)S(1)}, f32[8,1,128]{2,1,0:T(1,128)S(1)}, u32[]{:S(2)}, u32[]{:S(2)}) collective-permute-start(f32[8,1,128]{2,1,0:T(1,128)S(1)} %bitcast.14), channel_id=1, source_target_pairs={{0,128},{8,136},{16,144},{24,152},{32,160},{40,168},{48,176},{56,1... | collective-permute-start | bytes 12296 | tf_op jit(solution)/shard_map/ppermute | solution.py:516
  103.2 4.5 %collective-permute-start.29 = (f32[8,1,128]{2,1,0:T(1,128)S(1)}, f32[8,1,128]{2,1,0:T(1,128)S(1)}, u32[]{:S(2)}, u32[]{:S(2)}) collective-permute-start(f32[8,1,128]{2,1,0:T(1,128)S(1)} %bitcast.15), channel_id=1, source_target_pairs={{0,64},{8,72},{16,80},{24,88},{32,96},{40,104},{48,112},{56,120},{... | collective-permute-start | bytes 12296 | tf_op jit(solution)/shard_map/ppermute | solution.py:516
  110.3 12.8 %all-to-all-start = ((f32[8,1,128]{2,1,0:T(1,128)}), f32[8,1,128]{2,1,0:T(1,128)S(1)}, u32[]{:S(2)}, u32[]{:S(2)}) async-start(f32[8,1,128]{2,1,0:T(1,128)} %bitcast.11), calls=%async_computation | async-start | bytes 8192 | tf_op jit(solution)/shard_map/all_to_all | solution.py:501
